TPU v7x, 256 devices: a whole 4x4x8 slice. The times are simulated.
256 devices in a mesh: dp: 8 (over x_hi, y), ctx: 32 (over z, x_lo, core).
Axes of the slice: x: 4 (x_hi: 2, x_lo: 2; x = x_hi * 2 + x_lo), y: 4, z: 8, core: 2. Of those that a mesh axis runs over, the one named last changes fastest.
Arguments:
- queries: bfloat16 [65536, 512], P(('dp', 'ctx')), parts along dimension 0, may hold values from -60 to 60
- keys: bfloat16 [65536, 512], P(('dp', 'ctx')), parts along dimension 0, may hold values from -6 to 6
- values: bfloat16 [65536, 512], P(('dp', 'ctx')), parts along dimension 0, may hold values from -6 to 6
- grad_out: bfloat16 [65536, 512], P(('dp', 'ctx')), parts along dimension 0, may hold values from -6 to 6
- window: int32 [4], replicated, may hold values from 128 to 256, as said below
- offsets: int32 [1024, 4], P(('dp', 'ctx')), parts along dimension 0, may hold values from 5 to 67, as said below
Outputs:
- attended: bfloat16 [65536, 512], P(('dp', 'ctx')), parts along dimension 0
- grad_queries: bfloat16 [65536, 512], P(('dp', 'ctx')), parts along dimension 0
- grad_keys: bfloat16 [65536, 512], P(('dp', 'ctx')), parts along dimension 0
- grad_values: bfloat16 [65536, 512], P(('dp', 'ctx')), parts along dimension 0
There are 8 independent parts, one for each index of `dp`. A program takes and returns all parts, laid end to end along the dimension named above; an argument that names none is the same for every part. Nothing has to cross between parts.
Inputs may be any that keep to these rules, and one draw needn't show every extreme that they name: `window`: every entry is between 128 and 256; some head has exactly 256 and some exactly 128. offsets[b, j] = 2 ** (j + 1) * 4 + (b % 4) - c with 0 <= c < 4, so the key block b - offsets[b, j] lies among the blocks of group b // 4 - 2 ** (j + 1).
All inputs are finite; a program needn't handle non-finite values.
Results may differ from a plain program's by a relative error of at most 0.017.
Values may be sent and summed in bfloat16 or wider, within the bound.
No kernel may reach another device: no remote copies, remote signals or barrier semaphores. Data moves between devices by JAX's collectives and lax.ppermute only.
A program may use at most 64 MiB of HBM per device.

v0:
```python
import jax
import jax.numpy as jnp
from jax import lax
from jax.sharding import PartitionSpec as P

BLOCK = 64
LEVELS = 4


def passed_along(array, axis, by):
    size = lax.axis_size(axis)
    pairs = [(i, i + by) for i in range(size) if 0 <= i + by < size]
    return lax.ppermute(array, axis, pairs)


def as_sent(array):

    def short(part):
        return part.astype(jnp.bfloat16) if part.dtype == jnp.float32 else part

    return jax.tree.map(short, array)


def local_pass(
    rank_index,
    query_rows,
    key_prev,
    key_own,
    value_prev,
    value_own,
    level_kv,
    grad_rows,
    window,
    offset_rows,
):
    row_count, feat_count = query_rows.shape
    head_count = window.shape[0]
    head_size = feat_count // head_count
    block_count = row_count // BLOCK
    score_scale = head_size ** (-0.5)
    f32 = jnp.float32
    query_pos = rank_index * row_count + jnp.arange(row_count, dtype=jnp.int32)
    key_pos = rank_index * row_count - row_count + jnp.arange(2 * row_count, dtype=jnp.int32)
    query_heads = query_rows.reshape(row_count, head_count, head_size)
    query_blocks = query_rows.reshape(block_count, BLOCK, head_count, head_size)
    grad_heads = grad_rows.reshape(row_count, head_count, head_size)
    grad_blocks = grad_rows.reshape(block_count, BLOCK, head_count, head_size)
    win_keys = jnp.concatenate([key_prev, key_own], 0).reshape(2 * row_count, head_count, head_size)
    win_values = jnp.concatenate([value_prev, value_own], 0).reshape(
        2 * row_count, head_count, head_size
    )
    block_ids = rank_index * block_count + jnp.arange(block_count, dtype=jnp.int32)
    picked_keys = []
    picked_values = []
    level_ok = []
    block_index = []
    for depth_index in range(LEVELS):
        source = rank_index - 2 ** (depth_index + 1)
        inside = jnp.clip(
            block_ids - offset_rows[:, depth_index] - source * block_count, 0, block_count - 1
        )
        block_index.append(inside)
        far_keys, far_values = level_kv[depth_index]
        picked_keys.append(far_keys.reshape(block_count, BLOCK, feat_count)[inside])
        picked_values.append(far_values.reshape(block_count, BLOCK, feat_count)[inside])
        level_ok.append(jnp.broadcast_to(source >= 0, (BLOCK,)))
    log_width = LEVELS * BLOCK
    log_keys = jnp.stack(picked_keys, 1).reshape(block_count, log_width, head_count, head_size)
    log_values = jnp.stack(picked_values, 1).reshape(block_count, log_width, head_count, head_size)
    log_allowed = jnp.concatenate(level_ok, 0)
    win_scores = (
        jnp.einsum("qhd,khd->hqk", query_heads, win_keys, preferred_element_type=f32) * score_scale
    )
    log_scores = (
        jnp.einsum("pqhd,pkhd->hpqk", query_blocks, log_keys, preferred_element_type=f32).reshape(
            head_count, row_count, log_width
        )
        * score_scale
    )
    win_allowed = (
        (key_pos[None, None, :] <= query_pos[None, :, None])
        & (key_pos[None, None, :] > query_pos[None, :, None] - window[:, None, None])
        & (key_pos[None, None, :] >= 0)
    )
    allowed = jnp.concatenate(
        [
            win_allowed,
            jnp.broadcast_to(log_allowed[None, None, :], (head_count, row_count, log_width)),
        ],
        -1,
    )
    scores = jnp.where(allowed, jnp.concatenate([win_scores, log_scores], -1), f32(-1e30))
    top = jnp.max(scores, -1)
    weights = jnp.exp(scores - top[..., None])
    total = jnp.sum(weights, -1)
    weights_low = weights.astype(jnp.bfloat16)
    split_at = 2 * row_count
    out_win = jnp.einsum(
        "hqk,khd->qhd", weights_low[..., :split_at], win_values, preferred_element_type=f32
    )
    out_log = jnp.einsum(
        "hpqk,pkhd->pqhd",
        weights_low[..., split_at:].reshape(head_count, block_count, BLOCK, log_width),
        log_values,
        preferred_element_type=f32,
    ).reshape(row_count, head_count, head_size)
    attended = ((out_win + out_log) / total.T[:, :, None]).astype(jnp.bfloat16)
    lse = top + jnp.log(total)
    probs = jnp.exp(scores - lse[..., None])
    probs_low = probs.astype(jnp.bfloat16)
    delta = jnp.sum(grad_heads.astype(f32) * attended.astype(f32), -1).T
    dprob_win = jnp.einsum("qhd,khd->hqk", grad_heads, win_values, preferred_element_type=f32)
    dprob_log = jnp.einsum(
        "pqhd,pkhd->hpqk", grad_blocks, log_values, preferred_element_type=f32
    ).reshape(head_count, row_count, log_width)
    dscore = probs * (jnp.concatenate([dprob_win, dprob_log], -1) - delta[..., None])
    dscore_low = dscore.astype(jnp.bfloat16)
    dscore_win = dscore_low[..., :split_at]
    dscore_log = dscore_low[..., split_at:].reshape(head_count, block_count, BLOCK, log_width)
    probs_win = probs_low[..., :split_at]
    probs_log = probs_low[..., split_at:].reshape(head_count, block_count, BLOCK, log_width)
    grad_q = (
        jnp.einsum("hqk,khd->qhd", dscore_win, win_keys, preferred_element_type=f32)
        + jnp.einsum("hpqk,pkhd->pqhd", dscore_log, log_keys, preferred_element_type=f32).reshape(
            row_count, head_count, head_size
        )
    ) * score_scale
    grad_q = grad_q.astype(jnp.bfloat16).reshape(row_count, feat_count)
    dkey_win = (
        jnp.einsum("hqk,qhd->khd", dscore_win, query_heads, preferred_element_type=f32)
        * score_scale
    ).reshape(split_at, feat_count)
    dval_win = jnp.einsum(
        "hqk,qhd->khd", probs_win, grad_heads, preferred_element_type=f32
    ).reshape(split_at, feat_count)
    dkey_log = (
        jnp.einsum("hpqk,pqhd->pkhd", dscore_log, query_blocks, preferred_element_type=f32)
        * score_scale
    ).reshape(block_count, LEVELS, BLOCK, feat_count)
    dval_log = jnp.einsum(
        "hpqk,pqhd->pkhd", probs_log, grad_blocks, preferred_element_type=f32
    ).reshape(block_count, LEVELS, BLOCK, feat_count)
    level_parts = []
    for depth_index in range(LEVELS):
        onehot = (
            block_index[depth_index][:, None] == jnp.arange(block_count, dtype=jnp.int32)[None, :]
        ).astype(f32)
        part_key = (
            jnp.einsum(
                "pc,pkf->ckf", onehot, dkey_log[:, depth_index], precision=lax.Precision.HIGHEST
            )
            .reshape(row_count, feat_count)
            .astype(jnp.bfloat16)
        )
        part_value = (
            jnp.einsum(
                "pc,pkf->ckf", onehot, dval_log[:, depth_index], precision=lax.Precision.HIGHEST
            )
            .reshape(row_count, feat_count)
            .astype(jnp.bfloat16)
        )
        level_parts.append((part_key, part_value))
    prev_part = (
        dkey_win[:row_count].astype(jnp.bfloat16),
        dval_win[:row_count].astype(jnp.bfloat16),
    )
    return (
        attended.reshape(row_count, feat_count),
        grad_q,
        dkey_win[row_count:],
        dval_win[row_count:],
        prev_part,
        level_parts,
    )


def on_device(queries, keys, values, grad_out, window, offsets):
    rank_index = lax.axis_index("ctx")
    key_prev, value_prev = passed_along((keys, values), "ctx", 1)
    level_kv = []
    for depth_index in range(LEVELS):
        level_kv.append(passed_along((keys, values), "ctx", 2 ** (depth_index + 1)))
    attended, grad_q, own_dkey, own_dval, prev_part, level_parts = local_pass(
        rank_index, queries, key_prev, keys, value_prev, values, level_kv, grad_out, window, offsets
    )
    back_key, back_value = passed_along((prev_part[0], prev_part[1]), "ctx", -1)
    grad_keys = own_dkey + back_key.astype(jnp.float32)
    grad_values = own_dval + back_value.astype(jnp.float32)
    for depth_index in range(LEVELS):
        far_key, far_value = passed_along(
            as_sent(level_parts[depth_index]), "ctx", -(2 ** (depth_index + 1))
        )
        grad_keys = grad_keys + far_key.astype(jnp.float32)
        grad_values = grad_values + far_value.astype(jnp.float32)
    return (attended, grad_q, grad_keys.astype(jnp.bfloat16), grad_values.astype(jnp.bfloat16))


def solution(mesh):
    return jax.shard_map(
        on_device,
        mesh=mesh,
        in_specs=(
            P(("dp", "ctx"), None),
            P(("dp", "ctx"), None),
            P(("dp", "ctx"), None),
            P(("dp", "ctx"), None),
            P(),
            P(("dp", "ctx"), None),
        ),
        out_specs=(
            P(("dp", "ctx"), None),
            P(("dp", "ctx"), None),
            P(("dp", "ctx"), None),
            P(("dp", "ctx"), None),
        ),
        check_vma=False,
    )
```

profile of v0, /device:TPU:56, one launch (start us, length us, event | category | flops | bytes accessed | tf_op | source)
XLA Modules:
  0.0 226.8 jit_solution(13464495358204060993)
XLA Ops:
  0.7 3.5 %collective-permute-start.2 = (bf16[256,512]{1,0:T(8,128)(2,1)}, bf16[256,512]{1,0:T(8,128)(2,1)S(1)}, u32[]{:S(2)}, u32[]{:S(2)}) collective-permute-start(bf16[256,512]{1,0:T(8,128)(2,1)} %param.7), channel_id=1, source_target_pairs={{0,2},{1,3},{2,4},{3,5},{4,6},{5,7},{6,8},{7,9},{8,10},{9,11},{10,... | collective-permute-start | bytes 786440 | tf_op jit(solution)/shard_map/ppermute | solution.py:13
  4.2 3.8 %collective-permute-start.3 = (bf16[256,512]{1,0:T(8,128)(2,1)}, bf16[256,512]{1,0:T(8,128)(2,1)S(1)}, u32[]{:S(2)}, u32[]{:S(2)}) collective-permute-start(bf16[256,512]{1,0:T(8,128)(2,1)} %param.7), channel_id=1, source_target_pairs={{0,4},{1,5},{2,6},{3,7},{4,8},{5,9},{6,10},{7,11},{8,12},{9,13},{1... | collective-permute-start | bytes 786440 | tf_op jit(solution)/shard_map/ppermute | solution.py:13
  8.0 7.3 %collective-permute-start.5 = (bf16[256,512]{1,0:T(8,128)(2,1)}, bf16[256,512]{1,0:T(8,128)(2,1)S(1)}, u32[]{:S(2)}, u32[]{:S(2)}) collective-permute-start(bf16[256,512]{1,0:T(8,128)(2,1)} %param.7), channel_id=1, source_target_pairs={{0,16},{1,17},{2,18},{3,19},{4,20},{5,21},{6,22},{7,23},{8,24},{9,... | collective-permute-start | bytes 786440 | tf_op jit(solution)/shard_map/ppermute | solution.py:13
  17.1 3.1 %collective-permute-start.7 = (bf16[256,512]{1,0:T(8,128)(2,1)}, bf16[256,512]{1,0:T(8,128)(2,1)S(1)}, u32[]{:S(2)}, u32[]{:S(2)}) collective-permute-start(bf16[256,512]{1,0:T(8,128)(2,1)} %param.8), channel_id=1, source_target_pairs={{0,4},{1,5},{2,6},{3,7},{4,8},{5,9},{6,10},{7,11},{8,12},{9,13},{1... | collective-permute-start | bytes 786440 | tf_op jit(solution)/shard_map/ppermute | solution.py:13
  34.1 4.0 %collective-permute-start.9 = (bf16[256,512]{1,0:T(8,128)(2,1)}, bf16[256,512]{1,0:T(8,128)(2,1)S(1)}, u32[]{:S(2)}, u32[]{:S(2)}) collective-permute-start(bf16[256,512]{1,0:T(8,128)(2,1)} %param.8), channel_id=1, source_target_pairs={{0,16},{1,17},{2,18},{3,19},{4,20},{5,21},{6,22},{7,23},{8,24},{9,... | collective-permute-start | bytes 786440 | tf_op jit(solution)/shard_map/ppermute | solution.py:13
  38.7 4.6 %collective-permute-start.8 = (bf16[256,512]{1,0:T(8,128)(2,1)}, bf16[256,512]{1,0:T(8,128)(2,1)S(1)}, u32[]{:S(2)}, u32[]{:S(2)}) collective-permute-start(bf16[256,512]{1,0:T(8,128)(2,1)} %param.8), channel_id=1, source_target_pairs={{0,8},{1,9},{2,10},{3,11},{4,12},{5,13},{6,14},{7,15},{8,16},{9,17... | collective-permute-start | bytes 786440 | tf_op jit(solution)/shard_map/ppermute | solution.py:13
  44.4 5.0 %collective-permute-start.1 = (bf16[256,512]{0,1:T(8,128)(2,1)}, bf16[256,512]{0,1:T(8,128)(2,1)}, u32[]{:S(2)}, u32[]{:S(2)}) collective-permute-start(bf16[256,512]{0,1:T(8,128)(2,1)} %copy.42), channel_id=1, source_target_pairs={{0,1},{1,2},{2,3},{3,4},{4,5},{5,6},{6,7},{7,8},{8,9},{9,10},{10,1... | collective-permute-start | bytes 786440 | tf_op jit(solution)/shard_map/ppermute | solution.py:13
  54.1 5.3 %collective-permute-done.8 = bf16[256,512]{1,0:T(8,128)(2,1)S(1)} collective-permute-done((bf16[256,512]{1,0:T(8,128)(2,1)}, bf16[256,512]{1,0:T(8,128)(2,1)S(1)}, u32[]{:S(2)}, u32[]{:S(2)}) %collective-permute-start.8) | collective-permute-done | bytes 262176 | tf_op jit(solution)/shard_map/ppermute | solution.py:13
  71.8 2.1 copy.50
  76.3 2.0 copy.54
  81.9 2.1 fusion.4
  90.9 2.7 %copy.106 = f32[4,256,4,128]{3,2,0,1:T(4,128)} copy(f32[4,256,4,128]{3,1,2,0:T(8,128)S(1)} %multiply_bitcast_fusion) | data formatting | bytes 4194304 | tf_op jit(solution)/shard_map/reshape | solution.py:139
  93.6 2.7 %reshape.297 = f32[4,4,64,512]{3,0,2,1:T(4,128)S(1)} reshape(f32[4,256,4,128]{3,2,0,1:T(4,128)} %copy.106) | data formatting | bytes 4194304 | tf_op jit(solution)/shard_map/reshape | solution.py:139
  99.5 2.7 %copy.108 = f32[4,256,4,128]{3,2,0,1:T(4,128)} copy(f32[4,256,4,128]{3,1,2,0:T(8,128)S(1)} %convolution_bitcast_fusion) | data formatting | bytes 4194304 | tf_op jit(solution)/shard_map/reshape | solution.py:142
  102.2 3.4 %reshape.298 = f32[4,4,64,512]{3,0,2,1:T(4,128)} reshape(f32[4,256,4,128]{3,2,0,1:T(4,128)} %copy.108) | data formatting | bytes 4194304 | tf_op jit(solution)/shard_map/reshape | solution.py:142
  105.6 2.5 %convolution_convert_fusion = bf16[4,64,512]{2,0,1:T(4,128)(2,1)} fusion(f32[4,4,64,512]{3,0,2,1:T(4,128)} %reshape.298, s32[4]{0:T(128)S(1)} %get-tuple-element.17), kind=kOutput, calls=%fused_computation.36 | convolution fusion | flops 6422544 | bytes 786448 | tf_op jit(solution)/shard_map/pc,pkf->ckf/dot_general | solution.py:156
  108.1 2.3 %convolution_convert_fusion.1 = bf16[4,64,512]{2,0,1:T(4,128)(2,1)} fusion(f32[4,4,64,512]{3,0,2,1:T(4,128)} %reshape.298, s32[4]{0:T(128)S(1)} %get-tuple-element.18), kind=kOutput, calls=%fused_computation.37 | convolution fusion | flops 6422544 | bytes 786448 | tf_op jit(solution)/shard_map/pc,pkf->ckf/dot_general | solution.py:156
  130.7 2.1 collective-permute-start.11
  147.8 2.0 collective-permute-start.15
  153.8 16.9 %collective-permute-done.13 = bf16[256,512]{1,0:T(8,128)(2,1)} collective-permute-done((bf16[256,512]{1,0:T(8,128)(2,1)}, bf16[256,512]{1,0:T(8,128)(2,1)}, u32[]{:S(2)}, u32[]{:S(2)}) %collective-permute-start.13) | collective-permute-done | bytes 262176 | tf_op jit(solution)/shard_map/ppermute | solution.py:13
  171.9 19.3 %collective-permute-done.14 = bf16[256,512]{1,0:T(8,128)(2,1)} collective-permute-done((bf16[256,512]{1,0:T(8,128)(2,1)}, bf16[256,512]{1,0:T(8,128)(2,1)}, u32[]{:S(2)}, u32[]{:S(2)}) %collective-permute-start.14) | collective-permute-done | bytes 262176 | tf_op jit(solution)/shard_map/ppermute | solution.py:13
  192.5 2.2 add_convert_fusion.1
  194.7 5.6 %collective-permute-done.18 = bf16[256,512]{1,0:T(8,128)(2,1)S(1)} collective-permute-done((bf16[256,512]{1,0:T(8,128)(2,1)S(1)}, bf16[256,512]{1,0:T(8,128)(2,1)S(1)}, u32[]{:S(2)}, u32[]{:S(2)}) %collective-permute-start.18) | collective-permute-done | bytes 262176 | tf_op jit(solution)/shard_map/ppermute | solution.py:13
  200.2 25.7 %collective-permute-done.19 = bf16[256,512]{1,0:T(8,128)(2,1)S(1)} collective-permute-done((bf16[256,512]{1,0:T(8,128)(2,1)S(1)}, bf16[256,512]{1,0:T(8,128)(2,1)S(1)}, u32[]{:S(2)}, u32[]{:S(2)}) %collective-permute-start.19) | collective-permute-done | bytes 262176 | tf_op jit(solution)/shard_map/ppermute | solution.py:13
  (166 shorter events, 92.4 us)
Async XLA Ops:
  0.6 29.8 %copy-start.24 = (bf16[256,512]{1,0:T(8,128)(2,1)S(1)}, bf16[256,512]{1,0:T(8,128)(2,1)}, u32[]{:S(2)}) copy-start(bf16[256,512]{1,0:T(8,128)(2,1)} %param.7) | copy-start | bytes 786436
  0.6 30.7 %copy-start.21 = (bf16[256,512]{1,0:T(8,128)(2,1)S(1)}, bf16[256,512]{1,0:T(8,128)(2,1)}, u32[]{:S(2)}) copy-start(bf16[256,512]{1,0:T(8,128)(2,1)} %param.6) | copy-start | bytes 786436
  0.7 23.0 %collective-permute-start.2 = (bf16[256,512]{1,0:T(8,128)(2,1)}, bf16[256,512]{1,0:T(8,128)(2,1)S(1)}, u32[]{:S(2)}, u32[]{:S(2)}) collective-permute-start(bf16[256,512]{1,0:T(8,128)(2,1)} %param.7), channel_id=1, source_target_pairs={{0,2},{1,3},{2,4},{3,5},{4,6},{5,7},{6,8},{7,9},{8,10},{9,11},{10,... | collective-permute-start | bytes 786440 | tf_op jit(solution)/shard_map/ppermute | solution.py:13
  4.2 21.4 %collective-permute-start.3 = (bf16[256,512]{1,0:T(8,128)(2,1)}, bf16[256,512]{1,0:T(8,128)(2,1)S(1)}, u32[]{:S(2)}, u32[]{:S(2)}) collective-permute-start(bf16[256,512]{1,0:T(8,128)(2,1)} %param.7), channel_id=1, source_target_pairs={{0,4},{1,5},{2,6},{3,7},{4,8},{5,9},{6,10},{7,11},{8,12},{9,13},{1... | collective-permute-start | bytes 786440 | tf_op jit(solution)/shard_map/ppermute | solution.py:13
  8.0 26.0 %collective-permute-start.5 = (bf16[256,512]{1,0:T(8,128)(2,1)}, bf16[256,512]{1,0:T(8,128)(2,1)S(1)}, u32[]{:S(2)}, u32[]{:S(2)}) collective-permute-start(bf16[256,512]{1,0:T(8,128)(2,1)} %param.7), channel_id=1, source_target_pairs={{0,16},{1,17},{2,18},{3,19},{4,20},{5,21},{6,22},{7,23},{8,24},{9,... | collective-permute-start | bytes 786440 | tf_op jit(solution)/shard_map/ppermute | solution.py:13
  15.3 23.4 %collective-permute-start.4 = (bf16[256,512]{1,0:T(8,128)(2,1)}, bf16[256,512]{1,0:T(8,128)(2,1)S(1)}, u32[]{:S(2)}, u32[]{:S(2)}) collective-permute-start(bf16[256,512]{1,0:T(8,128)(2,1)} %param.7), channel_id=1, source_target_pairs={{0,8},{1,9},{2,10},{3,11},{4,12},{5,13},{6,14},{7,15},{8,16},{9,17... | collective-permute-start | bytes 786440 | tf_op jit(solution)/shard_map/ppermute | solution.py:13
  17.1 27.3 %collective-permute-start.7 = (bf16[256,512]{1,0:T(8,128)(2,1)}, bf16[256,512]{1,0:T(8,128)(2,1)S(1)}, u32[]{:S(2)}, u32[]{:S(2)}) collective-permute-start(bf16[256,512]{1,0:T(8,128)(2,1)} %param.8), channel_id=1, source_target_pairs={{0,4},{1,5},{2,6},{3,7},{4,8},{5,9},{6,10},{7,11},{8,12},{9,13},{1... | collective-permute-start | bytes 786440 | tf_op jit(solution)/shard_map/ppermute | solution.py:13
  23.6 26.3 %collective-permute-start.6 = (bf16[256,512]{1,0:T(8,128)(2,1)}, bf16[256,512]{1,0:T(8,128)(2,1)}, u32[]{:S(2)}, u32[]{:S(2)}) collective-permute-start(bf16[256,512]{1,0:T(8,128)(2,1)} %param.8), channel_id=1, source_target_pairs={{0,2},{1,3},{2,4},{3,5},{4,6},{5,7},{6,8},{7,9},{8,10},{9,11},{10,... | collective-permute-start | bytes 786440 | tf_op jit(solution)/shard_map/ppermute | solution.py:13
  25.6 25.9 %collective-permute-start = (bf16[256,512]{1,0:T(8,128)(2,1)}, bf16[256,512]{1,0:T(8,128)(2,1)}, u32[]{:S(2)}, u32[]{:S(2)}) collective-permute-start(bf16[256,512]{1,0:T(8,128)(2,1)} %param.8), channel_id=1, source_target_pairs={{0,1},{1,2},{2,3},{3,4},{4,5},{5,6},{6,7},{7,8},{8,9},{9,10},{10,1... | collective-permute-start | bytes 786440 | tf_op jit(solution)/shard_map/ppermute | solution.py:13
  34.1 19.5 %collective-permute-start.9 = (bf16[256,512]{1,0:T(8,128)(2,1)}, bf16[256,512]{1,0:T(8,128)(2,1)S(1)}, u32[]{:S(2)}, u32[]{:S(2)}) collective-permute-start(bf16[256,512]{1,0:T(8,128)(2,1)} %param.8), channel_id=1, source_target_pairs={{0,16},{1,17},{2,18},{3,19},{4,20},{5,21},{6,22},{7,23},{8,24},{9,... | collective-permute-start | bytes 786440 | tf_op jit(solution)/shard_map/ppermute | solution.py:13
  38.7 20.8 %collective-permute-start.8 = (bf16[256,512]{1,0:T(8,128)(2,1)}, bf16[256,512]{1,0:T(8,128)(2,1)S(1)}, u32[]{:S(2)}, u32[]{:S(2)}) collective-permute-start(bf16[256,512]{1,0:T(8,128)(2,1)} %param.8), channel_id=1, source_target_pairs={{0,8},{1,9},{2,10},{3,11},{4,12},{5,13},{6,14},{7,15},{8,16},{9,17... | collective-permute-start | bytes 786440 | tf_op jit(solution)/shard_map/ppermute | solution.py:13
  44.4 19.7 %collective-permute-start.1 = (bf16[256,512]{0,1:T(8,128)(2,1)}, bf16[256,512]{0,1:T(8,128)(2,1)}, u32[]{:S(2)}, u32[]{:S(2)}) collective-permute-start(bf16[256,512]{0,1:T(8,128)(2,1)} %copy.42), channel_id=1, source_target_pairs={{0,1},{1,2},{2,3},{3,4},{4,5},{5,6},{6,7},{7,8},{8,9},{9,10},{10,1... | collective-permute-start | bytes 786440 | tf_op jit(solution)/shard_map/ppermute | solution.py:13
  116.6 18.8 %copy-start.7 = (f32[4,4,64,512]{3,0,2,1:T(4,128)S(1)}, f32[4,4,64,512]{3,0,2,1:T(4,128)}, u32[]{:S(2)}) copy-start(f32[4,4,64,512]{3,0,2,1:T(4,128)} %reshape.298) | copy-start | bytes 6291460
  118.5 29.3 %collective-permute-start.10 = (bf16[256,512]{1,0:T(8,128)(2,1)}, bf16[256,512]{1,0:T(8,128)(2,1)}, u32[]{:S(2)}, u32[]{:S(2)}) collective-permute-start(bf16[256,512]{1,0:T(8,128)(2,1)} %copy.69), channel_id=1, source_target_pairs={{1,0},{2,1},{3,2},{4,3},{5,4},{6,5},{7,6},{8,7},{9,8},{10,9},{11,1... | collective-permute-start | bytes 786440 | tf_op jit(solution)/shard_map/ppermute | solution.py:13
  128.7 21.1 %collective-permute-start.12 = (bf16[256,512]{1,0:T(8,128)(2,1)}, bf16[256,512]{1,0:T(8,128)(2,1)}, u32[]{:S(2)}, u32[]{:S(2)}) collective-permute-start(bf16[256,512]{1,0:T(8,128)(2,1)} %bitcast.46), channel_id=1, source_target_pairs={{4,0},{5,1},{6,2},{7,3},{8,4},{9,5},{10,6},{11,7},{12,8},{13,9},{1... | collective-permute-start | bytes 786440 | tf_op jit(solution)/shard_map/ppermute | solution.py:13
  130.7 21.2 %collective-permute-start.11 = (bf16[256,512]{1,0:T(8,128)(2,1)}, bf16[256,512]{1,0:T(8,128)(2,1)}, u32[]{:S(2)}, u32[]{:S(2)}) collective-permute-start(bf16[256,512]{1,0:T(8,128)(2,1)} %bitcast.43), channel_id=1, source_target_pairs={{2,0},{3,1},{4,2},{5,3},{6,4},{7,5},{8,6},{9,7},{10,8},{11,9},{12,... | collective-permute-start | bytes 786440 | tf_op jit(solution)/shard_map/ppermute | solution.py:13
  132.8 37.9 %collective-permute-start.13 = (bf16[256,512]{1,0:T(8,128)(2,1)}, bf16[256,512]{1,0:T(8,128)(2,1)}, u32[]{:S(2)}, u32[]{:S(2)}) collective-permute-start(bf16[256,512]{1,0:T(8,128)(2,1)} %bitcast.49), channel_id=1, source_target_pairs={{8,0},{9,1},{10,2},{11,3},{12,4},{13,5},{14,6},{15,7},{16,8},{17,9... | collective-permute-start | bytes 786440 | tf_op jit(solution)/shard_map/ppermute | solution.py:13
  134.1 57.1 %collective-permute-start.14 = (bf16[256,512]{1,0:T(8,128)(2,1)}, bf16[256,512]{1,0:T(8,128)(2,1)}, u32[]{:S(2)}, u32[]{:S(2)}) collective-permute-start(bf16[256,512]{1,0:T(8,128)(2,1)} %bitcast.52), channel_id=1, source_target_pairs={{16,0},{17,1},{18,2},{19,3},{20,4},{21,5},{22,6},{23,7},{24,8},{25... | collective-permute-start | bytes 786440 | tf_op jit(solution)/shard_map/ppermute | solution.py:13
  145.0 47.4 %copy-start.19 = (f32[256,512]{1,0:T(8,128)S(1)}, f32[256,512]{1,0:T(8,128)}, u32[]{:S(2)}) copy-start(f32[256,512]{1,0:T(8,128)} %copy.70) | copy-start | bytes 1572868
  147.8 46.8 %collective-permute-start.15 = (bf16[256,512]{1,0:T(8,128)(2,1)S(1)}, bf16[256,512]{1,0:T(8,128)(2,1)S(1)}, u32[]{:S(2)}, u32[]{:S(2)}) collective-permute-start(bf16[256,512]{1,0:T(8,128)(2,1)S(1)} %copy-done.25), channel_id=1, source_target_pairs={{1,0},{2,1},{3,2},{4,3},{5,4},{6,5},{7,6},{8,7},{9,8},{10,9},{11,1... | collective-permute-start | bytes 786440 | tf_op jit(solution)/shard_map/ppermute | solution.py:13
  149.9 44.8 %collective-permute-start.17 = (bf16[256,512]{1,0:T(8,128)(2,1)S(1)}, bf16[256,512]{1,0:T(8,128)(2,1)S(1)}, u32[]{:S(2)}, u32[]{:S(2)}) collective-permute-start(bf16[256,512]{1,0:T(8,128)(2,1)S(1)} %bitcast.176), channel_id=1, source_target_pairs={{4,0},{5,1},{6,2},{7,3},{8,4},{9,5},{10,6},{11,7},{12,8},{13,9},{1... | collective-permute-start | bytes 786440 | tf_op jit(solution)/shard_map/ppermute | solution.py:13
  151.8 42.8 %collective-permute-start.16 = (bf16[256,512]{1,0:T(8,128)(2,1)S(1)}, bf16[256,512]{1,0:T(8,128)(2,1)S(1)}, u32[]{:S(2)}, u32[]{:S(2)}) collective-permute-start(bf16[256,512]{1,0:T(8,128)(2,1)S(1)} %bitcast.175), channel_id=1, source_target_pairs={{2,0},{3,1},{4,2},{5,3},{6,4},{7,5},{8,6},{9,7},{10,8},{11,9},{12,... | collective-permute-start | bytes 786440 | tf_op jit(solution)/shard_map/ppermute | solution.py:13
  170.6 29.6 %collective-permute-start.18 = (bf16[256,512]{1,0:T(8,128)(2,1)S(1)}, bf16[256,512]{1,0:T(8,128)(2,1)S(1)}, u32[]{:S(2)}, u32[]{:S(2)}) collective-permute-start(bf16[256,512]{1,0:T(8,128)(2,1)S(1)} %bitcast.174), channel_id=1, source_target_pairs={{8,0},{9,1},{10,2},{11,3},{12,4},{13,5},{14,6},{15,7},{16,8},{17,9... | collective-permute-start | bytes 786440 | tf_op jit(solution)/shard_map/ppermute | solution.py:13
  191.2 34.8 %collective-permute-start.19 = (bf16[256,512]{1,0:T(8,128)(2,1)S(1)}, bf16[256,512]{1,0:T(8,128)(2,1)S(1)}, u32[]{:S(2)}, u32[]{:S(2)}) collective-permute-start(bf16[256,512]{1,0:T(8,128)(2,1)S(1)} %bitcast.173), channel_id=1, source_target_pairs={{16,0},{17,1},{18,2},{19,3},{20,4},{21,5},{22,6},{23,7},{24,8},{25... | collective-permute-start | bytes 786440 | tf_op jit(solution)/shard_map/ppermute | solution.py:13
  (23 other events, 95.2 us)
where the time goes:
time: 228 us; the launch traced here: 227 us
  waiting for transfers between devices  72.8 us (32%)
  local copies, waits for them, and re-layouts  58.4 us (26%)
  starting transfers between devices  54 us (24%)
  matrix products  26.9 us (12%)
  other arithmetic  13.4 us (6%)
    ppermute x20, waiting for transfers between devices, passed_along(): return lax.ppermute(array, axis, pairs)  72.8 us
    ppermute x20, starting transfers between devices, passed_along(): return lax.ppermute(array, axis, pairs)  54 us
    unnamed x56, local copies, waits for them, and re-layouts  8.02 us
    dot_general x4, matrix products, local_pass(): jnp.einsum('pc,pkf->ckf', onehot, dval_log[:, depth_index], precision=lax...  6.75 us
    reshape x2, local copies, waits for them, and re-layouts, local_pass(): dval_log = jnp.einsum('hpqk,pqhd->pkhd', probs_log, grad_blocks, preferre...  6.13 us
    dot_general x4, matrix products, local_pass(): jnp.einsum('pc,pkf->ckf', onehot, dkey_log[:, depth_index], precision=lax...  5.95 us
    reshape x2, local copies, waits for them, and re-layouts, local_pass(): dkey_log = (jnp.einsum('hpqk,pqhd->pkhd', dscore_log, query_blocks, prefe...  5.36 us
    convert_element_type x4, local copies, waits for them, and re-layouts, local_pass(): part_key = jnp.einsum('pc,pkf->ckf', onehot, dkey_log[:, depth_index], pr...  5 us
  transfers between devices with their start and end apart: 20, of which 5 were waited for; matrix products, arithmetic and copies ran while one was open for 19% of the time, Pallas kernels for 0%

commit v1 on v0

v1 whole, which is shorter than its diff:
```python
import functools

import jax
import jax.numpy as jnp
from jax import lax
from jax.experimental import pallas as pl
from jax.experimental.pallas import tpu as pltpu
from jax.sharding import PartitionSpec as P

HEADS = 4
HEAD_DIM = 128
FEAT = HEADS * HEAD_DIM
ROWS = 256
BLOCK = 64
BLOCKS = ROWS // BLOCK
LEVELS = 4
SCALE = HEAD_DIM**-0.5
WINDOW_COLS = ROWS + BLOCK
COLS = WINDOW_COLS + LEVELS * BLOCK
MASKED = -1e30
STAT_ROWS = 16
F32 = jnp.float32
BF16 = jnp.bfloat16


def rows_by_rows(a, b):
    return lax.dot_general(a, b, (((1,), (1,)), ((), ())), preferred_element_type=F32)


def rows_by_columns(a, b):
    return lax.dot_general(a, b, (((1,), (0,)), ((), ())), preferred_element_type=F32)


def query_side(win, off, qd, kv0, kv1, kv2, kv4, kv8, kv16, att, dq, stats, bias, tall):
    rank = lax.axis_index("ctx")
    far = (kv2, kv4, kv8, kv16)
    row = lax.broadcasted_iota(jnp.int32, (BLOCK, COLS), 0)
    col = lax.broadcasted_iota(jnp.int32, (BLOCK, COLS), 1)
    gap = col - row
    for h in range(HEADS):
        near = (gap <= ROWS) & (gap > ROWS - win[h])
        bias[h] = jnp.where(near | (col >= WINDOW_COLS), F32(0), F32(MASKED))
    lane = lax.broadcasted_iota(jnp.int32, (1, COLS), 1)
    stat_lane = lax.broadcasted_iota(jnp.int32, (BLOCK, 128), 1)
    for p in range(BLOCKS):
        need = jnp.where(lane + BLOCK * p < ROWS, 1, 0)
        for j in range(LEVELS):
            need = jnp.where(lane >= WINDOW_COLS + BLOCK * j, 2 ** (j + 1), need)
        exists = jnp.where(rank >= need, F32(0), F32(MASKED))
        picks = []
        for j in range(LEVELS):
            picked = jnp.clip(BLOCKS * 2 ** (j + 1) + p - off[p, j], 0, BLOCKS - 1)
            picks.append(pl.multiple_of(picked * BLOCK, BLOCK))
        mine = slice(BLOCK * p, BLOCK * (p + 1))
        kept = jnp.zeros((BLOCK, 128), F32)
        for h in range(HEADS):
            head = slice(HEAD_DIM * h, HEAD_DIM * (h + 1))

            def gathered(base):
                parts = [
                    kv1[base + BLOCK * p : base + ROWS, head],
                    kv0[base : base + BLOCK * (p + 1), head],
                ]
                for j in range(LEVELS):
                    parts.append(far[j][pl.ds(base + picks[j], BLOCK), head])
                return jnp.concatenate(parts, 0)

            k = gathered(0)
            v = gathered(ROWS)
            q = qd[mine, head]
            do = qd[ROWS + BLOCK * p : ROWS + BLOCK * (p + 1), head]
            scores = rows_by_rows(q, k) * SCALE + (bias[h] + exists)
            top = jnp.max(scores, 1, keepdims=True)
            weights = jnp.exp(scores - top)
            total = jnp.sum(weights, 1, keepdims=True)
            inverse = 1.0 / total
            out = (rows_by_columns(weights.astype(BF16), v) * inverse).astype(BF16)
            att[mine, head] = out
            delta = jnp.sum(do.astype(F32) * out.astype(F32), 1, keepdims=True)
            dscore = (weights * inverse) * (rows_by_rows(do, v) - delta)
            dq[mine, head] = (rows_by_columns(dscore.astype(BF16), k) * SCALE).astype(BF16)
            kept = jnp.where(stat_lane == h, top + jnp.log(total), kept)
            kept = jnp.where(stat_lane == HEADS + h, delta, kept)
        tall[mine, :] = kept
    stats[0 : 2 * HEADS, :] = tall[...].T[0 : 2 * HEADS]
    wide_row = lax.broadcasted_iota(jnp.int32, (STAT_ROWS - 2 * HEADS, ROWS), 0)
    wide_block = lax.broadcasted_iota(jnp.int32, (STAT_ROWS - 2 * HEADS, ROWS), 1) // BLOCK
    chosen = jnp.zeros((STAT_ROWS - 2 * HEADS, ROWS), F32)
    for p in range(BLOCKS):
        for j in range(LEVELS):
            picked = jnp.clip(BLOCKS * 2 ** (j + 1) + p - off[p, j], 0, BLOCKS - 1)
            chosen = jnp.where((wide_row == j) & (wide_block == p), picked.astype(F32), chosen)
    stats[2 * HEADS :, :] = chosen


def key_side(win, kv, qd0, qd1, qd2, qd4, qd8, qd16, st0, st1, st2, st4, st8, st16, dk, dv):
    far = ((qd2, st2), (qd4, st4), (qd8, st8), (qd16, st16))
    half = ROWS // 2
    wide = ROWS + half
    key_block = (lax.broadcasted_iota(jnp.int32, (ROWS, ROWS), 0) // BLOCK).astype(F32)
    row = lax.broadcasted_iota(jnp.int32, (half, wide), 0)
    col = lax.broadcasted_iota(jnp.int32, (half, wide), 1)
    gap = col - row
    for h in range(HEADS):
        head = slice(HEAD_DIM * h, HEAD_DIM * (h + 1))

        def pair(k, v, q, do, lse, delta, allowed):
            scores = rows_by_rows(k, q) * SCALE
            probs = jnp.exp(jnp.where(allowed, scores - lse, F32(MASKED)))
            dscore = probs * (rows_by_rows(v, do) - delta)
            return (
                rows_by_columns(dscore.astype(BF16), q),
                rows_by_columns(probs.astype(BF16), do),
            )

        near = []
        allowed = (gap >= 0) & (gap < win[h])
        for c in range(2):
            cut = half * c
            both = lambda a, b, base: jnp.concatenate(
                [a[base + cut : base + ROWS, head], b[base : base + cut + half, head]], 0
            )
            lanes = lambda r: jnp.concatenate([st0[r, cut:ROWS], st1[r, 0 : cut + half]], 0)[None, :]
            near.append(
                pair(
                    kv[cut : cut + half, head],
                    kv[ROWS + cut : ROWS + cut + half, head],
                    both(qd0, qd1, 0),
                    both(qd0, qd1, ROWS),
                    lanes(h),
                    lanes(HEADS + h),
                    allowed,
                )
            )
        dk_sum = jnp.concatenate([near[0][0], near[1][0]], 0)
        dv_sum = jnp.concatenate([near[0][1], near[1][1]], 0)
        for j in range(LEVELS):
            qd, st = far[j]
            dk_part, dv_part = pair(
                kv[0:ROWS, head],
                kv[ROWS : 2 * ROWS, head],
                qd[0:ROWS, head],
                qd[ROWS : 2 * ROWS, head],
                st[h : h + 1, :],
                st[HEADS + h : HEADS + h + 1, :],
                key_block == st[2 * HEADS + j : 2 * HEADS + j + 1, :],
            )
            dk_sum += dk_part
            dv_sum += dv_part
        dk[:, head] = (dk_sum * SCALE).astype(BF16)
        dv[:, head] = dv_sum.astype(BF16)


def moved(array, by):
    size = lax.axis_size("ctx")
    return lax.ppermute(array, "ctx", [(i, i + by) for i in range(size) if 0 <= i + by < size])


def on_device(queries, keys, values, grad_out, window, offsets):
    kv0 = jnp.concatenate([keys, values], 0)
    qd0 = jnp.concatenate([queries, grad_out], 0)
    kv4 = moved(kv0, 4)
    qd4 = moved(qd0, -4)
    kv2 = moved(kv0, 2)
    qd2 = moved(qd0, -2)
    kv1 = moved(kv0, 1)
    qd1 = moved(qd0, -1)
    kv8 = moved(kv4, 4)
    qd8 = moved(qd4, -4)
    kv16 = moved(kv8, 8)
    qd16 = moved(qd8, -8)
    smem = pl.BlockSpec(memory_space=pltpu.SMEM)
    vmem = pl.BlockSpec(memory_space=pltpu.VMEM)
    params = pltpu.CompilerParams(vmem_limit_bytes=32 * 2**20)
    half = jax.ShapeDtypeStruct((ROWS, FEAT), BF16)
    attended, grad_q, stats = pl.pallas_call(
        query_side,
        out_shape=(half, half, jax.ShapeDtypeStruct((STAT_ROWS, ROWS), F32)),
        in_specs=[smem, smem] + [vmem] * 7,
        out_specs=(vmem, vmem, vmem),
        scratch_shapes=[
            pltpu.VMEM((HEADS, BLOCK, COLS), F32),
            pltpu.VMEM((ROWS, 128), F32),
        ],
        compiler_params=params,
        cost_estimate=pl.CostEstimate(
            flops=8 * ROWS * COLS * FEAT, bytes_accessed=9 * ROWS * FEAT * 4, transcendentals=0
        ),
        name="query_side",
    )(window, offsets, qd0, kv0, kv1, kv2, kv4, kv8, kv16)
    received = [moved(stats, -by) for by in (1, 2, 4, 8, 16)]
    grad_k, grad_v = pl.pallas_call(
        key_side,
        out_shape=(half, half),
        in_specs=[smem] + [vmem] * 13,
        out_specs=(vmem, vmem),
        compiler_params=params,
        cost_estimate=pl.CostEstimate(
            flops=8 * ROWS * 6 * ROWS * FEAT, bytes_accessed=9 * ROWS * FEAT * 4, transcendentals=0
        ),
        name="key_side",
    )(window, kv0, qd0, qd1, qd2, qd4, qd8, qd16, stats, *received)
    return attended, grad_q, grad_k, grad_v


def solution(mesh):
    split = P(("dp", "ctx"), None)
    return jax.shard_map(
        on_device,
        mesh=mesh,
        in_specs=(split, split, split, split, P(), split),
        out_specs=(split,) * 4,
        check_vma=False,
    )
```

time: 228 us -> 106 us (0.46)
  the two profiles are of different devices: /device:TPU:56 before, /device:TPU:249 now
where the time goes in v1:
time: 106 us; the launch traced here: 105 us
  starting transfers between devices  62 us (58%)
  waiting for transfers between devices  24.8 us (23%)
  Pallas kernels  16.5 us (16%)
  local copies, waits for them, and re-layouts  1.1 us (1%)
    ppermute x15, starting transfers between devices, moved(): lax.ppermute(array, 'ctx', [(i, i + by) for i in range(size) if 0 <= i +...  62 us
    ppermute x15, waiting for transfers between devices, moved(): lax.ppermute(array, 'ctx', [(i, i + by) for i in range(size) if 0 <= i +...  24.8 us
    pallas_call x1, Pallas kernels, on_device(): pl.pallas_call(query_side, out_shape=(half, half, jax.ShapeDtypeStruct((S...  9.47 us
    pallas_call x1, Pallas kernels, on_device(): pl.pallas_call(key_side, out_shape=(half, half), in_specs=[smem] + [vmem]...  7.06 us
  transfers between devices with their start and end apart: 15, of which 5 were waited for; matrix products, arithmetic and copies ran while one was open for 0% of the time, Pallas kernels for 9%

profile of v1, /device:TPU:249, one launch (start us, length us, event | category | flops | bytes accessed | tf_op | source)
XLA Modules:
  0.0 105.4 jit_solution(8524049077134694727)
XLA Ops:
  0.6 1.0 constant_dynamic-update-slice_fusion.3
  1.7 0.0 copy-done.2
  1.7 1.4 %collective-permute-start.2 = (bf16[512,512]{1,0:T(8,128)(2,1)S(1)}, bf16[512,512]{1,0:T(8,128)(2,1)S(1)}, u32[]{:S(2)}, u32[]{:S(2)}) collective-permute-start(bf16[512,512]{1,0:T(8,128)(2,1)S(1)} %constant_dynamic-update-slice_fusion.2.kv0.kv), channel_id=1, source_target_pairs={{0,4},{1,5},{2,6},{3,7},{4,8},{5,9},{6,10},{7,11},{8,12},{9,13},{1... | collective-permute-start | bytes 1572872 | tf_op jit(solution)/shard_map/ppermute | solution.py:156
  3.2 4.0 %collective-permute-start.7 = (bf16[512,512]{1,0:T(8,128)(2,1)S(1)}, bf16[512,512]{1,0:T(8,128)(2,1)S(1)}, u32[]{:S(2)}, u32[]{:S(2)}) collective-permute-start(bf16[512,512]{1,0:T(8,128)(2,1)S(1)} %constant_dynamic-update-slice_fusion.qd.qd0), channel_id=1, source_target_pairs={{4,0},{5,1},{6,2},{7,3},{8,4},{9,5},{10,6},{11,7},{12,8},{13,9},{1... | collective-permute-start | bytes 1572872 | tf_op jit(solution)/shard_map/ppermute | solution.py:156
  7.3 9.3 %collective-permute-done.2.kv4 = bf16[512,512]{1,0:T(8,128)(2,1)S(1)} collective-permute-done((bf16[512,512]{1,0:T(8,128)(2,1)S(1)}, bf16[512,512]{1,0:T(8,128)(2,1)S(1)}, u32[]{:S(2)}, u32[]{:S(2)}) %collective-permute-start.2) | collective-permute-done | bytes 524320 | tf_op jit(solution)/shard_map/ppermute | solution.py:156
  16.5 1.3 %collective-permute-start.3 = (bf16[512,512]{1,0:T(8,128)(2,1)S(1)}, bf16[512,512]{1,0:T(8,128)(2,1)S(1)}, u32[]{:S(2)}, u32[]{:S(2)}) collective-permute-start(bf16[512,512]{1,0:T(8,128)(2,1)S(1)} %collective-permute-done.2.kv4), channel_id=1, source_target_pairs={{0,4},{1,5},{2,6},{3,7},{4,8},{5,9},{6,10},{7,11},{8,12},{9,13},{1... | collective-permute-start | bytes 1572872 | tf_op jit(solution)/shard_map/ppermute | solution.py:156
  17.8 3.1 %collective-permute-start.1 = (bf16[512,512]{1,0:T(8,128)(2,1)S(1)}, bf16[512,512]{1,0:T(8,128)(2,1)S(1)}, u32[]{:S(2)}, u32[]{:S(2)}) collective-permute-start(bf16[512,512]{1,0:T(8,128)(2,1)S(1)} %constant_dynamic-update-slice_fusion.2.kv0.kv), channel_id=1, source_target_pairs={{0,2},{1,3},{2,4},{3,5},{4,6},{5,7},{6,8},{7,9},{8,10},{9,11},{10,... | collective-permute-start | bytes 1572872 | tf_op jit(solution)/shard_map/ppermute | solution.py:156
  21.0 4.0 %collective-permute-start.8 = (bf16[512,512]{1,0:T(8,128)(2,1)S(1)}, bf16[512,512]{1,0:T(8,128)(2,1)S(1)}, u32[]{:S(2)}, u32[]{:S(2)}) collective-permute-start(bf16[512,512]{1,0:T(8,128)(2,1)S(1)} %collective-permute-done.7.qd4), channel_id=1, source_target_pairs={{4,0},{5,1},{6,2},{7,3},{8,4},{9,5},{10,6},{11,7},{12,8},{13,9},{1... | collective-permute-start | bytes 1572872 | tf_op jit(solution)/shard_map/ppermute | solution.py:156
  25.0 3.9 %collective-permute-start = (bf16[512,512]{1,0:T(8,128)(2,1)S(1)}, bf16[512,512]{1,0:T(8,128)(2,1)S(1)}, u32[]{:S(2)}, u32[]{:S(2)}) collective-permute-start(bf16[512,512]{1,0:T(8,128)(2,1)S(1)} %constant_dynamic-update-slice_fusion.2.kv0.kv), channel_id=1, source_target_pairs={{0,1},{1,2},{2,3},{3,4},{4,5},{5,6},{6,7},{7,8},{8,9},{9,10},{10,1... | collective-permute-start | bytes 1572872 | tf_op jit(solution)/shard_map/ppermute | solution.py:156
  28.9 1.4 %collective-permute-done.3.kv8 = bf16[512,512]{1,0:T(8,128)(2,1)S(1)} collective-permute-done((bf16[512,512]{1,0:T(8,128)(2,1)S(1)}, bf16[512,512]{1,0:T(8,128)(2,1)S(1)}, u32[]{:S(2)}, u32[]{:S(2)}) %collective-permute-start.3) | collective-permute-done | bytes 524320 | tf_op jit(solution)/shard_map/ppermute | solution.py:156
  30.3 1.3 %collective-permute-start.4 = (bf16[512,512]{1,0:T(8,128)(2,1)S(1)}, bf16[512,512]{1,0:T(8,128)(2,1)S(1)}, u32[]{:S(2)}, u32[]{:S(2)}) collective-permute-start(bf16[512,512]{1,0:T(8,128)(2,1)S(1)} %collective-permute-done.3.kv8), channel_id=1, source_target_pairs={{0,8},{1,9},{2,10},{3,11},{4,12},{5,13},{6,14},{7,15},{8,16},{9,17... | collective-permute-start | bytes 1572872 | tf_op jit(solution)/shard_map/ppermute | solution.py:156
  31.6 3.6 %collective-permute-start.6 = (bf16[512,512]{1,0:T(8,128)(2,1)S(1)}, bf16[512,512]{1,0:T(8,128)(2,1)S(1)}, u32[]{:S(2)}, u32[]{:S(2)}) collective-permute-start(bf16[512,512]{1,0:T(8,128)(2,1)S(1)} %constant_dynamic-update-slice_fusion.qd.qd0), channel_id=1, source_target_pairs={{2,0},{3,1},{4,2},{5,3},{6,4},{7,5},{8,6},{9,7},{10,8},{11,9},{12,... | collective-permute-start | bytes 1572872 | tf_op jit(solution)/shard_map/ppermute | solution.py:156
  35.1 7.3 %collective-permute-done.1.kv2 = bf16[512,512]{1,0:T(8,128)(2,1)S(1)} collective-permute-done((bf16[512,512]{1,0:T(8,128)(2,1)S(1)}, bf16[512,512]{1,0:T(8,128)(2,1)S(1)}, u32[]{:S(2)}, u32[]{:S(2)}) %collective-permute-start.1) | collective-permute-done | bytes 524320 | tf_op jit(solution)/shard_map/ppermute | solution.py:156
  42.5 6.5 %collective-permute-start.5 = (bf16[512,512]{1,0:T(8,128)(2,1)S(1)}, bf16[512,512]{1,0:T(8,128)(2,1)S(1)}, u32[]{:S(2)}, u32[]{:S(2)}) collective-permute-start(bf16[512,512]{1,0:T(8,128)(2,1)S(1)} %constant_dynamic-update-slice_fusion.qd.qd0), channel_id=1, source_target_pairs={{1,0},{2,1},{3,2},{4,3},{5,4},{6,5},{7,6},{8,7},{9,8},{10,9},{11,1... | collective-permute-start | bytes 1572872 | tf_op jit(solution)/shard_map/ppermute | solution.py:156
  49.0 3.3 %collective-permute-start.9 = (bf16[512,512]{1,0:T(8,128)(2,1)S(1)}, bf16[512,512]{1,0:T(8,128)(2,1)S(1)}, u32[]{:S(2)}, u32[]{:S(2)}) collective-permute-start(bf16[512,512]{1,0:T(8,128)(2,1)S(1)} %collective-permute-done.8.qd8), channel_id=1, source_target_pairs={{8,0},{9,1},{10,2},{11,3},{12,4},{13,5},{14,6},{15,7},{16,8},{17,9... | collective-permute-start | bytes 1572872 | tf_op jit(solution)/shard_map/ppermute | solution.py:156
  52.3 3.7 %collective-permute-done.4.kv16 = bf16[512,512]{1,0:T(8,128)(2,1)S(1)} collective-permute-done((bf16[512,512]{1,0:T(8,128)(2,1)S(1)}, bf16[512,512]{1,0:T(8,128)(2,1)S(1)}, u32[]{:S(2)}, u32[]{:S(2)}) %collective-permute-start.4) | collective-permute-done | bytes 524320 | tf_op jit(solution)/shard_map/ppermute | solution.py:156
  56.0 9.5 %query_side.1 = (bf16[256,512]{1,0:T(8,128)(2,1)}, bf16[256,512]{1,0:T(8,128)(2,1)}, f32[16,256]{1,0:T(8,128)S(1)}) custom-call(s32[4]{0:T(128)S(1)} %copy-done.1, s32[4,4]{1,0:T(4,128)S(1)} %copy-done, bf16[512,512]{1,0:T(8,128)(2,1)S(1)} %constant_dynamic-update-slice_fusion.qd.qd0, bf16[512,512]{1,0:T(8,128)(2,1)S(1)} %constant_dynamic-update-slice_fusion.2.kv0.kv, ...), custom_call_target="tpu_custom_call" | custom-call | flops 603979776 | bytes 4718592 | tf_op jit(solution)/shard_map/query_side/pallas_call | solution.py:176
  65.5 7.6 %collective-permute-start.14 = (f32[16,256]{1,0:T(8,128)S(1)}, f32[16,256]{1,0:T(8,128)S(1)}, u32[]{:S(2)}, u32[]{:S(2)}) collective-permute-start(f32[16,256]{1,0:T(8,128)S(1)} %get-tuple-element.11.st0), channel_id=1, source_target_pairs={{16,0},{17,1},{18,2},{19,3},{20,4},{21,5},{22,6},{23,7},{24,8},{25... | collective-permute-start | bytes 49160 | tf_op jit(solution)/shard_map/ppermute | solution.py:156
  73.1 1.3 %collective-permute-start.13 = (f32[16,256]{1,0:T(8,128)S(1)}, f32[16,256]{1,0:T(8,128)S(1)}, u32[]{:S(2)}, u32[]{:S(2)}) collective-permute-start(f32[16,256]{1,0:T(8,128)S(1)} %get-tuple-element.11.st0), channel_id=1, source_target_pairs={{8,0},{9,1},{10,2},{11,3},{12,4},{13,5},{14,6},{15,7},{16,8},{17,9... | collective-permute-start | bytes 49160 | tf_op jit(solution)/shard_map/ppermute | solution.py:156
  74.4 1.3 %collective-permute-start.12 = (f32[16,256]{1,0:T(8,128)S(1)}, f32[16,256]{1,0:T(8,128)S(1)}, u32[]{:S(2)}, u32[]{:S(2)}) collective-permute-start(f32[16,256]{1,0:T(8,128)S(1)} %get-tuple-element.11.st0), channel_id=1, source_target_pairs={{4,0},{5,1},{6,2},{7,3},{8,4},{9,5},{10,6},{11,7},{12,8},{13,9},{1... | collective-permute-start | bytes 49160 | tf_op jit(solution)/shard_map/ppermute | solution.py:156
  75.7 17.5 %collective-permute-start.11 = (f32[16,256]{1,0:T(8,128)S(1)}, f32[16,256]{1,0:T(8,128)S(1)}, u32[]{:S(2)}, u32[]{:S(2)}) collective-permute-start(f32[16,256]{1,0:T(8,128)S(1)} %get-tuple-element.11.st0), channel_id=1, source_target_pairs={{2,0},{3,1},{4,2},{5,3},{6,4},{7,5},{8,6},{9,7},{10,8},{11,9},{12,... | collective-permute-start | bytes 49160 | tf_op jit(solution)/shard_map/ppermute | solution.py:156
  93.2 1.9 %collective-permute-start.10 = (f32[16,256]{1,0:T(8,128)S(1)}, f32[16,256]{1,0:T(8,128)S(1)}, u32[]{:S(2)}, u32[]{:S(2)}) collective-permute-start(f32[16,256]{1,0:T(8,128)S(1)} %get-tuple-element.11.st0), channel_id=1, source_target_pairs={{1,0},{2,1},{3,2},{4,3},{5,4},{6,5},{7,6},{8,7},{9,8},{10,9},{11,1... | collective-permute-start | bytes 49160 | tf_op jit(solution)/shard_map/ppermute | solution.py:156
  95.2 3.1 %collective-permute-done.10.st1 = f32[16,256]{1,0:T(8,128)S(1)} collective-permute-done((f32[16,256]{1,0:T(8,128)S(1)}, f32[16,256]{1,0:T(8,128)S(1)}, u32[]{:S(2)}, u32[]{:S(2)}) %collective-permute-start.10) | collective-permute-done | bytes 16416 | tf_op jit(solution)/shard_map/ppermute | solution.py:156
  98.3 7.1 %key_side.1 = (bf16[256,512]{1,0:T(8,128)(2,1)}, bf16[256,512]{1,0:T(8,128)(2,1)}) custom-call(s32[4]{0:T(128)S(1)} %copy-done.1, bf16[512,512]{1,0:T(8,128)(2,1)S(1)} %constant_dynamic-update-slice_fusion.2.kv0.kv, bf16[512,512]{1,0:T(8,128)(2,1)S(1)} %constant_dynamic-update-slice_fusion.qd.qd0, bf16[512,512]{1,0:T(8,128)(2,1)S(1)} %collective-permute-done.5.qd1, ...), custom_call_target="tpu_custom_call" | custom-call | flops 1610612736 | bytes 4718592 | tf_op jit(solution)/shard_map/key_side/pallas_call | solution.py:192
  (22 shorter events, 0.1 us)
Async XLA Ops:
  0.6 1.0 copy-start.2
  1.7 1.5 %copy-start.3 = (bf16[256,512]{1,0:T(8,128)(2,1)S(1)}, bf16[256,512]{1,0:T(8,128)(2,1)}, u32[]{:S(2)}) copy-start(bf16[256,512]{1,0:T(8,128)(2,1)} %param.6) | copy-start | bytes 786436
  1.7 1.5 %copy-start.4 = (bf16[256,512]{1,0:T(8,128)(2,1)S(1)}, bf16[256,512]{1,0:T(8,128)(2,1)}, u32[]{:S(2)}) copy-start(bf16[256,512]{1,0:T(8,128)(2,1)} %param.9) | copy-start | bytes 786436
  1.7 14.8 %collective-permute-start.2 = (bf16[512,512]{1,0:T(8,128)(2,1)S(1)}, bf16[512,512]{1,0:T(8,128)(2,1)S(1)}, u32[]{:S(2)}, u32[]{:S(2)}) collective-permute-start(bf16[512,512]{1,0:T(8,128)(2,1)S(1)} %constant_dynamic-update-slice_fusion.2.kv0.kv), channel_id=1, source_target_pairs={{0,4},{1,5},{2,6},{3,7},{4,8},{5,9},{6,10},{7,11},{8,12},{9,13},{1... | collective-permute-start | bytes 1572872 | tf_op jit(solution)/shard_map/ppermute | solution.py:156
  3.2 52.8 %copy-start = (s32[4,4]{1,0:T(4,128)S(1)}, s32[4,4]{1,0:T(4,128)}, u32[]{:S(2)}) copy-start(s32[4,4]{1,0:T(4,128)} %off.1) | copy-start | bytes 196
  3.2 52.8 %copy-start.1 = (s32[4]{0:T(128)S(1)}, s32[4]{0:T(128)}, u32[]{:S(2)}) copy-start(s32[4]{0:T(128)} %win.3) | copy-start | bytes 52
  3.2 17.7 %collective-permute-start.7 = (bf16[512,512]{1,0:T(8,128)(2,1)S(1)}, bf16[512,512]{1,0:T(8,128)(2,1)S(1)}, u32[]{:S(2)}, u32[]{:S(2)}) collective-permute-start(bf16[512,512]{1,0:T(8,128)(2,1)S(1)} %constant_dynamic-update-slice_fusion.qd.qd0), channel_id=1, source_target_pairs={{4,0},{5,1},{6,2},{7,3},{8,4},{9,5},{10,6},{11,7},{12,8},{13,9},{1... | collective-permute-start | bytes 1572872 | tf_op jit(solution)/shard_map/ppermute | solution.py:156
  16.5 13.8 %collective-permute-start.3 = (bf16[512,512]{1,0:T(8,128)(2,1)S(1)}, bf16[512,512]{1,0:T(8,128)(2,1)S(1)}, u32[]{:S(2)}, u32[]{:S(2)}) collective-permute-start(bf16[512,512]{1,0:T(8,128)(2,1)S(1)} %collective-permute-done.2.kv4), channel_id=1, source_target_pairs={{0,4},{1,5},{2,6},{3,7},{4,8},{5,9},{6,10},{7,11},{8,12},{9,13},{1... | collective-permute-start | bytes 1572872 | tf_op jit(solution)/shard_map/ppermute | solution.py:156
  17.8 24.7 %collective-permute-start.1 = (bf16[512,512]{1,0:T(8,128)(2,1)S(1)}, bf16[512,512]{1,0:T(8,128)(2,1)S(1)}, u32[]{:S(2)}, u32[]{:S(2)}) collective-permute-start(bf16[512,512]{1,0:T(8,128)(2,1)S(1)} %constant_dynamic-update-slice_fusion.2.kv0.kv), channel_id=1, source_target_pairs={{0,2},{1,3},{2,4},{3,5},{4,6},{5,7},{6,8},{7,9},{8,10},{9,11},{10,... | collective-permute-start | bytes 1572872 | tf_op jit(solution)/shard_map/ppermute | solution.py:156
  21.0 28.0 %collective-permute-start.8 = (bf16[512,512]{1,0:T(8,128)(2,1)S(1)}, bf16[512,512]{1,0:T(8,128)(2,1)S(1)}, u32[]{:S(2)}, u32[]{:S(2)}) collective-permute-start(bf16[512,512]{1,0:T(8,128)(2,1)S(1)} %collective-permute-done.7.qd4), channel_id=1, source_target_pairs={{4,0},{5,1},{6,2},{7,3},{8,4},{9,5},{10,6},{11,7},{12,8},{13,9},{1... | collective-permute-start | bytes 1572872 | tf_op jit(solution)/shard_map/ppermute | solution.py:156
  25.0 27.3 %collective-permute-start = (bf16[512,512]{1,0:T(8,128)(2,1)S(1)}, bf16[512,512]{1,0:T(8,128)(2,1)S(1)}, u32[]{:S(2)}, u32[]{:S(2)}) collective-permute-start(bf16[512,512]{1,0:T(8,128)(2,1)S(1)} %constant_dynamic-update-slice_fusion.2.kv0.kv), channel_id=1, source_target_pairs={{0,1},{1,2},{2,3},{3,4},{4,5},{5,6},{6,7},{7,8},{8,9},{9,10},{10,1... | collective-permute-start | bytes 1572872 | tf_op jit(solution)/shard_map/ppermute | solution.py:156
  30.3 25.7 %collective-permute-start.4 = (bf16[512,512]{1,0:T(8,128)(2,1)S(1)}, bf16[512,512]{1,0:T(8,128)(2,1)S(1)}, u32[]{:S(2)}, u32[]{:S(2)}) collective-permute-start(bf16[512,512]{1,0:T(8,128)(2,1)S(1)} %collective-permute-done.3.kv8), channel_id=1, source_target_pairs={{0,8},{1,9},{2,10},{3,11},{4,12},{5,13},{6,14},{7,15},{8,16},{9,17... | collective-permute-start | bytes 1572872 | tf_op jit(solution)/shard_map/ppermute | solution.py:156
  31.6 42.8 %collective-permute-start.6 = (bf16[512,512]{1,0:T(8,128)(2,1)S(1)}, bf16[512,512]{1,0:T(8,128)(2,1)S(1)}, u32[]{:S(2)}, u32[]{:S(2)}) collective-permute-start(bf16[512,512]{1,0:T(8,128)(2,1)S(1)} %constant_dynamic-update-slice_fusion.qd.qd0), channel_id=1, source_target_pairs={{2,0},{3,1},{4,2},{5,3},{6,4},{7,5},{8,6},{9,7},{10,8},{11,9},{12,... | collective-permute-start | bytes 1572872 | tf_op jit(solution)/shard_map/ppermute | solution.py:156
  42.5 33.2 %collective-permute-start.5 = (bf16[512,512]{1,0:T(8,128)(2,1)S(1)}, bf16[512,512]{1,0:T(8,128)(2,1)S(1)}, u32[]{:S(2)}, u32[]{:S(2)}) collective-permute-start(bf16[512,512]{1,0:T(8,128)(2,1)S(1)} %constant_dynamic-update-slice_fusion.qd.qd0), channel_id=1, source_target_pairs={{1,0},{2,1},{3,2},{4,3},{5,4},{6,5},{7,6},{8,7},{9,8},{10,9},{11,1... | collective-permute-start | bytes 1572872 | tf_op jit(solution)/shard_map/ppermute | solution.py:156
  49.0 44.2 %collective-permute-start.9 = (bf16[512,512]{1,0:T(8,128)(2,1)S(1)}, bf16[512,512]{1,0:T(8,128)(2,1)S(1)}, u32[]{:S(2)}, u32[]{:S(2)}) collective-permute-start(bf16[512,512]{1,0:T(8,128)(2,1)S(1)} %collective-permute-done.8.qd8), channel_id=1, source_target_pairs={{8,0},{9,1},{10,2},{11,3},{12,4},{13,5},{14,6},{15,7},{16,8},{17,9... | collective-permute-start | bytes 1572872 | tf_op jit(solution)/shard_map/ppermute | solution.py:156
  65.5 29.7 %collective-permute-start.14 = (f32[16,256]{1,0:T(8,128)S(1)}, f32[16,256]{1,0:T(8,128)S(1)}, u32[]{:S(2)}, u32[]{:S(2)}) collective-permute-start(f32[16,256]{1,0:T(8,128)S(1)} %get-tuple-element.11.st0), channel_id=1, source_target_pairs={{16,0},{17,1},{18,2},{19,3},{20,4},{21,5},{22,6},{23,7},{24,8},{25... | collective-permute-start | bytes 49160 | tf_op jit(solution)/shard_map/ppermute | solution.py:156
  73.1 22.1 %collective-permute-start.13 = (f32[16,256]{1,0:T(8,128)S(1)}, f32[16,256]{1,0:T(8,128)S(1)}, u32[]{:S(2)}, u32[]{:S(2)}) collective-permute-start(f32[16,256]{1,0:T(8,128)S(1)} %get-tuple-element.11.st0), channel_id=1, source_target_pairs={{8,0},{9,1},{10,2},{11,3},{12,4},{13,5},{14,6},{15,7},{16,8},{17,9... | collective-permute-start | bytes 49160 | tf_op jit(solution)/shard_map/ppermute | solution.py:156
  74.4 20.8 %collective-permute-start.12 = (f32[16,256]{1,0:T(8,128)S(1)}, f32[16,256]{1,0:T(8,128)S(1)}, u32[]{:S(2)}, u32[]{:S(2)}) collective-permute-start(f32[16,256]{1,0:T(8,128)S(1)} %get-tuple-element.11.st0), channel_id=1, source_target_pairs={{4,0},{5,1},{6,2},{7,3},{8,4},{9,5},{10,6},{11,7},{12,8},{13,9},{1... | collective-permute-start | bytes 49160 | tf_op jit(solution)/shard_map/ppermute | solution.py:156
  75.7 19.5 %collective-permute-start.11 = (f32[16,256]{1,0:T(8,128)S(1)}, f32[16,256]{1,0:T(8,128)S(1)}, u32[]{:S(2)}, u32[]{:S(2)}) collective-permute-start(f32[16,256]{1,0:T(8,128)S(1)} %get-tuple-element.11.st0), channel_id=1, source_target_pairs={{2,0},{3,1},{4,2},{5,3},{6,4},{7,5},{8,6},{9,7},{10,8},{11,9},{12,... | collective-permute-start | bytes 49160 | tf_op jit(solution)/shard_map/ppermute | solution.py:156
  93.2 5.1 %collective-permute-start.10 = (f32[16,256]{1,0:T(8,128)S(1)}, f32[16,256]{1,0:T(8,128)S(1)}, u32[]{:S(2)}, u32[]{:S(2)}) collective-permute-start(f32[16,256]{1,0:T(8,128)S(1)} %get-tuple-element.11.st0), channel_id=1, source_target_pairs={{1,0},{2,1},{3,2},{4,3},{5,4},{6,5},{7,6},{8,7},{9,8},{10,9},{11,1... | collective-permute-start | bytes 49160 | tf_op jit(solution)/shard_map/ppermute | solution.py:156

commit v2 on v1

v2 whole, which is shorter than its diff:
```python
import jax
import jax.numpy as jnp
from jax import lax
from jax.experimental import pallas as pl
from jax.experimental.pallas import tpu as pltpu
from jax.sharding import PartitionSpec as P

HEADS = 4
HEAD_DIM = 128
FEAT = HEADS * HEAD_DIM
ROWS = 256
BLOCK = 64
BLOCKS = ROWS // BLOCK
LEVELS = 4
SCALE = HEAD_DIM**-0.5
MASKED = -1e30
STAT_ROWS = 16
F32 = jnp.float32
BF16 = jnp.bfloat16


def rows_by_rows(a, b):
    return lax.dot_general(a, b, (((1,), (1,)), ((), ())), preferred_element_type=F32)


def rows_by_columns(a, b):
    return lax.dot_general(a, b, (((1,), (0,)), ((), ())), preferred_element_type=F32)


def picks_of(off, p):
    rows = []
    for j in range(LEVELS):
        picked = jnp.clip(BLOCKS * 2 ** (j + 1) + p - off[p, j], 0, BLOCKS - 1)
        rows.append(pl.multiple_of(picked * BLOCK, BLOCK))
    return rows


def block_keys(p, head, base, own, before, levels, picks):
    parts = []
    if before is not None:
        parts.append(before[base + BLOCK * p : base + ROWS, head])
    if own is not None:
        parts.append(own[base : base + BLOCK * (p + 1), head])
    for j, ref in levels:
        parts.append(ref[pl.ds(base + picks[j], BLOCK), head])
    return jnp.concatenate(parts, 0)


def block_bias(p, rank, length, own, before, levels):
    pieces = []
    row = lambda n: lax.broadcasted_iota(jnp.int32, (BLOCK, n), 0)
    col = lambda n: lax.broadcasted_iota(jnp.int32, (BLOCK, n), 1)
    if before:
        n = ROWS - BLOCK * p
        pieces.append((col(n) - row(n) > ROWS - length) & (rank > 0))
    if own:
        n = BLOCK * (p + 1)
        gap = BLOCK * p + row(n) - col(n)
        pieces.append((gap >= 0) & (gap < length))
    for j in levels:
        pieces.append((col(BLOCK) >= 0) & (rank >= 2 ** (j + 1)))
    return jnp.concatenate([jnp.where(x, F32(0), F32(MASKED)) for x in pieces], 1)


def across(column, width):
    return jnp.broadcast_to(column, (column.shape[0], width))


def widened(rows, width):
    return jnp.concatenate([rows] * (-(-width // 128)), 1)[:, :width]


def head_columns(h):
    return slice(HEAD_DIM * h, HEAD_DIM * (h + 1))


def with_ones(v):
    return jnp.concatenate([v, jnp.ones((v.shape[0], HEAD_DIM), BF16)], 1)


def early_attention(win, off, qd, kv0, kv4, kv8, acc, top_out, total_out):
    rank = lax.axis_index("ctx")
    levels = ((1, kv4), (2, kv8))
    heads = range(HEADS)
    for p in range(BLOCKS):
        picks = picks_of(off, p)
        mine = slice(BLOCK * p, BLOCK * (p + 1))
        k = [block_keys(p, head_columns(h), 0, kv0, None, levels, picks) for h in heads]
        v = [block_keys(p, head_columns(h), ROWS, kv0, None, levels, picks) for h in heads]
        width = k[0].shape[0]
        scores = [rows_by_rows(qd[mine, head_columns(h)], k[h]) for h in heads]
        scores = [scores[h] * SCALE + block_bias(p, rank, win[h], True, False, (1, 2)) for h in heads]
        top = [across(jnp.max(s, 1, keepdims=True), HEAD_DIM) for s in scores]
        weights = [jnp.exp(scores[h] - widened(top[h], width)).astype(BF16) for h in heads]
        sums = [rows_by_columns(weights[h], with_ones(v[h])) for h in heads]
        for h in heads:
            acc[mine, head_columns(h)] = sums[h][:, :HEAD_DIM]
            total_out[mine, head_columns(h)] = sums[h][:, HEAD_DIM:]
            top_out[mine, head_columns(h)] = top[h]


def late_attention(win, off, qd, kv1, kv2, kv16, acc, top0, total0, att, stats, tall):
    rank = lax.axis_index("ctx")
    levels = ((0, kv2), (3, kv16))
    heads = range(HEADS)
    lane = lax.broadcasted_iota(jnp.int32, (BLOCK, 128), 1)
    for p in range(BLOCKS):
        picks = picks_of(off, p)
        mine = slice(BLOCK * p, BLOCK * (p + 1))
        theirs = slice(ROWS + BLOCK * p, ROWS + BLOCK * (p + 1))
        k = [block_keys(p, head_columns(h), 0, None, kv1, levels, picks) for h in heads]
        v = [block_keys(p, head_columns(h), ROWS, None, kv1, levels, picks) for h in heads]
        width = k[0].shape[0]
        scores = [rows_by_rows(qd[mine, head_columns(h)], k[h]) for h in heads]
        scores = [scores[h] * SCALE + block_bias(p, rank, win[h], False, True, (0, 3)) for h in heads]
        before = [top0[mine, head_columns(h)] for h in heads]
        top = [jnp.maximum(before[h], across(jnp.max(scores[h], 1, keepdims=True), HEAD_DIM)) for h in heads]
        weights = [jnp.exp(scores[h] - widened(top[h], width)).astype(BF16) for h in heads]
        fade = [jnp.exp(before[h] - top[h]) for h in heads]
        sums = [rows_by_columns(weights[h], with_ones(v[h])) for h in heads]
        total = [total0[mine, head_columns(h)] * fade[h] + sums[h][:, HEAD_DIM:] for h in heads]
        out = [acc[mine, head_columns(h)] * fade[h] + sums[h][:, :HEAD_DIM] for h in heads]
        out = [(out[h] * (1.0 / total[h])).astype(BF16) for h in heads]
        lse = [top[h] + jnp.log(total[h]) for h in heads]
        delta = [
            across(jnp.sum(qd[theirs, head_columns(h)].astype(F32) * out[h].astype(F32), 1, keepdims=True), HEAD_DIM)
            for h in heads
        ]
        kept = jnp.zeros((BLOCK, 128), F32)
        for h in heads:
            att[mine, head_columns(h)] = out[h]
            kept = jnp.where(lane == h, lse[h], kept)
            kept = jnp.where(lane == HEADS + h, delta[h], kept)
        tall[mine, :] = kept
    stats[0 : 2 * HEADS, :] = tall[...].T[0 : 2 * HEADS]
    wide_row = lax.broadcasted_iota(jnp.int32, (STAT_ROWS - 2 * HEADS, ROWS), 0)
    wide_block = lax.broadcasted_iota(jnp.int32, (STAT_ROWS - 2 * HEADS, ROWS), 1) // BLOCK
    chosen = jnp.zeros((STAT_ROWS - 2 * HEADS, ROWS), F32)
    for p in range(BLOCKS):
        for j in range(LEVELS):
            picked = jnp.clip(BLOCKS * 2 ** (j + 1) + p - off[p, j], 0, BLOCKS - 1)
            chosen = jnp.where((wide_row == j) & (wide_block == p), picked.astype(F32), chosen)
    stats[2 * HEADS :, :] = chosen


def query_gradient(win, off, qd, kv0, kv1, kv2, kv4, kv8, kv16, tall, dq):
    rank = lax.axis_index("ctx")
    levels = ((0, kv2), (1, kv4), (2, kv8), (3, kv16))
    heads = range(HEADS)
    for p in range(BLOCKS):
        picks = picks_of(off, p)
        mine = slice(BLOCK * p, BLOCK * (p + 1))
        theirs = slice(ROWS + BLOCK * p, ROWS + BLOCK * (p + 1))
        k = [block_keys(p, head_columns(h), 0, kv0, kv1, levels, picks) for h in heads]
        v = [block_keys(p, head_columns(h), ROWS, kv0, kv1, levels, picks) for h in heads]
        scores = [rows_by_rows(qd[mine, head_columns(h)], k[h]) for h in heads]
        dprob = [rows_by_rows(qd[theirs, head_columns(h)], v[h]) for h in heads]
        scores = [scores[h] * SCALE + block_bias(p, rank, win[h], True, True, range(LEVELS)) for h in heads]
        probs = [jnp.exp(scores[h] - tall[mine, h : h + 1]) for h in heads]
        dscore = [(probs[h] * (dprob[h] - tall[mine, HEADS + h : HEADS + h + 1])).astype(BF16) for h in heads]
        for h in heads:
            dq[mine, head_columns(h)] = (rows_by_columns(dscore[h], k[h]) * SCALE).astype(BF16)


def key_side(win, kv, qd0, qd1, qd2, qd4, qd8, qd16, st0, st1, st2, st4, st8, st16, dk, dv):
    far = ((qd2, st2), (qd4, st4), (qd8, st8), (qd16, st16))
    half = ROWS // 2
    wide = ROWS + half
    key_block = (lax.broadcasted_iota(jnp.int32, (ROWS, ROWS), 0) // BLOCK).astype(F32)
    row = lax.broadcasted_iota(jnp.int32, (half, wide), 0)
    col = lax.broadcasted_iota(jnp.int32, (half, wide), 1)
    gap = col - row

    def tiles(h):
        head = head_columns(h)
        out = []
        allowed = (gap >= 0) & (gap < win[h])
        for c in range(2):
            cut = half * c
            both = lambda base: jnp.concatenate(
                [qd0[base + cut : base + ROWS, head], qd1[base : base + cut + half, head]], 0
            )
            lanes = lambda r: jnp.concatenate([st0[r : r + 1, cut:ROWS], st1[r : r + 1, 0 : cut + half]], 1)
            mine = slice(cut, cut + half)
            theirs = slice(ROWS + cut, ROWS + cut + half)
            out.append((kv[mine, head], kv[theirs, head], both(0), both(ROWS), lanes(h), lanes(HEADS + h), allowed))
        for j in range(LEVELS):
            qd, st = far[j]
            out.append(
                (
                    kv[0:ROWS, head],
                    kv[ROWS : 2 * ROWS, head],
                    qd[0:ROWS, head],
                    qd[ROWS : 2 * ROWS, head],
                    st[h : h + 1, :],
                    st[HEADS + h : HEADS + h + 1, :],
                    key_block == st[2 * HEADS + j : 2 * HEADS + j + 1, :],
                )
            )
        return out

    for h in range(HEADS):
        all_tiles = tiles(h)
        scores = [rows_by_rows(k, q) for k, _, q, _, _, _, _ in all_tiles]
        dprob = [rows_by_rows(v, do) for _, v, _, do, _, _, _ in all_tiles]
        probs = [
            jnp.exp(jnp.where(t[6], s * SCALE - t[4], F32(MASKED))) for s, t in zip(scores, all_tiles)
        ]
        dscore = [(p * (d - t[5])).astype(BF16) for p, d, t in zip(probs, dprob, all_tiles)]
        wide_q = jnp.concatenate([t[2] for t in all_tiles[2:]], 0)
        wide_do = jnp.concatenate([t[3] for t in all_tiles[2:]], 0)
        near_dv = jnp.concatenate([rows_by_columns(p.astype(BF16), t[3]) for p, t in zip(probs[:2], all_tiles)], 0)
        near_dk = jnp.concatenate([rows_by_columns(d, t[2]) for d, t in zip(dscore[:2], all_tiles)], 0)
        far_dv = rows_by_columns(jnp.concatenate([p.astype(BF16) for p in probs[2:]], 1), wide_do)
        far_dk = rows_by_columns(jnp.concatenate(dscore[2:], 1), wide_q)
        dk[:, head_columns(h)] = ((near_dk + far_dk) * SCALE).astype(BF16)
        dv[:, head_columns(h)] = (near_dv + far_dv).astype(BF16)


def moved(array, by):
    size = lax.axis_size("ctx")
    return lax.ppermute(array, "ctx", [(i, i + by) for i in range(size) if 0 <= i + by < size])


def swapped(array, bit):
    size = lax.axis_size("ctx")
    return lax.ppermute(array, "ctx", [(i, i ^ bit) for i in range(size)])


def kernel(body, out_shape, n_smem, n_vmem, flops, scratch=()):
    smem = pl.BlockSpec(memory_space=pltpu.SMEM)
    vmem = pl.BlockSpec(memory_space=pltpu.VMEM)
    return pl.pallas_call(
        body,
        out_shape=tuple(out_shape),
        in_specs=[smem] * n_smem + [vmem] * n_vmem,
        out_specs=(vmem,) * len(out_shape),
        scratch_shapes=list(scratch),
        compiler_params=pltpu.CompilerParams(vmem_limit_bytes=32 * 2**20),
        cost_estimate=pl.CostEstimate(flops=flops, bytes_accessed=n_vmem * ROWS * FEAT * 4, transcendentals=0),
        name=body.__name__,
    )


def on_device(queries, keys, values, grad_out, window, offsets):
    rank = lax.axis_index("ctx")
    kv0 = jnp.concatenate([keys, values], 0)
    qd0 = jnp.concatenate([queries, grad_out], 0)
    kv4 = moved(kv0, 4)
    qd4 = moved(qd0, -4)
    kv2 = swapped(jnp.where(rank % 4 < 2, kv0, kv4), 2)
    qd2 = swapped(jnp.where(rank % 4 < 2, qd4, qd0), 2)
    kv1 = swapped(jnp.where(rank % 2 == 0, kv0, kv2), 1)
    qd1 = swapped(jnp.where(rank % 2 == 0, qd2, qd0), 1)
    kv8 = moved(kv4, 4)
    qd8 = moved(qd4, -4)
    kv16 = moved(kv8, 8)
    qd16 = moved(qd8, -8)
    half = jax.ShapeDtypeStruct((ROWS, FEAT), BF16)
    whole = jax.ShapeDtypeStruct((ROWS, FEAT), F32)
    table = jax.ShapeDtypeStruct((ROWS, 128), F32)
    stat = jax.ShapeDtypeStruct((STAT_ROWS, ROWS), F32)
    unit = 2 * ROWS * FEAT
    early = kernel(early_attention, (whole,) * 3, 2, 4, unit * 2 * 320)(
        window, offsets, qd0, kv0, kv4, kv8
    )
    attended, stats, tall = kernel(late_attention, (half, stat, table), 2, 7, unit * 2 * 320)(
        window, offsets, qd0, kv1, kv2, kv16, *early
    )
    received = [moved(stats, -by) for by in (16, 8, 4, 2, 1)][::-1]
    (grad_q,) = kernel(query_gradient, (half,), 2, 8, unit * 3 * 576)(
        window, offsets, qd0, kv0, kv1, kv2, kv4, kv8, kv16, tall
    )
    grad_k, grad_v = kernel(key_side, (half, half), 1, 13, unit * 4 * 6 * ROWS)(
        window, kv0, qd0, qd1, qd2, qd4, qd8, qd16, stats, *received
    )
    return attended, grad_q, grad_k, grad_v


def solution(mesh):
    split = P(("dp", "ctx"), None)
    return jax.shard_map(
        on_device,
        mesh=mesh,
        in_specs=(split, split, split, split, P(), split),
        out_specs=(split,) * 4,
        check_vma=False,
    )
```

time: 106 us -> 92.6 us (0.87)
  the two profiles are of different devices: /device:TPU:249 before, /device:TPU:1 now
where the time goes in v2:
time: 92.6 us; the launch traced here: 92.1 us
  waiting for transfers between devices  37 us (40%)
  starting transfers between devices  36.5 us (39%)
  Pallas kernels  14.8 us (16%)
  other arithmetic  1.83 us (2%)
  local copies, waits for them, and re-layouts  1.1 us (1%)
    ppermute x11, waiting for transfers between devices, moved(): lax.ppermute(array, 'ctx', [(i, i + by) for i in range(size) if 0 <= i +...  31.5 us
    ppermute x11, starting transfers between devices, moved(): lax.ppermute(array, 'ctx', [(i, i + by) for i in range(size) if 0 <= i +...  26.8 us
    ppermute x4, starting transfers between devices, swapped(): return lax.ppermute(array, 'ctx', [(i, i ^ bit) for i in range(size)])  9.68 us
    pallas_call x1, Pallas kernels, on_device(): kernel(key_side, (half, half), 1, 13, unit * 4 * 6 * ROWS)  5.95 us
    ppermute x4, waiting for transfers between devices, swapped(): return lax.ppermute(array, 'ctx', [(i, i ^ bit) for i in range(size)])  5.47 us
    pallas_call x1, Pallas kernels, on_device(): kernel(query_gradient, (half,), 2, 8, unit * 3 * 576)  3.81 us
    pallas_call x1, Pallas kernels, on_device(): kernel(late_attention, (half, stat, table), 2, 7, unit * 2 * 320)  2.9 us
    pallas_call x1, Pallas kernels, on_device(): kernel(early_attention, (whole,) * 3, 2, 4, unit * 2 * 320)  2.11 us
  transfers between devices with their start and end apart: 15, of which 7 were waited for; matrix products, arithmetic and copies ran while one was open for 2% of the time, Pallas kernels for 10%

profile of v2, /device:TPU:1, one launch (start us, length us, event | category | flops | bytes accessed | tf_op | source)
XLA Modules:
  0.0 92.1 jit_solution(16685007257011823155)
XLA Ops:
  1.7 4.5 %collective-permute-start = (bf16[512,512]{1,0:T(8,128)(2,1)S(1)}, bf16[512,512]{1,0:T(8,128)(2,1)S(1)}, u32[]{:S(2)}, u32[]{:S(2)}) collective-permute-start(bf16[512,512]{1,0:T(8,128)(2,1)S(1)} %constant_dynamic-update-slice_fusion.2.kv0.kv), channel_id=1, source_target_pairs={{0,4},{1,5},{2,6},{3,7},{4,8},{5,9},{6,10},{7,11},{8,12},{9,13},{1... | collective-permute-start | bytes 1572872 | tf_op jit(solution)/shard_map/ppermute | solution.py:222
  6.3 1.3 %collective-permute-start.5 = (bf16[512,512]{1,0:T(8,128)(2,1)S(1)}, bf16[512,512]{1,0:T(8,128)(2,1)S(1)}, u32[]{:S(2)}, u32[]{:S(2)}) collective-permute-start(bf16[512,512]{1,0:T(8,128)(2,1)S(1)} %constant_dynamic-update-slice_fusion.qd.qd0), channel_id=1, source_target_pairs={{4,0},{5,1},{6,2},{7,3},{8,4},{9,5},{10,6},{11,7},{12,8},{13,9},{1... | collective-permute-start | bytes 1572872 | tf_op jit(solution)/shard_map/ppermute | solution.py:222
  7.6 9.2 %collective-permute-done.kv4 = bf16[512,512]{1,0:T(8,128)(2,1)S(1)} collective-permute-done((bf16[512,512]{1,0:T(8,128)(2,1)S(1)}, bf16[512,512]{1,0:T(8,128)(2,1)S(1)}, u32[]{:S(2)}, u32[]{:S(2)}) %collective-permute-start) | collective-permute-done | bytes 524320 | tf_op jit(solution)/shard_map/ppermute | solution.py:222
  17.7 1.2 %collective-permute-start.1 = (bf16[512,512]{1,0:T(8,128)(2,1)}, bf16[512,512]{1,0:T(8,128)(2,1)S(1)}, u32[]{:S(2)}, u32[]{:S(2)}) collective-permute-start(bf16[512,512]{1,0:T(8,128)(2,1)} %broadcast_select_fusion.1), channel_id=1, source_target_pairs={{0,2},{1,3},{2,0},{3,1},{4,6},{5,7},{6,4},{7,5},{8,10},{9,11},{10,... | collective-permute-start | bytes 1572872 | tf_op jit(solution)/shard_map/ppermute | solution.py:227
  18.9 4.1 %collective-permute-start.3 = (bf16[512,512]{1,0:T(8,128)(2,1)S(1)}, bf16[512,512]{1,0:T(8,128)(2,1)S(1)}, u32[]{:S(2)}, u32[]{:S(2)}) collective-permute-start(bf16[512,512]{1,0:T(8,128)(2,1)S(1)} %collective-permute-done.kv4), channel_id=1, source_target_pairs={{0,4},{1,5},{2,6},{3,7},{4,8},{5,9},{6,10},{7,11},{8,12},{9,13},{1... | collective-permute-start | bytes 1572872 | tf_op jit(solution)/shard_map/ppermute | solution.py:222
  24.1 1.3 %collective-permute-start.8 = (bf16[512,512]{1,0:T(8,128)(2,1)S(1)}, bf16[512,512]{1,0:T(8,128)(2,1)S(1)}, u32[]{:S(2)}, u32[]{:S(2)}) collective-permute-start(bf16[512,512]{1,0:T(8,128)(2,1)S(1)} %collective-permute-done.5.qd4), channel_id=1, source_target_pairs={{4,0},{5,1},{6,2},{7,3},{8,4},{9,5},{10,6},{11,7},{12,8},{13,9},{1... | collective-permute-start | bytes 1572872 | tf_op jit(solution)/shard_map/ppermute | solution.py:222
  25.4 4.3 %collective-permute-done.1.kv2 = bf16[512,512]{1,0:T(8,128)(2,1)S(1)} collective-permute-done((bf16[512,512]{1,0:T(8,128)(2,1)}, bf16[512,512]{1,0:T(8,128)(2,1)S(1)}, u32[]{:S(2)}, u32[]{:S(2)}) %collective-permute-start.1) | collective-permute-done | bytes 524320 | tf_op jit(solution)/shard_map/ppermute | solution.py:227
  29.8 4.6 %collective-permute-start.2 = (bf16[512,512]{1,0:T(8,128)(2,1)S(1)}, bf16[512,512]{1,0:T(8,128)(2,1)S(1)}, u32[]{:S(2)}, u32[]{:S(2)}) collective-permute-start(bf16[512,512]{1,0:T(8,128)(2,1)S(1)} %broadcast_select_fusion.3), channel_id=1, source_target_pairs={{0,1},{1,0},{2,3},{3,2},{4,5},{5,4},{6,7},{7,6},{8,9},{9,8},{10,11... | collective-permute-start | bytes 1572872 | tf_op jit(solution)/shard_map/ppermute | solution.py:227
  34.5 5.5 %collective-permute-start.4 = (bf16[512,512]{1,0:T(8,128)(2,1)S(1)}, bf16[512,512]{1,0:T(8,128)(2,1)S(1)}, u32[]{:S(2)}, u32[]{:S(2)}) collective-permute-start(bf16[512,512]{1,0:T(8,128)(2,1)S(1)} %collective-permute-done.3.kv8), channel_id=1, source_target_pairs={{0,8},{1,9},{2,10},{3,11},{4,12},{5,13},{6,14},{7,15},{8,16},{9,17... | collective-permute-start | bytes 1572872 | tf_op jit(solution)/shard_map/ppermute | solution.py:222
  39.9 1.1 %collective-permute-done.6.qd2 = bf16[512,512]{1,0:T(8,128)(2,1)} collective-permute-done((bf16[512,512]{1,0:T(8,128)(2,1)}, bf16[512,512]{1,0:T(8,128)(2,1)}, u32[]{:S(2)}, u32[]{:S(2)}) %collective-permute-start.6) | collective-permute-done | bytes 524320 | tf_op jit(solution)/shard_map/ppermute | solution.py:227
  41.1 3.6 %collective-permute-start.7 = (bf16[512,512]{1,0:T(8,128)(2,1)S(1)}, bf16[512,512]{1,0:T(8,128)(2,1)S(1)}, u32[]{:S(2)}, u32[]{:S(2)}) collective-permute-start(bf16[512,512]{1,0:T(8,128)(2,1)S(1)} %broadcast_select_fusion.2), channel_id=1, source_target_pairs={{0,1},{1,0},{2,3},{3,2},{4,5},{5,4},{6,7},{7,6},{8,9},{9,8},{10,11... | collective-permute-start | bytes 1572872 | tf_op jit(solution)/shard_map/ppermute | solution.py:227
  44.7 1.3 %collective-permute-start.9 = (bf16[512,512]{1,0:T(8,128)(2,1)S(1)}, bf16[512,512]{1,0:T(8,128)(2,1)S(1)}, u32[]{:S(2)}, u32[]{:S(2)}) collective-permute-start(bf16[512,512]{1,0:T(8,128)(2,1)S(1)} %collective-permute-done.8.qd8), channel_id=1, source_target_pairs={{8,0},{9,1},{10,2},{11,3},{12,4},{13,5},{14,6},{15,7},{16,8},{17,9... | collective-permute-start | bytes 1572872 | tf_op jit(solution)/shard_map/ppermute | solution.py:222
  46.1 2.1 %early_attention.1 = (f32[256,512]{1,0:T(8,128)S(1)}, f32[256,512]{1,0:T(8,128)S(1)}, f32[256,512]{1,0:T(8,128)S(1)}) custom-call(s32[4]{0:T(128)S(1)} %copy-done.1, s32[4,4]{1,0:T(4,128)S(1)} %copy-done, bf16[512,512]{1,0:T(8,128)(2,1)S(1)} %constant_dynamic-update-slice_fusion.qd.qd0, bf16[512,512]{1,0:T(8,128)(2,1)S(1)} %constant_dynamic-update-slice_fusion.2.kv0.kv, ...), custom_call_target="tpu_custom_call" | custom-call | flops 167772160 | bytes 2097152 | tf_op jit(solution)/shard_map/early_attention/pallas_call | solution.py:264
  48.2 2.3 %collective-permute-done.4.kv16 = bf16[512,512]{1,0:T(8,128)(2,1)S(1)} collective-permute-done((bf16[512,512]{1,0:T(8,128)(2,1)S(1)}, bf16[512,512]{1,0:T(8,128)(2,1)S(1)}, u32[]{:S(2)}, u32[]{:S(2)}) %collective-permute-start.4) | collective-permute-done | bytes 524320 | tf_op jit(solution)/shard_map/ppermute | solution.py:222
  50.5 2.9 %late_attention.1 = (bf16[256,512]{1,0:T(8,128)(2,1)}, f32[16,256]{1,0:T(8,128)S(1)}, f32[256,128]{1,0:T(8,128)S(1)}) custom-call(s32[4]{0:T(128)S(1)} %copy-done.1, s32[4,4]{1,0:T(4,128)S(1)} %copy-done, bf16[512,512]{1,0:T(8,128)(2,1)S(1)} %constant_dynamic-update-slice_fusion.qd.qd0, bf16[512,512]{1,0:T(8,128)(2,1)S(1)} %collective-permute-done.2.kv1, ...), custom_call_target="tpu_custom_call" | custom-call | flops 167772160 | bytes 3670016 | tf_op jit(solution)/shard_map/late_attention/pallas_call | solution.py:267
  53.4 3.5 %collective-permute-start.10 = (f32[16,256]{1,0:T(8,128)S(1)}, f32[16,256]{1,0:T(8,128)S(1)}, u32[]{:S(2)}, u32[]{:S(2)}) collective-permute-start(f32[16,256]{1,0:T(8,128)S(1)} %get-tuple-element.17.st0), channel_id=1, source_target_pairs={{1,0},{2,1},{3,2},{4,3},{5,4},{6,5},{7,6},{8,7},{9,8},{10,9},{11,1... | collective-permute-start | bytes 49160 | tf_op jit(solution)/shard_map/ppermute | solution.py:222
  56.9 1.3 %collective-permute-start.11 = (f32[16,256]{1,0:T(8,128)S(1)}, f32[16,256]{1,0:T(8,128)S(1)}, u32[]{:S(2)}, u32[]{:S(2)}) collective-permute-start(f32[16,256]{1,0:T(8,128)S(1)} %get-tuple-element.17.st0), channel_id=1, source_target_pairs={{2,0},{3,1},{4,2},{5,3},{6,4},{7,5},{8,6},{9,7},{10,8},{11,9},{12,... | collective-permute-start | bytes 49160 | tf_op jit(solution)/shard_map/ppermute | solution.py:222
  58.2 1.3 %collective-permute-start.12 = (f32[16,256]{1,0:T(8,128)S(1)}, f32[16,256]{1,0:T(8,128)S(1)}, u32[]{:S(2)}, u32[]{:S(2)}) collective-permute-start(f32[16,256]{1,0:T(8,128)S(1)} %get-tuple-element.17.st0), channel_id=1, source_target_pairs={{4,0},{5,1},{6,2},{7,3},{8,4},{9,5},{10,6},{11,7},{12,8},{13,9},{1... | collective-permute-start | bytes 49160 | tf_op jit(solution)/shard_map/ppermute | solution.py:222
  59.5 1.3 %collective-permute-start.13 = (f32[16,256]{1,0:T(8,128)S(1)}, f32[16,256]{1,0:T(8,128)S(1)}, u32[]{:S(2)}, u32[]{:S(2)}) collective-permute-start(f32[16,256]{1,0:T(8,128)S(1)} %get-tuple-element.17.st0), channel_id=1, source_target_pairs={{8,0},{9,1},{10,2},{11,3},{12,4},{13,5},{14,6},{15,7},{16,8},{17,9... | collective-permute-start | bytes 49160 | tf_op jit(solution)/shard_map/ppermute | solution.py:222
  60.8 13.3 %collective-permute-done.9.qd16 = bf16[512,512]{1,0:T(8,128)(2,1)S(1)} collective-permute-done((bf16[512,512]{1,0:T(8,128)(2,1)S(1)}, bf16[512,512]{1,0:T(8,128)(2,1)S(1)}, u32[]{:S(2)}, u32[]{:S(2)}) %collective-permute-start.9) | collective-permute-done | bytes 524320 | tf_op jit(solution)/shard_map/ppermute | solution.py:222
  74.1 1.5 %collective-permute-start.14 = (f32[16,256]{1,0:T(8,128)S(1)}, f32[16,256]{1,0:T(8,128)S(1)}, u32[]{:S(2)}, u32[]{:S(2)}) collective-permute-start(f32[16,256]{1,0:T(8,128)S(1)} %get-tuple-element.17.st0), channel_id=1, source_target_pairs={{16,0},{17,1},{18,2},{19,3},{20,4},{21,5},{22,6},{23,7},{24,8},{25... | collective-permute-start | bytes 49160 | tf_op jit(solution)/shard_map/ppermute | solution.py:222
  75.6 3.8 %query_gradient.1 = bf16[256,512]{1,0:T(8,128)(2,1)} custom-call(s32[4]{0:T(128)S(1)} %copy-done.1, s32[4,4]{1,0:T(4,128)S(1)} %copy-done, bf16[512,512]{1,0:T(8,128)(2,1)S(1)} %constant_dynamic-update-slice_fusion.qd.qd0, bf16[512,512]{1,0:T(8,128)(2,1)S(1)} %constant_dynamic-update-slice_fusion.2.kv0.kv, bf16[512,512]{1,0:T(8,128)(2,1)S(1)} %collective-permute-done.2.kv1, ...), custom_call_target="tpu_custom_call" | custom-call | flops 452984832 | bytes 4194304 | tf_op jit(solution)/shard_map/query_gradient/pallas_call | solution.py:271
  80.3 5.8 %collective-permute-done.14.st16 = f32[16,256]{1,0:T(8,128)S(1)} collective-permute-done((f32[16,256]{1,0:T(8,128)S(1)}, f32[16,256]{1,0:T(8,128)S(1)}, u32[]{:S(2)}, u32[]{:S(2)}) %collective-permute-start.14) | collective-permute-done | bytes 16416 | tf_op jit(solution)/shard_map/ppermute | solution.py:222
  86.1 5.9 %key_side.1 = (bf16[256,512]{1,0:T(8,128)(2,1)}, bf16[256,512]{1,0:T(8,128)(2,1)}) custom-call(s32[4]{0:T(128)S(1)} %copy-done.1, bf16[512,512]{1,0:T(8,128)(2,1)S(1)} %constant_dynamic-update-slice_fusion.2.kv0.kv, bf16[512,512]{1,0:T(8,128)(2,1)S(1)} %constant_dynamic-update-slice_fusion.qd.qd0, bf16[512,512]{1,0:T(8,128)(2,1)S(1)} %collective-permute-done.7.qd1, ...), custom_call_target="tpu_custom_call" | custom-call | flops 1610612736 | bytes 6815744 | tf_op jit(solution)/shard_map/key_side/pallas_call | solution.py:274
  (28 shorter events, 4.1 us)
Async XLA Ops:
  0.6 1.0 %copy-start.2 = (bf16[256,512]{1,0:T(8,128)(2,1)S(1)}, bf16[256,512]{1,0:T(8,128)(2,1)}, u32[]{:S(2)}) copy-start(bf16[256,512]{1,0:T(8,128)(2,1)} %param.8) | copy-start | bytes 786436
  1.7 4.6 %copy-start.3 = (bf16[256,512]{1,0:T(8,128)(2,1)S(1)}, bf16[256,512]{1,0:T(8,128)(2,1)}, u32[]{:S(2)}) copy-start(bf16[256,512]{1,0:T(8,128)(2,1)} %param.6) | copy-start | bytes 786436
  1.7 4.6 %copy-start.4 = (bf16[256,512]{1,0:T(8,128)(2,1)S(1)}, bf16[256,512]{1,0:T(8,128)(2,1)}, u32[]{:S(2)}) copy-start(bf16[256,512]{1,0:T(8,128)(2,1)} %param.9) | copy-start | bytes 786436
  1.7 15.1 %collective-permute-start = (bf16[512,512]{1,0:T(8,128)(2,1)S(1)}, bf16[512,512]{1,0:T(8,128)(2,1)S(1)}, u32[]{:S(2)}, u32[]{:S(2)}) collective-permute-start(bf16[512,512]{1,0:T(8,128)(2,1)S(1)} %constant_dynamic-update-slice_fusion.2.kv0.kv), channel_id=1, source_target_pairs={{0,4},{1,5},{2,6},{3,7},{4,8},{5,9},{6,10},{7,11},{8,12},{9,13},{1... | collective-permute-start | bytes 1572872 | tf_op jit(solution)/shard_map/ppermute | solution.py:222
  6.3 16.7 %collective-permute-start.5 = (bf16[512,512]{1,0:T(8,128)(2,1)S(1)}, bf16[512,512]{1,0:T(8,128)(2,1)S(1)}, u32[]{:S(2)}, u32[]{:S(2)}) collective-permute-start(bf16[512,512]{1,0:T(8,128)(2,1)S(1)} %constant_dynamic-update-slice_fusion.qd.qd0), channel_id=1, source_target_pairs={{4,0},{5,1},{6,2},{7,3},{8,4},{9,5},{10,6},{11,7},{12,8},{13,9},{1... | collective-permute-start | bytes 1572872 | tf_op jit(solution)/shard_map/ppermute | solution.py:222
  17.7 12.1 %collective-permute-start.1 = (bf16[512,512]{1,0:T(8,128)(2,1)}, bf16[512,512]{1,0:T(8,128)(2,1)S(1)}, u32[]{:S(2)}, u32[]{:S(2)}) collective-permute-start(bf16[512,512]{1,0:T(8,128)(2,1)} %broadcast_select_fusion.1), channel_id=1, source_target_pairs={{0,2},{1,3},{2,0},{3,1},{4,6},{5,7},{6,4},{7,5},{8,10},{9,11},{10,... | collective-permute-start | bytes 1572872 | tf_op jit(solution)/shard_map/ppermute | solution.py:227
  18.9 15.6 %collective-permute-start.3 = (bf16[512,512]{1,0:T(8,128)(2,1)S(1)}, bf16[512,512]{1,0:T(8,128)(2,1)S(1)}, u32[]{:S(2)}, u32[]{:S(2)}) collective-permute-start(bf16[512,512]{1,0:T(8,128)(2,1)S(1)} %collective-permute-done.kv4), channel_id=1, source_target_pairs={{0,4},{1,5},{2,6},{3,7},{4,8},{5,9},{6,10},{7,11},{8,12},{9,13},{1... | collective-permute-start | bytes 1572872 | tf_op jit(solution)/shard_map/ppermute | solution.py:222
  23.9 17.2 %collective-permute-start.6 = (bf16[512,512]{1,0:T(8,128)(2,1)}, bf16[512,512]{1,0:T(8,128)(2,1)}, u32[]{:S(2)}, u32[]{:S(2)}) collective-permute-start(bf16[512,512]{1,0:T(8,128)(2,1)} %broadcast_select_fusion), channel_id=1, source_target_pairs={{0,2},{1,3},{2,0},{3,1},{4,6},{5,7},{6,4},{7,5},{8,10},{9,11},{10,... | collective-permute-start | bytes 1572872 | tf_op jit(solution)/shard_map/ppermute | solution.py:227
  24.1 20.6 %collective-permute-start.8 = (bf16[512,512]{1,0:T(8,128)(2,1)S(1)}, bf16[512,512]{1,0:T(8,128)(2,1)S(1)}, u32[]{:S(2)}, u32[]{:S(2)}) collective-permute-start(bf16[512,512]{1,0:T(8,128)(2,1)S(1)} %collective-permute-done.5.qd4), channel_id=1, source_target_pairs={{4,0},{5,1},{6,2},{7,3},{8,4},{9,5},{10,6},{11,7},{12,8},{13,9},{1... | collective-permute-start | bytes 1572872 | tf_op jit(solution)/shard_map/ppermute | solution.py:222
  29.8 16.2 %copy-start = (s32[4,4]{1,0:T(4,128)S(1)}, s32[4,4]{1,0:T(4,128)}, u32[]{:S(2)}) copy-start(s32[4,4]{1,0:T(4,128)} %off.5) | copy-start | bytes 196
  29.8 16.2 %copy-start.1 = (s32[4]{0:T(128)S(1)}, s32[4]{0:T(128)}, u32[]{:S(2)}) copy-start(s32[4]{0:T(128)} %win.7) | copy-start | bytes 52
  29.8 18.3 %collective-permute-start.2 = (bf16[512,512]{1,0:T(8,128)(2,1)S(1)}, bf16[512,512]{1,0:T(8,128)(2,1)S(1)}, u32[]{:S(2)}, u32[]{:S(2)}) collective-permute-start(bf16[512,512]{1,0:T(8,128)(2,1)S(1)} %broadcast_select_fusion.3), channel_id=1, source_target_pairs={{0,1},{1,0},{2,3},{3,2},{4,5},{5,4},{6,7},{7,6},{8,9},{9,8},{10,11... | collective-permute-start | bytes 1572872 | tf_op jit(solution)/shard_map/ppermute | solution.py:227
  34.5 16.0 %collective-permute-start.4 = (bf16[512,512]{1,0:T(8,128)(2,1)S(1)}, bf16[512,512]{1,0:T(8,128)(2,1)S(1)}, u32[]{:S(2)}, u32[]{:S(2)}) collective-permute-start(bf16[512,512]{1,0:T(8,128)(2,1)S(1)} %collective-permute-done.3.kv8), channel_id=1, source_target_pairs={{0,8},{1,9},{2,10},{3,11},{4,12},{5,13},{6,14},{7,15},{8,16},{9,17... | collective-permute-start | bytes 1572872 | tf_op jit(solution)/shard_map/ppermute | solution.py:222
  41.1 18.3 %collective-permute-start.7 = (bf16[512,512]{1,0:T(8,128)(2,1)S(1)}, bf16[512,512]{1,0:T(8,128)(2,1)S(1)}, u32[]{:S(2)}, u32[]{:S(2)}) collective-permute-start(bf16[512,512]{1,0:T(8,128)(2,1)S(1)} %broadcast_select_fusion.2), channel_id=1, source_target_pairs={{0,1},{1,0},{2,3},{3,2},{4,5},{5,4},{6,7},{7,6},{8,9},{9,8},{10,11... | collective-permute-start | bytes 1572872 | tf_op jit(solution)/shard_map/ppermute | solution.py:227
  44.7 29.4 %collective-permute-start.9 = (bf16[512,512]{1,0:T(8,128)(2,1)S(1)}, bf16[512,512]{1,0:T(8,128)(2,1)S(1)}, u32[]{:S(2)}, u32[]{:S(2)}) collective-permute-start(bf16[512,512]{1,0:T(8,128)(2,1)S(1)} %collective-permute-done.8.qd8), channel_id=1, source_target_pairs={{8,0},{9,1},{10,2},{11,3},{12,4},{13,5},{14,6},{15,7},{16,8},{17,9... | collective-permute-start | bytes 1572872 | tf_op jit(solution)/shard_map/ppermute | solution.py:222
  53.4 26.0 %collective-permute-start.10 = (f32[16,256]{1,0:T(8,128)S(1)}, f32[16,256]{1,0:T(8,128)S(1)}, u32[]{:S(2)}, u32[]{:S(2)}) collective-permute-start(f32[16,256]{1,0:T(8,128)S(1)} %get-tuple-element.17.st0), channel_id=1, source_target_pairs={{1,0},{2,1},{3,2},{4,3},{5,4},{6,5},{7,6},{8,7},{9,8},{10,9},{11,1... | collective-permute-start | bytes 49160 | tf_op jit(solution)/shard_map/ppermute | solution.py:222
  56.9 22.5 %collective-permute-start.11 = (f32[16,256]{1,0:T(8,128)S(1)}, f32[16,256]{1,0:T(8,128)S(1)}, u32[]{:S(2)}, u32[]{:S(2)}) collective-permute-start(f32[16,256]{1,0:T(8,128)S(1)} %get-tuple-element.17.st0), channel_id=1, source_target_pairs={{2,0},{3,1},{4,2},{5,3},{6,4},{7,5},{8,6},{9,7},{10,8},{11,9},{12,... | collective-permute-start | bytes 49160 | tf_op jit(solution)/shard_map/ppermute | solution.py:222
  58.2 21.2 %collective-permute-start.12 = (f32[16,256]{1,0:T(8,128)S(1)}, f32[16,256]{1,0:T(8,128)S(1)}, u32[]{:S(2)}, u32[]{:S(2)}) collective-permute-start(f32[16,256]{1,0:T(8,128)S(1)} %get-tuple-element.17.st0), channel_id=1, source_target_pairs={{4,0},{5,1},{6,2},{7,3},{8,4},{9,5},{10,6},{11,7},{12,8},{13,9},{1... | collective-permute-start | bytes 49160 | tf_op jit(solution)/shard_map/ppermute | solution.py:222
  59.5 20.8 %collective-permute-start.13 = (f32[16,256]{1,0:T(8,128)S(1)}, f32[16,256]{1,0:T(8,128)S(1)}, u32[]{:S(2)}, u32[]{:S(2)}) collective-permute-start(f32[16,256]{1,0:T(8,128)S(1)} %get-tuple-element.17.st0), channel_id=1, source_target_pairs={{8,0},{9,1},{10,2},{11,3},{12,4},{13,5},{14,6},{15,7},{16,8},{17,9... | collective-permute-start | bytes 49160 | tf_op jit(solution)/shard_map/ppermute | solution.py:222
  74.1 12.0 %collective-permute-start.14 = (f32[16,256]{1,0:T(8,128)S(1)}, f32[16,256]{1,0:T(8,128)S(1)}, u32[]{:S(2)}, u32[]{:S(2)}) collective-permute-start(f32[16,256]{1,0:T(8,128)S(1)} %get-tuple-element.17.st0), channel_id=1, source_target_pairs={{16,0},{17,1},{18,2},{19,3},{20,4},{21,5},{22,6},{23,7},{24,8},{25... | collective-permute-start | bytes 49160 | tf_op jit(solution)/shard_map/ppermute | solution.py:222

commit v3 on v2

v3 whole, which is shorter than its diff:
```python
import jax
import jax.numpy as jnp
from jax import lax
from jax.experimental import pallas as pl
from jax.experimental.pallas import tpu as pltpu
from jax.sharding import PartitionSpec as P

HEADS = 4
HEAD_DIM = 128
FEAT = HEADS * HEAD_DIM
ROWS = 256
BLOCK = 64
BLOCKS = ROWS // BLOCK
LEVELS = 4
SCALE = HEAD_DIM**-0.5
MASKED = -1e30
STAT_ROWS = 16
WINDOW = ROWS + BLOCK
FIRST = WINDOW + (LEVELS - 1) * BLOCK
HALF = ROWS // 2
WIDE = ROWS + HALF
F32 = jnp.float32
BF16 = jnp.bfloat16


def rows_by_rows(a, b):
    return lax.dot_general(a, b, (((1,), (1,)), ((), ())), preferred_element_type=F32)


def rows_by_columns(a, b):
    return lax.dot_general(a, b, (((1,), (0,)), ((), ())), preferred_element_type=F32)


def picks_of(off, p):
    rows = []
    for j in range(LEVELS):
        picked = jnp.clip(BLOCKS * 2 ** (j + 1) + p - off[p, j], 0, BLOCKS - 1)
        rows.append(pl.multiple_of(picked * BLOCK, BLOCK))
    return rows


def across(column, width):
    return jnp.broadcast_to(column, (column.shape[0], width))


def widened(rows, width):
    return jnp.concatenate([rows] * (-(-width // 128)), 1)[:, :width]


def head_columns(h):
    return slice(HEAD_DIM * h, HEAD_DIM * (h + 1))


def with_ones(v):
    return jnp.concatenate([v, jnp.ones((v.shape[0], HEAD_DIM), BF16)], 1)


def first_keys(p, head, base, own, before, levels, picks):
    parts = [before[base + BLOCK * p : base + ROWS, head], own[base : base + BLOCK * (p + 1), head]]
    for j, ref in enumerate(levels):
        parts.append(ref[pl.ds(base + picks[j], BLOCK), head])
    return jnp.concatenate(parts, 0)


def first_bias(p, rank, length):
    row = lax.broadcasted_iota(jnp.int32, (BLOCK, FIRST), 0)
    col = lax.broadcasted_iota(jnp.int32, (BLOCK, FIRST), 1)
    gap = col - row
    need = jnp.where(col + BLOCK * p < ROWS, 1, 0)
    for j in range(LEVELS - 1):
        need = jnp.where(col >= WINDOW + BLOCK * j, 2 ** (j + 1), need)
    near = (gap <= ROWS) & (gap > ROWS - length)
    return jnp.where((near | (col >= WINDOW)) & (rank >= need), F32(0), F32(MASKED))


def query_first(win, off, qd, kv0, kv1, kv2, kv4, kv8, scores_out, dprob_out, acc, top_out, total_out):
    rank = lax.axis_index("ctx")
    levels = (kv2, kv4, kv8)
    heads = range(HEADS)
    for p in range(BLOCKS):
        picks = picks_of(off, p)
        mine = slice(BLOCK * p, BLOCK * (p + 1))
        theirs = slice(ROWS + BLOCK * p, ROWS + BLOCK * (p + 1))
        k = [first_keys(p, head_columns(h), 0, kv0, kv1, levels, picks) for h in heads]
        v = [first_keys(p, head_columns(h), ROWS, kv0, kv1, levels, picks) for h in heads]
        scores = [rows_by_rows(qd[mine, head_columns(h)], k[h]) for h in heads]
        scores = [scores[h] * SCALE + first_bias(p, rank, win[h]) for h in heads]
        top = [across(jnp.max(s, 1, keepdims=True), HEAD_DIM) for s in scores]
        for h in heads:
            scores_out[h, mine, :] = scores[h]
            dprob_out[h, mine, :] = rows_by_rows(qd[theirs, head_columns(h)], v[h])
        weights = [jnp.exp(scores[h] - widened(top[h], FIRST)).astype(BF16) for h in heads]
        sums = [rows_by_columns(weights[h], with_ones(v[h])) for h in heads]
        for h in heads:
            acc[mine, head_columns(h)] = sums[h][:, :HEAD_DIM]
            total_out[mine, head_columns(h)] = sums[h][:, HEAD_DIM:]
            top_out[mine, head_columns(h)] = top[h]


def query_last(off, qd, kv16, acc, top0, total0, _, att, stats, lse_out, delta_out, tall):
    rank = lax.axis_index("ctx")
    heads = range(HEADS)
    lane = lax.broadcasted_iota(jnp.int32, (BLOCK, 128), 1)
    bias = jnp.where(rank >= 2**LEVELS, F32(0), F32(MASKED))
    tiles = [(p, h) for p in range(BLOCKS) for h in heads]
    picks = [picks_of(off, p)[LEVELS - 1] for p in range(BLOCKS)]
    rows = lambda p, base=0: slice(base + BLOCK * p, base + BLOCK * (p + 1))
    at = lambda ref, p, h: ref[rows(p), head_columns(h)]
    scores = [
        rows_by_rows(at(qd, p, h), kv16[pl.ds(picks[p], BLOCK), head_columns(h)]) * SCALE + bias for p, h in tiles
    ]
    before = [at(top0, p, h) for p, h in tiles]
    top = [jnp.maximum(b, across(jnp.max(s, 1, keepdims=True), HEAD_DIM)) for b, s in zip(before, scores)]
    weights = [jnp.exp(s - t[:, :BLOCK]).astype(BF16) for s, t in zip(scores, top)]
    sums = [
        rows_by_columns(w, with_ones(kv16[pl.ds(ROWS + picks[p], BLOCK), head_columns(h)]))
        for w, (p, h) in zip(weights, tiles)
    ]
    fade = [jnp.exp(b - t) for b, t in zip(before, top)]
    total = [at(total0, p, h) * f + x[:, HEAD_DIM:] for f, x, (p, h) in zip(fade, sums, tiles)]
    out = [at(acc, p, h) * f + x[:, :HEAD_DIM] for f, x, (p, h) in zip(fade, sums, tiles)]
    out = [(o * (1.0 / t)).astype(BF16) for o, t in zip(out, total)]
    lse = [t + jnp.log(x) for t, x in zip(top, total)]
    delta = [
        across(jnp.sum(qd[rows(p, ROWS), head_columns(h)].astype(F32) * o.astype(F32), 1, keepdims=True), HEAD_DIM)
        for o, (p, h) in zip(out, tiles)
    ]
    for p in range(BLOCKS):
        kept = jnp.zeros((BLOCK, 128), F32)
        for h in heads:
            i = p * HEADS + h
            att[rows(p), head_columns(h)] = out[i]
            lse_out[rows(p), head_columns(h)] = lse[i]
            delta_out[rows(p), head_columns(h)] = delta[i]
            kept = jnp.where(lane == h, lse[i], kept)
            kept = jnp.where(lane == HEADS + h, delta[i], kept)
        tall[rows(p), :] = kept
    stats[0 : 2 * HEADS, :] = tall[...].T[0 : 2 * HEADS]
    wide_row = lax.broadcasted_iota(jnp.int32, (STAT_ROWS - 2 * HEADS, ROWS), 0)
    wide_block = lax.broadcasted_iota(jnp.int32, (STAT_ROWS - 2 * HEADS, ROWS), 1) // BLOCK
    chosen = jnp.zeros((STAT_ROWS - 2 * HEADS, ROWS), F32)
    for p in range(BLOCKS):
        for j in range(LEVELS):
            picked = jnp.clip(BLOCKS * 2 ** (j + 1) + p - off[p, j], 0, BLOCKS - 1)
            chosen = jnp.where((wide_row == j) & (wide_block == p), picked.astype(F32), chosen)
    stats[2 * HEADS :, :] = chosen


def query_gradient(off, qd, kv0, kv1, kv2, kv4, kv8, kv16, scores, dprob, lse, delta, dq):
    rank = lax.axis_index("ctx")
    levels = (kv2, kv4, kv8)
    heads = range(HEADS)
    bias = jnp.where(rank >= 2**LEVELS, F32(0), F32(MASKED))
    for p in range(BLOCKS):
        picks = picks_of(off, p)
        mine = slice(BLOCK * p, BLOCK * (p + 1))
        theirs = slice(ROWS + BLOCK * p, ROWS + BLOCK * (p + 1))
        k = [first_keys(p, head_columns(h), 0, kv0, kv1, levels, picks) for h in heads]
        last_k = [kv16[pl.ds(picks[-1], BLOCK), head_columns(h)] for h in heads]
        last_v = [kv16[pl.ds(ROWS + picks[-1], BLOCK), head_columns(h)] for h in heads]
        last = [rows_by_rows(qd[mine, head_columns(h)], last_k[h]) * SCALE + bias for h in heads]
        last_dprob = [rows_by_rows(qd[theirs, head_columns(h)], last_v[h]) for h in heads]
        my_lse = [lse[mine, head_columns(h)] for h in heads]
        my_delta = [delta[mine, head_columns(h)] for h in heads]
        first = [
            jnp.exp(scores[h, mine, :] - widened(my_lse[h], FIRST)) * (dprob[h, mine, :] - widened(my_delta[h], FIRST))
            for h in heads
        ]
        last = [jnp.exp(last[h] - my_lse[h][:, :BLOCK]) * (last_dprob[h] - my_delta[h][:, :BLOCK]) for h in heads]
        for h in heads:
            total = rows_by_columns(first[h].astype(BF16), k[h]) + rows_by_columns(last[h].astype(BF16), last_k[h])
            dq[mine, head_columns(h)] = (total * SCALE).astype(BF16)


def joined(a, b, base, cut, head):
    return jnp.concatenate([a[base + cut : base + ROWS, head], b[base : base + cut + HALF, head]], 0)


def key_first(kv, qd2, qd4, qd8, scores, dprob):
    for h in range(HEADS):
        head = head_columns(h)
        for j, qd in enumerate((qd2, qd4, qd8)):
            columns = slice(ROWS * j, ROWS * (j + 1))
            scores[h, :, columns] = rows_by_rows(kv[0:ROWS, head], qd[0:ROWS, head]) * SCALE
            dprob[h, :, columns] = rows_by_rows(kv[ROWS : 2 * ROWS, head], qd[ROWS : 2 * ROWS, head])


def key_last(
    win, kv, qd0, qd1, qd2, qd4, qd8, qd16, far_scores, far_dprob, st16, st8, st4, st2, st1, st0, dk, dv
):
    key_block = (lax.broadcasted_iota(jnp.int32, (ROWS, ROWS), 0) // BLOCK).astype(F32)
    far = ((qd2, st2), (qd4, st4), (qd8, st8), (qd16, st16))
    row = lax.broadcasted_iota(jnp.int32, (HALF, WIDE), 0)
    col = lax.broadcasted_iota(jnp.int32, (HALF, WIDE), 1)
    gap = col - row
    chosen = [key_block == st[2 * HEADS + j : 2 * HEADS + j + 1, :] for j, (_, st) in enumerate(far)]
    for h in range(HEADS):
        head = head_columns(h)
        lanes = lambda r, cut: jnp.concatenate([st0[r : r + 1, cut:ROWS], st1[r : r + 1, 0 : cut + HALF]], 1)
        bias = jnp.where((gap >= 0) & (gap < win[h]), F32(0), F32(MASKED))
        scores = [
            rows_by_rows(kv[HALF * c : HALF * (c + 1), head], joined(qd0, qd1, 0, HALF * c, head)) * SCALE + bias
            for c in range(2)
        ]
        dprob = [
            rows_by_rows(kv[ROWS + HALF * c : ROWS + HALF * (c + 1), head], joined(qd0, qd1, ROWS, HALF * c, head))
            for c in range(2)
        ]
        scores += [far_scores[h, :, ROWS * j : ROWS * (j + 1)] for j in range(LEVELS - 1)]
        dprob += [far_dprob[h, :, ROWS * j : ROWS * (j + 1)] for j in range(LEVELS - 1)]
        scores.append(rows_by_rows(kv[0:ROWS, head], qd16[0:ROWS, head]) * SCALE)
        dprob.append(rows_by_rows(kv[ROWS : 2 * ROWS, head], qd16[ROWS : 2 * ROWS, head]))
        lse = [lanes(h, HALF * c) for c in range(2)] + [st[h : h + 1, :] for _, st in far]
        delta = [lanes(HEADS + h, HALF * c) for c in range(2)]
        delta += [st[HEADS + h : HEADS + h + 1, :] for _, st in far]
        probs = [jnp.exp(scores[i] - lse[i]) for i in range(2)]
        probs += [jnp.exp(jnp.where(chosen[j], scores[2 + j] - lse[2 + j], F32(MASKED))) for j in range(LEVELS)]
        dscore = [(probs[i] * (dprob[i] - delta[i])).astype(BF16) for i in range(2 + LEVELS)]
        probs = [x.astype(BF16) for x in probs]
        for rows, base, out, scale in ((dscore, 0, dk, SCALE), (probs, ROWS, dv, 1.0)):
            near = [rows_by_columns(rows[c], joined(qd0, qd1, base, HALF * c, head)) for c in range(2)]
            stack = jnp.concatenate([qd[base : base + ROWS, head] for qd, _ in far], 0)
            total = jnp.concatenate(near, 0) + rows_by_columns(jnp.concatenate(rows[2:], 1), stack)
            out[:, head] = (total * scale).astype(BF16)


def moved(array, by):
    size = lax.axis_size("ctx")
    return lax.ppermute(array, "ctx", [(i, i + by) for i in range(size) if 0 <= i + by < size])


def swapped(array, bit):
    size = lax.axis_size("ctx")
    return lax.ppermute(array, "ctx", [(i, i ^ bit) for i in range(size)])


def kernel(body, out_shape, n_smem, n_vmem, flops, scratch=(), n_any=0):
    smem = pl.BlockSpec(memory_space=pltpu.SMEM)
    vmem = pl.BlockSpec(memory_space=pltpu.VMEM)
    return pl.pallas_call(
        body,
        out_shape=tuple(out_shape),
        in_specs=[smem] * n_smem + [vmem] * n_vmem + [pl.BlockSpec(memory_space=pl.ANY)] * n_any,
        out_specs=(vmem,) * len(out_shape),
        scratch_shapes=list(scratch),
        compiler_params=pltpu.CompilerParams(vmem_limit_bytes=32 * 2**20),
        cost_estimate=pl.CostEstimate(flops=flops, bytes_accessed=n_vmem * ROWS * FEAT * 4, transcendentals=0),
        name=body.__name__,
    )


def on_device(queries, keys, values, grad_out, window, offsets):
    rank = lax.axis_index("ctx")
    kv0 = jnp.concatenate([keys, values], 0)
    qd0 = jnp.concatenate([queries, grad_out], 0)
    kv4 = moved(kv0, 4)
    qd4 = moved(qd0, -4)
    kv2 = swapped(jnp.where(rank % 4 < 2, kv0, kv4), 2)
    qd2 = swapped(jnp.where(rank % 4 < 2, qd4, qd0), 2)
    kv1 = swapped(jnp.where(rank % 2 == 0, kv0, kv2), 1)
    qd1 = swapped(jnp.where(rank % 2 == 0, qd2, qd0), 1)
    kv8 = moved(kv4, 4)
    qd8 = moved(qd4, -4)
    kv16 = moved(kv8, 8)
    qd16 = moved(qd8, -8)
    half = jax.ShapeDtypeStruct((ROWS, FEAT), BF16)
    f32 = lambda *shape: jax.ShapeDtypeStruct(shape, F32)
    unit = 2 * ROWS * FEAT
    scores, dprob, *sums = kernel(
        query_first, (f32(HEADS, ROWS, FIRST), f32(HEADS, ROWS, FIRST)) + (f32(ROWS, FEAT),) * 3, 2, 6, unit * 3 * FIRST
    )(window, offsets, qd0, kv0, kv1, kv2, kv4, kv8)
    pre = kernel(key_first, (f32(HEADS, ROWS, 3 * ROWS),) * 2, 0, 4, unit * 2 * 3 * ROWS)(kv0, qd2, qd4, qd8)
    attended, stats, lse, delta = kernel(
        query_last,
        (half, f32(STAT_ROWS, ROWS), f32(ROWS, FEAT), f32(ROWS, FEAT)),
        1,
        5,
        unit * 2 * BLOCK,
        (pltpu.VMEM((ROWS, 128), F32),),
        n_any=1,
    )(offsets, qd0, kv16, *sums, pre[1])
    received = [moved(stats, -by) for by in (1, 2, 4, 8, 16)]
    (grad_q,) = kernel(query_gradient, (half,), 1, 11, unit * FIRST)(
        offsets, qd0, kv0, kv1, kv2, kv4, kv8, kv16, scores, dprob, lse, delta
    )
    grad_k, grad_v = kernel(key_last, (half, half), 1, 15, unit * 2 * 6 * ROWS)(
        window, kv0, qd0, qd1, qd2, qd4, qd8, qd16, *pre, *received[::-1], stats
    )
    return attended, grad_q, grad_k, grad_v


def solution(mesh):
    split = P(("dp", "ctx"), None)
    return jax.shard_map(
        on_device,
        mesh=mesh,
        in_specs=(split, split, split, split, P(), split),
        out_specs=(split,) * 4,
        check_vma=False,
    )
```

time: 92.6 us -> 88.5 us (0.956)
  the two profiles are of different devices: /device:TPU:1 before, /device:TPU:249 now
where the time goes in v3:
time: 88.5 us; the launch traced here: 87.9 us
  starting transfers between devices  41.2 us (47%)
  waiting for transfers between devices  26.3 us (30%)
  Pallas kernels  13.8 us (16%)
  local copies, waits for them, and re-layouts  3.89 us (4%)
  other arithmetic  1.84 us (2%)
    ppermute x11, starting transfers between devices, moved(): lax.ppermute(array, 'ctx', [(i, i + by) for i in range(size) if 0 <= i +...  32.3 us
    ppermute x11, waiting for transfers between devices, moved(): lax.ppermute(array, 'ctx', [(i, i + by) for i in range(size) if 0 <= i +...  17 us
    ppermute x4, waiting for transfers between devices, swapped(): return lax.ppermute(array, 'ctx', [(i, i ^ bit) for i in range(size)])  9.28 us
    ppermute x4, starting transfers between devices, swapped(): return lax.ppermute(array, 'ctx', [(i, i ^ bit) for i in range(size)])  8.94 us
    pallas_call x1, Pallas kernels, on_device(): kernel(key_last, (half, half), 1, 15, unit * 2 * 6 * ROWS)  4.67 us
    pallas_call x1, Pallas kernels, on_device(): kernel(query_first, (f32(HEADS, ROWS, FIRST), f32(HEADS, ROWS, FIRST)) +...  3.15 us
    pallas_call x1, Pallas kernels, on_device(): kernel(query_gradient, (half,), 1, 11, unit * FIRST)  3.08 us
    pallas_call x1, Pallas kernels, on_device(): kernel(query_last, (half, f32(STAT_ROWS, ROWS), f32(ROWS, FEAT), f32(ROWS...  1.96 us
  transfers between devices with their start and end apart: 15, of which 4 were waited for; matrix products, arithmetic and copies ran while one was open for 4% of the time, Pallas kernels for 10%

profile of v3, /device:TPU:249, one launch (start us, length us, event | category | flops | bytes accessed | tf_op | source)
XLA Modules:
  0.0 87.9 jit_solution(7910945713625650534)
XLA Ops:
  1.6 1.0 %constant_dynamic-update-slice_fusion.2.kv0.kv = bf16[512,512]{1,0:T(8,128)(2,1)S(1)} fusion(bf16[512,512]{1,0:T(8,128)(2,1)S(1)} %constant_dynamic-update-slice_fusion.3, bf16[256,512]{1,0:T(8,128)(2,1)} %param.8), kind=kLoop, calls=%fused_computation.6 | loop fusion | bytes 524288 | tf_op jit(solution)/shard_map/concatenate | solution.py:254
  2.6 1.3 %collective-permute-start = (bf16[512,512]{1,0:T(8,128)(2,1)S(1)}, bf16[512,512]{1,0:T(8,128)(2,1)S(1)}, u32[]{:S(2)}, u32[]{:S(2)}) collective-permute-start(bf16[512,512]{1,0:T(8,128)(2,1)S(1)} %constant_dynamic-update-slice_fusion.2.kv0.kv), channel_id=1, source_target_pairs={{0,4},{1,5},{2,6},{3,7},{4,8},{5,9},{6,10},{7,11},{8,12},{9,13},{1... | collective-permute-start | bytes 1572872 | tf_op jit(solution)/shard_map/ppermute | solution.py:229
  5.8 4.0 %collective-permute-start.5 = (bf16[512,512]{1,0:T(8,128)(2,1)S(1)}, bf16[512,512]{1,0:T(8,128)(2,1)S(1)}, u32[]{:S(2)}, u32[]{:S(2)}) collective-permute-start(bf16[512,512]{1,0:T(8,128)(2,1)S(1)} %constant_dynamic-update-slice_fusion.qd.qd0), channel_id=1, source_target_pairs={{4,0},{5,1},{6,2},{7,3},{8,4},{9,5},{10,6},{11,7},{12,8},{13,9},{1... | collective-permute-start | bytes 1572872 | tf_op jit(solution)/shard_map/ppermute | solution.py:229
  9.9 7.4 %collective-permute-done.kv4 = bf16[512,512]{1,0:T(8,128)(2,1)S(1)} collective-permute-done((bf16[512,512]{1,0:T(8,128)(2,1)S(1)}, bf16[512,512]{1,0:T(8,128)(2,1)S(1)}, u32[]{:S(2)}, u32[]{:S(2)}) %collective-permute-start) | collective-permute-done | bytes 524320 | tf_op jit(solution)/shard_map/ppermute | solution.py:229
  18.1 1.2 %collective-permute-start.3 = (bf16[512,512]{1,0:T(8,128)(2,1)}, bf16[512,512]{1,0:T(8,128)(2,1)S(1)}, u32[]{:S(2)}, u32[]{:S(2)}) collective-permute-start(bf16[512,512]{1,0:T(8,128)(2,1)} %broadcast_select_fusion.1), channel_id=1, source_target_pairs={{0,2},{1,3},{2,0},{3,1},{4,6},{5,7},{6,4},{7,5},{8,10},{9,11},{10,... | collective-permute-start | bytes 1572872 | tf_op jit(solution)/shard_map/ppermute | solution.py:234
  19.3 1.3 %collective-permute-start.1 = (bf16[512,512]{1,0:T(8,128)(2,1)S(1)}, bf16[512,512]{1,0:T(8,128)(2,1)}, u32[]{:S(2)}, u32[]{:S(2)}) collective-permute-start(bf16[512,512]{1,0:T(8,128)(2,1)S(1)} %collective-permute-done.kv4), channel_id=1, source_target_pairs={{0,4},{1,5},{2,6},{3,7},{4,8},{5,9},{6,10},{7,11},{8,12},{9,13},{1... | collective-permute-start | bytes 1572872 | tf_op jit(solution)/shard_map/ppermute | solution.py:229
  22.2 4.1 %collective-permute-start.7 = (bf16[512,512]{1,0:T(8,128)(2,1)S(1)}, bf16[512,512]{1,0:T(8,128)(2,1)S(1)}, u32[]{:S(2)}, u32[]{:S(2)}) collective-permute-start(bf16[512,512]{1,0:T(8,128)(2,1)S(1)} %collective-permute-done.5.qd4), channel_id=1, source_target_pairs={{4,0},{5,1},{6,2},{7,3},{8,4},{9,5},{10,6},{11,7},{12,8},{13,9},{1... | collective-permute-start | bytes 1572872 | tf_op jit(solution)/shard_map/ppermute | solution.py:229
  26.3 4.0 %collective-permute-done.3.kv2 = bf16[512,512]{1,0:T(8,128)(2,1)S(1)} collective-permute-done((bf16[512,512]{1,0:T(8,128)(2,1)}, bf16[512,512]{1,0:T(8,128)(2,1)S(1)}, u32[]{:S(2)}, u32[]{:S(2)}) %collective-permute-start.3) | collective-permute-done | bytes 524320 | tf_op jit(solution)/shard_map/ppermute | solution.py:234
  30.4 4.5 %collective-permute-start.4 = (bf16[512,512]{1,0:T(8,128)(2,1)S(1)}, bf16[512,512]{1,0:T(8,128)(2,1)S(1)}, u32[]{:S(2)}, u32[]{:S(2)}) collective-permute-start(bf16[512,512]{1,0:T(8,128)(2,1)S(1)} %broadcast_select_fusion.3), channel_id=1, source_target_pairs={{0,1},{1,0},{2,3},{3,2},{4,5},{5,4},{6,7},{7,6},{8,9},{9,8},{10,11... | collective-permute-start | bytes 1572872 | tf_op jit(solution)/shard_map/ppermute | solution.py:234
  34.9 1.3 %collective-permute-start.2 = (bf16[512,512]{1,0:T(8,128)(2,1)}, bf16[512,512]{1,0:T(8,128)(2,1)S(1)}, u32[]{:S(2)}, u32[]{:S(2)}) collective-permute-start(bf16[512,512]{1,0:T(8,128)(2,1)} %collective-permute-done.1.kv8), channel_id=1, source_target_pairs={{0,8},{1,9},{2,10},{3,11},{4,12},{5,13},{6,14},{7,15},{8,16},{9,17... | collective-permute-start | bytes 1572872 | tf_op jit(solution)/shard_map/ppermute | solution.py:229
  36.2 5.3 %collective-permute-done.6.qd2 = bf16[512,512]{1,0:T(8,128)(2,1)S(1)} collective-permute-done((bf16[512,512]{1,0:T(8,128)(2,1)}, bf16[512,512]{1,0:T(8,128)(2,1)S(1)}, u32[]{:S(2)}, u32[]{:S(2)}) %collective-permute-start.6) | collective-permute-done | bytes 524320 | tf_op jit(solution)/shard_map/ppermute | solution.py:234
  41.5 2.6 %collective-permute-start.8 = (bf16[512,512]{1,0:T(8,128)(2,1)S(1)}, bf16[512,512]{1,0:T(8,128)(2,1)S(1)}, u32[]{:S(2)}, u32[]{:S(2)}) collective-permute-start(bf16[512,512]{1,0:T(8,128)(2,1)S(1)} %broadcast_select_fusion.2), channel_id=1, source_target_pairs={{0,1},{1,0},{2,3},{3,2},{4,5},{5,4},{6,7},{7,6},{8,9},{9,8},{10,11... | collective-permute-start | bytes 1572872 | tf_op jit(solution)/shard_map/ppermute | solution.py:234
  44.1 3.1 %collective-permute-start.9 = (bf16[512,512]{1,0:T(8,128)(2,1)S(1)}, bf16[512,512]{1,0:T(8,128)(2,1)S(1)}, u32[]{:S(2)}, u32[]{:S(2)}) collective-permute-start(bf16[512,512]{1,0:T(8,128)(2,1)S(1)} %collective-permute-done.7.qd8), channel_id=1, source_target_pairs={{8,0},{9,1},{10,2},{11,3},{12,4},{13,5},{14,6},{15,7},{16,8},{17,9... | collective-permute-start | bytes 1572872 | tf_op jit(solution)/shard_map/ppermute | solution.py:229
  47.2 1.0 %key_first.1 = (f32[4,256,768]{2,1,0:T(8,128)S(1)}, f32[4,256,768]{2,1,0:T(8,128)S(1)}) custom-call(bf16[512,512]{1,0:T(8,128)(2,1)S(1)} %constant_dynamic-update-slice_fusion.2.kv0.kv, bf16[512,512]{1,0:T(8,128)(2,1)S(1)} %collective-permute-done.6.qd2, bf16[512,512]{1,0:T(8,128)(2,1)S(1)} %collective-permute-done.5.qd4, ...), custom_call_target="tpu_custom_call" | custom-call | flops 402653184 | bytes 2097152 | tf_op jit(solution)/shard_map/key_first/pallas_call | solution.py:272
  48.2 3.1 %query_first.1 = (f32[4,256,512]{2,1,0:T(8,128)S(1)}, f32[4,256,512]{2,1,0:T(8,128)S(1)}, f32[256,512]{1,0:T(8,128)S(1)}, f32[256,512]{1,0:T(8,128)S(1)}, f32[256,512]{1,0:T(8,128)S(1)}) custom-call(s32[4]{0:T(128)S(1)} %copy-done.1, s32[4,4]{1,0:T(4,128)S(1)} %copy-done, bf16[512,512]{1,0:T(8,128)(2,1)S(1)} %constant_dynamic-update-slice_fusion.qd.qd0, ...), custom_call_target="tpu_custom_call" | custom-call | flops 402653184 | bytes 3145728 | tf_op jit(solution)/shard_map/query_first/pallas_call | solution.py:269
  51.3 9.6 %collective-permute-done.2.kv16 = bf16[512,512]{1,0:T(8,128)(2,1)S(1)} collective-permute-done((bf16[512,512]{1,0:T(8,128)(2,1)}, bf16[512,512]{1,0:T(8,128)(2,1)S(1)}, u32[]{:S(2)}, u32[]{:S(2)}) %collective-permute-start.2) | collective-permute-done | bytes 524320 | tf_op jit(solution)/shard_map/ppermute | solution.py:229
  60.9 2.0 %query_last.1 = (bf16[256,512]{1,0:T(8,128)(2,1)}, f32[16,256]{1,0:T(8,128)S(1)}, f32[256,512]{1,0:T(8,128)S(1)}, f32[256,512]{1,0:T(8,128)S(1)}) custom-call(s32[4,4]{1,0:T(4,128)S(1)} %copy-done, bf16[512,512]{1,0:T(8,128)(2,1)S(1)} %constant_dynamic-update-slice_fusion.qd.qd0, bf16[512,512]{1,0:T(8,128)(2,1)S(1)} %collective-permute-done.2.kv16, ...), custom_call_target="tpu_custom_call" | custom-call | flops 33554432 | bytes 2621440 | tf_op jit(solution)/shard_map/query_last/pallas_call | solution.py:273
  62.9 4.7 %collective-permute-start.10 = (f32[16,256]{1,0:T(8,128)S(1)}, f32[16,256]{1,0:T(8,128)S(1)}, u32[]{:S(2)}, u32[]{:S(2)}) collective-permute-start(f32[16,256]{1,0:T(8,128)S(1)} %get-tuple-element.27.st0), channel_id=1, source_target_pairs={{16,0},{17,1},{18,2},{19,3},{20,4},{21,5},{22,6},{23,7},{24,8},{25... | collective-permute-start | bytes 49160 | tf_op jit(solution)/shard_map/ppermute | solution.py:229
  67.6 1.3 %collective-permute-start.11 = (f32[16,256]{1,0:T(8,128)S(1)}, f32[16,256]{1,0:T(8,128)S(1)}, u32[]{:S(2)}, u32[]{:S(2)}) collective-permute-start(f32[16,256]{1,0:T(8,128)S(1)} %get-tuple-element.27.st0), channel_id=1, source_target_pairs={{8,0},{9,1},{10,2},{11,3},{12,4},{13,5},{14,6},{15,7},{16,8},{17,9... | collective-permute-start | bytes 49160 | tf_op jit(solution)/shard_map/ppermute | solution.py:229
  68.9 3.1 %collective-permute-start.12 = (f32[16,256]{1,0:T(8,128)S(1)}, f32[16,256]{1,0:T(8,128)S(1)}, u32[]{:S(2)}, u32[]{:S(2)}) collective-permute-start(f32[16,256]{1,0:T(8,128)S(1)} %get-tuple-element.27.st0), channel_id=1, source_target_pairs={{4,0},{5,1},{6,2},{7,3},{8,4},{9,5},{10,6},{11,7},{12,8},{13,9},{1... | collective-permute-start | bytes 49160 | tf_op jit(solution)/shard_map/ppermute | solution.py:229
  71.9 3.8 %collective-permute-start.13 = (f32[16,256]{1,0:T(8,128)S(1)}, f32[16,256]{1,0:T(8,128)S(1)}, u32[]{:S(2)}, u32[]{:S(2)}) collective-permute-start(f32[16,256]{1,0:T(8,128)S(1)} %get-tuple-element.27.st0), channel_id=1, source_target_pairs={{2,0},{3,1},{4,2},{5,3},{6,4},{7,5},{8,6},{9,7},{10,8},{11,9},{12,... | collective-permute-start | bytes 49160 | tf_op jit(solution)/shard_map/ppermute | solution.py:229
  75.8 4.4 %collective-permute-start.14 = (f32[16,256]{1,0:T(8,128)S(1)}, f32[16,256]{1,0:T(8,128)S(1)}, u32[]{:S(2)}, u32[]{:S(2)}) collective-permute-start(f32[16,256]{1,0:T(8,128)S(1)} %get-tuple-element.27.st0), channel_id=1, source_target_pairs={{1,0},{2,1},{3,2},{4,3},{5,4},{6,5},{7,6},{8,7},{9,8},{10,9},{11,1... | collective-permute-start | bytes 49160 | tf_op jit(solution)/shard_map/ppermute | solution.py:229
  80.1 3.1 %query_gradient.1 = bf16[256,512]{1,0:T(8,128)(2,1)} custom-call(s32[4,4]{1,0:T(4,128)S(1)} %copy-done, bf16[512,512]{1,0:T(8,128)(2,1)S(1)} %constant_dynamic-update-slice_fusion.qd.qd0, bf16[512,512]{1,0:T(8,128)(2,1)S(1)} %constant_dynamic-update-slice_fusion.2.kv0.kv, bf16[512,512]{1,0:T(8,128)(2,1)S(1)} %collective-permute-done.4.kv1, ...), custom_call_target="tpu_custom_call" | custom-call | flops 134217728 | bytes 5767168 | tf_op jit(solution)/shard_map/query_gradient/pallas_call | solution.py:283
  83.3 4.7 %key_last.1 = (bf16[256,512]{1,0:T(8,128)(2,1)}, bf16[256,512]{1,0:T(8,128)(2,1)}) custom-call(s32[4]{0:T(128)S(1)} %copy-done.1, bf16[512,512]{1,0:T(8,128)(2,1)S(1)} %constant_dynamic-update-slice_fusion.2.kv0.kv, bf16[512,512]{1,0:T(8,128)(2,1)S(1)} %constant_dynamic-update-slice_fusion.qd.qd0, bf16[512,512]{1,0:T(8,128)(2,1)S(1)} %collective-permute-done.8.qd1, ...), custom_call_target="tpu_custom_call" | custom-call | flops 805306368 | bytes 7864320 | tf_op jit(solution)/shard_map/key_last/pallas_call | solution.py:286
  (23 shorter events, 5.4 us)
Async XLA Ops:
  2.6 14.7 %collective-permute-start = (bf16[512,512]{1,0:T(8,128)(2,1)S(1)}, bf16[512,512]{1,0:T(8,128)(2,1)S(1)}, u32[]{:S(2)}, u32[]{:S(2)}) collective-permute-start(bf16[512,512]{1,0:T(8,128)(2,1)S(1)} %constant_dynamic-update-slice_fusion.2.kv0.kv), channel_id=1, source_target_pairs={{0,4},{1,5},{2,6},{3,7},{4,8},{5,9},{6,10},{7,11},{8,12},{9,13},{1... | collective-permute-start | bytes 1572872 | tf_op jit(solution)/shard_map/ppermute | solution.py:229
  5.8 14.8 %collective-permute-start.5 = (bf16[512,512]{1,0:T(8,128)(2,1)S(1)}, bf16[512,512]{1,0:T(8,128)(2,1)S(1)}, u32[]{:S(2)}, u32[]{:S(2)}) collective-permute-start(bf16[512,512]{1,0:T(8,128)(2,1)S(1)} %constant_dynamic-update-slice_fusion.qd.qd0), channel_id=1, source_target_pairs={{4,0},{5,1},{6,2},{7,3},{8,4},{9,5},{10,6},{11,7},{12,8},{13,9},{1... | collective-permute-start | bytes 1572872 | tf_op jit(solution)/shard_map/ppermute | solution.py:229
  18.1 30.0 %copy-start = (s32[4,4]{1,0:T(4,128)S(1)}, s32[4,4]{1,0:T(4,128)}, u32[]{:S(2)}) copy-start(s32[4,4]{1,0:T(4,128)} %off.5) | copy-start | bytes 196
  18.1 30.1 %copy-start.1 = (s32[4]{0:T(128)S(1)}, s32[4]{0:T(128)}, u32[]{:S(2)}) copy-start(s32[4]{0:T(128)} %win.3) | copy-start | bytes 52
  18.1 12.2 %collective-permute-start.3 = (bf16[512,512]{1,0:T(8,128)(2,1)}, bf16[512,512]{1,0:T(8,128)(2,1)S(1)}, u32[]{:S(2)}, u32[]{:S(2)}) collective-permute-start(bf16[512,512]{1,0:T(8,128)(2,1)} %broadcast_select_fusion.1), channel_id=1, source_target_pairs={{0,2},{1,3},{2,0},{3,1},{4,6},{5,7},{6,4},{7,5},{8,10},{9,11},{10,... | collective-permute-start | bytes 1572872 | tf_op jit(solution)/shard_map/ppermute | solution.py:234
  19.3 15.6 %collective-permute-start.1 = (bf16[512,512]{1,0:T(8,128)(2,1)S(1)}, bf16[512,512]{1,0:T(8,128)(2,1)}, u32[]{:S(2)}, u32[]{:S(2)}) collective-permute-start(bf16[512,512]{1,0:T(8,128)(2,1)S(1)} %collective-permute-done.kv4), channel_id=1, source_target_pairs={{0,4},{1,5},{2,6},{3,7},{4,8},{5,9},{6,10},{7,11},{8,12},{9,13},{1... | collective-permute-start | bytes 1572872 | tf_op jit(solution)/shard_map/ppermute | solution.py:229
  21.5 19.9 %collective-permute-start.6 = (bf16[512,512]{1,0:T(8,128)(2,1)}, bf16[512,512]{1,0:T(8,128)(2,1)S(1)}, u32[]{:S(2)}, u32[]{:S(2)}) collective-permute-start(bf16[512,512]{1,0:T(8,128)(2,1)} %broadcast_select_fusion), channel_id=1, source_target_pairs={{0,2},{1,3},{2,0},{3,1},{4,6},{5,7},{6,4},{7,5},{8,10},{9,11},{10,... | collective-permute-start | bytes 1572872 | tf_op jit(solution)/shard_map/ppermute | solution.py:234
  22.2 21.9 %collective-permute-start.7 = (bf16[512,512]{1,0:T(8,128)(2,1)S(1)}, bf16[512,512]{1,0:T(8,128)(2,1)S(1)}, u32[]{:S(2)}, u32[]{:S(2)}) collective-permute-start(bf16[512,512]{1,0:T(8,128)(2,1)S(1)} %collective-permute-done.5.qd4), channel_id=1, source_target_pairs={{4,0},{5,1},{6,2},{7,3},{8,4},{9,5},{10,6},{11,7},{12,8},{13,9},{1... | collective-permute-start | bytes 1572872 | tf_op jit(solution)/shard_map/ppermute | solution.py:229
  30.4 17.8 %collective-permute-start.4 = (bf16[512,512]{1,0:T(8,128)(2,1)S(1)}, bf16[512,512]{1,0:T(8,128)(2,1)S(1)}, u32[]{:S(2)}, u32[]{:S(2)}) collective-permute-start(bf16[512,512]{1,0:T(8,128)(2,1)S(1)} %broadcast_select_fusion.3), channel_id=1, source_target_pairs={{0,1},{1,0},{2,3},{3,2},{4,5},{5,4},{6,7},{7,6},{8,9},{9,8},{10,11... | collective-permute-start | bytes 1572872 | tf_op jit(solution)/shard_map/ppermute | solution.py:234
  34.9 26.0 %collective-permute-start.2 = (bf16[512,512]{1,0:T(8,128)(2,1)}, bf16[512,512]{1,0:T(8,128)(2,1)S(1)}, u32[]{:S(2)}, u32[]{:S(2)}) collective-permute-start(bf16[512,512]{1,0:T(8,128)(2,1)} %collective-permute-done.1.kv8), channel_id=1, source_target_pairs={{0,8},{1,9},{2,10},{3,11},{4,12},{5,13},{6,14},{7,15},{8,16},{9,17... | collective-permute-start | bytes 1572872 | tf_op jit(solution)/shard_map/ppermute | solution.py:229
  41.5 30.4 %collective-permute-start.8 = (bf16[512,512]{1,0:T(8,128)(2,1)S(1)}, bf16[512,512]{1,0:T(8,128)(2,1)S(1)}, u32[]{:S(2)}, u32[]{:S(2)}) collective-permute-start(bf16[512,512]{1,0:T(8,128)(2,1)S(1)} %broadcast_select_fusion.2), channel_id=1, source_target_pairs={{0,1},{1,0},{2,3},{3,2},{4,5},{5,4},{6,7},{7,6},{8,9},{9,8},{10,11... | collective-permute-start | bytes 1572872 | tf_op jit(solution)/shard_map/ppermute | solution.py:234
  44.1 31.7 %collective-permute-start.9 = (bf16[512,512]{1,0:T(8,128)(2,1)S(1)}, bf16[512,512]{1,0:T(8,128)(2,1)S(1)}, u32[]{:S(2)}, u32[]{:S(2)}) collective-permute-start(bf16[512,512]{1,0:T(8,128)(2,1)S(1)} %collective-permute-done.7.qd8), channel_id=1, source_target_pairs={{8,0},{9,1},{10,2},{11,3},{12,4},{13,5},{14,6},{15,7},{16,8},{17,9... | collective-permute-start | bytes 1572872 | tf_op jit(solution)/shard_map/ppermute | solution.py:229
  62.9 20.4 %collective-permute-start.10 = (f32[16,256]{1,0:T(8,128)S(1)}, f32[16,256]{1,0:T(8,128)S(1)}, u32[]{:S(2)}, u32[]{:S(2)}) collective-permute-start(f32[16,256]{1,0:T(8,128)S(1)} %get-tuple-element.27.st0), channel_id=1, source_target_pairs={{16,0},{17,1},{18,2},{19,3},{20,4},{21,5},{22,6},{23,7},{24,8},{25... | collective-permute-start | bytes 49160 | tf_op jit(solution)/shard_map/ppermute | solution.py:229
  67.6 15.7 %collective-permute-start.11 = (f32[16,256]{1,0:T(8,128)S(1)}, f32[16,256]{1,0:T(8,128)S(1)}, u32[]{:S(2)}, u32[]{:S(2)}) collective-permute-start(f32[16,256]{1,0:T(8,128)S(1)} %get-tuple-element.27.st0), channel_id=1, source_target_pairs={{8,0},{9,1},{10,2},{11,3},{12,4},{13,5},{14,6},{15,7},{16,8},{17,9... | collective-permute-start | bytes 49160 | tf_op jit(solution)/shard_map/ppermute | solution.py:229
  68.9 14.4 %collective-permute-start.12 = (f32[16,256]{1,0:T(8,128)S(1)}, f32[16,256]{1,0:T(8,128)S(1)}, u32[]{:S(2)}, u32[]{:S(2)}) collective-permute-start(f32[16,256]{1,0:T(8,128)S(1)} %get-tuple-element.27.st0), channel_id=1, source_target_pairs={{4,0},{5,1},{6,2},{7,3},{8,4},{9,5},{10,6},{11,7},{12,8},{13,9},{1... | collective-permute-start | bytes 49160 | tf_op jit(solution)/shard_map/ppermute | solution.py:229
  71.9 11.3 %collective-permute-start.13 = (f32[16,256]{1,0:T(8,128)S(1)}, f32[16,256]{1,0:T(8,128)S(1)}, u32[]{:S(2)}, u32[]{:S(2)}) collective-permute-start(f32[16,256]{1,0:T(8,128)S(1)} %get-tuple-element.27.st0), channel_id=1, source_target_pairs={{2,0},{3,1},{4,2},{5,3},{6,4},{7,5},{8,6},{9,7},{10,8},{11,9},{12,... | collective-permute-start | bytes 49160 | tf_op jit(solution)/shard_map/ppermute | solution.py:229
  75.8 7.5 %collective-permute-start.14 = (f32[16,256]{1,0:T(8,128)S(1)}, f32[16,256]{1,0:T(8,128)S(1)}, u32[]{:S(2)}, u32[]{:S(2)}) collective-permute-start(f32[16,256]{1,0:T(8,128)S(1)} %get-tuple-element.27.st0), channel_id=1, source_target_pairs={{1,0},{2,1},{3,2},{4,3},{5,4},{6,5},{7,6},{8,7},{9,8},{10,9},{11,1... | collective-permute-start | bytes 49160 | tf_op jit(solution)/shard_map/ppermute | solution.py:229

commit v4 on v3

--- a/solution.py
+++ b/solution.py
@@ -31,6 +31,17 @@
     return lax.dot_general(a, b, (((1,), (0,)), ((), ())), preferred_element_type=F32)
 
 
+class Rows:
+    def __init__(self, top, bottom):
+        self.top, self.bottom = top, bottom
+
+    def __getitem__(self, index):
+        rows, columns = index
+        if rows.start >= ROWS:
+            return self.bottom[rows.start - ROWS : rows.stop - ROWS, columns]
+        return self.top[rows, columns]
+
+
 def picks_of(off, p):
     rows = []
     for j in range(LEVELS):
@@ -73,10 +84,11 @@
     return jnp.where((near | (col >= WINDOW)) & (rank >= need), F32(0), F32(MASKED))
 
 
-def query_first(win, off, qd, kv0, kv1, kv2, kv4, kv8, scores_out, dprob_out, acc, top_out, total_out):
+def query_first(win, off, q, do, k0, v0, kv1, kv2, kv4, kv8, scores_out, dprob_out, acc, top_out, total_out):
     rank = lax.axis_index("ctx")
     levels = (kv2, kv4, kv8)
     heads = range(HEADS)
+    qd, kv0 = Rows(q, do), Rows(k0, v0)
     for p in range(BLOCKS):
         picks = picks_of(off, p)
         mine = slice(BLOCK * p, BLOCK * (p + 1))
@@ -97,9 +109,10 @@
             top_out[mine, head_columns(h)] = top[h]
 
 
-def query_last(off, qd, kv16, acc, top0, total0, _, att, stats, lse_out, delta_out, tall):
+def query_last(off, q, do, kv16, acc, top0, total0, _, att, stats, lse_out, delta_out, tall):
     rank = lax.axis_index("ctx")
     heads = range(HEADS)
+    qd = Rows(q, do)
     lane = lax.broadcasted_iota(jnp.int32, (BLOCK, 128), 1)
     bias = jnp.where(rank >= 2**LEVELS, F32(0), F32(MASKED))
     tiles = [(p, h) for p in range(BLOCKS) for h in heads]
@@ -146,9 +159,10 @@
     stats[2 * HEADS :, :] = chosen
 
 
-def query_gradient(off, qd, kv0, kv1, kv2, kv4, kv8, kv16, scores, dprob, lse, delta, dq):
+def query_gradient(off, q, do, k0, v0, kv1, kv2, kv4, kv8, kv16, scores, dprob, lse, delta, dq):
     rank = lax.axis_index("ctx")
     levels = (kv2, kv4, kv8)
+    qd, kv0 = Rows(q, do), Rows(k0, v0)
     heads = range(HEADS)
     bias = jnp.where(rank >= 2**LEVELS, F32(0), F32(MASKED))
     for p in range(BLOCKS):
@@ -176,7 +190,8 @@
     return jnp.concatenate([a[base + cut : base + ROWS, head], b[base : base + cut + HALF, head]], 0)
 
 
-def key_first(kv, qd2, qd4, qd8, scores, dprob):
+def key_first(k0, v0, qd2, qd4, qd8, scores, dprob):
+    kv = Rows(k0, v0)
     for h in range(HEADS):
         head = head_columns(h)
         for j, qd in enumerate((qd2, qd4, qd8)):
@@ -186,8 +201,9 @@
 
 
 def key_last(
-    win, kv, qd0, qd1, qd2, qd4, qd8, qd16, far_scores, far_dprob, st16, st8, st4, st2, st1, st0, dk, dv
+    win, k0, v0, q0, do0, qd1, qd2, qd4, qd8, qd16, far_scores, far_dprob, st16, st8, st4, st2, st1, st0, dk, dv
 ):
+    kv, qd0 = Rows(k0, v0), Rows(q0, do0)
     key_block = (lax.broadcasted_iota(jnp.int32, (ROWS, ROWS), 0) // BLOCK).astype(F32)
     far = ((qd2, st2), (qd4, st4), (qd8, st8), (qd16, st16))
     row = lax.broadcasted_iota(jnp.int32, (HALF, WIDE), 0)
@@ -234,6 +250,20 @@
     return lax.ppermute(array, "ctx", [(i, i ^ bit) for i in range(size)])
 
 
+def passed(array):
+    anywhere = pl.BlockSpec(memory_space=pl.ANY)
+    return pl.pallas_call(
+        lambda a, b: None,
+        out_shape=jax.ShapeDtypeStruct(array.shape, array.dtype),
+        in_specs=[anywhere],
+        out_specs=anywhere,
+        input_output_aliases={0: 0},
+        compiler_params=pltpu.CompilerParams(vmem_limit_bytes=2**20),
+        cost_estimate=pl.CostEstimate(flops=10**10, bytes_accessed=4 * 10**7, transcendentals=0),
+        name="passed",
+    )(array)
+
+
 def kernel(body, out_shape, n_smem, n_vmem, flops, scratch=(), n_any=0):
     smem = pl.BlockSpec(memory_space=pltpu.SMEM)
     vmem = pl.BlockSpec(memory_space=pltpu.VMEM)
@@ -259,32 +289,32 @@
     qd2 = swapped(jnp.where(rank % 4 < 2, qd4, qd0), 2)
     kv1 = swapped(jnp.where(rank % 2 == 0, kv0, kv2), 1)
     qd1 = swapped(jnp.where(rank % 2 == 0, qd2, qd0), 1)
-    kv8 = moved(kv4, 4)
-    qd8 = moved(qd4, -4)
+    kv8 = passed(moved(kv4, 4))
+    qd8 = passed(moved(qd4, -4))
     kv16 = moved(kv8, 8)
     qd16 = moved(qd8, -8)
     half = jax.ShapeDtypeStruct((ROWS, FEAT), BF16)
     f32 = lambda *shape: jax.ShapeDtypeStruct(shape, F32)
     unit = 2 * ROWS * FEAT
     scores, dprob, *sums = kernel(
-        query_first, (f32(HEADS, ROWS, FIRST), f32(HEADS, ROWS, FIRST)) + (f32(ROWS, FEAT),) * 3, 2, 6, unit * 3 * FIRST
-    )(window, offsets, qd0, kv0, kv1, kv2, kv4, kv8)
-    pre = kernel(key_first, (f32(HEADS, ROWS, 3 * ROWS),) * 2, 0, 4, unit * 2 * 3 * ROWS)(kv0, qd2, qd4, qd8)
+        query_first, (f32(HEADS, ROWS, FIRST), f32(HEADS, ROWS, FIRST)) + (f32(ROWS, FEAT),) * 3, 2, 8, unit * 3 * FIRST
+    )(window, offsets, queries, grad_out, keys, values, kv1, kv2, kv4, kv8)
+    pre = kernel(key_first, (f32(HEADS, ROWS, 3 * ROWS),) * 2, 0, 5, unit * 2 * 3 * ROWS)(keys, values, qd2, qd4, qd8)
     attended, stats, lse, delta = kernel(
         query_last,
         (half, f32(STAT_ROWS, ROWS), f32(ROWS, FEAT), f32(ROWS, FEAT)),
         1,
-        5,
+        6,
         unit * 2 * BLOCK,
         (pltpu.VMEM((ROWS, 128), F32),),
         n_any=1,
-    )(offsets, qd0, kv16, *sums, pre[1])
+    )(offsets, queries, grad_out, kv16, *sums, pre[1])
     received = [moved(stats, -by) for by in (1, 2, 4, 8, 16)]
-    (grad_q,) = kernel(query_gradient, (half,), 1, 11, unit * FIRST)(
-        offsets, qd0, kv0, kv1, kv2, kv4, kv8, kv16, scores, dprob, lse, delta
+    (grad_q,) = kernel(query_gradient, (half,), 1, 13, unit * FIRST)(
+        offsets, queries, grad_out, keys, values, kv1, kv2, kv4, kv8, kv16, scores, dprob, lse, delta
     )
-    grad_k, grad_v = kernel(key_last, (half, half), 1, 15, unit * 2 * 6 * ROWS)(
-        window, kv0, qd0, qd1, qd2, qd4, qd8, qd16, *pre, *received[::-1], stats
+    grad_k, grad_v = kernel(key_last, (half, half), 1, 17, unit * 2 * 6 * ROWS)(
+        window, keys, values, queries, grad_out, qd1, qd2, qd4, qd8, qd16, *pre, *received[::-1], stats
     )
     return attended, grad_q, grad_k, grad_v
 

time: 88.5 us -> 87 us (0.983)
  other arithmetic: 1.84 us -> 0.22 us
  starting transfers between devices: 41.2 us -> 42.1 us
    pallas_call x3 -> x5, Pallas kernels: 8.74 us -> 8.39 us  [the longest x1 4.78 us: on_device(): kernel(key_last, (half, half), 1, 17, unit * 2 * 6 * ROWS)]
    unnamed x6 -> x14, local copies, waits for them, and re-layouts: 1.95 us -> 1.98 us
  transfers between devices with their start and end apart: 15 -> 15, of which waited for: 4 -> 5; matrix products, arithmetic and copies ran while one was open for 4% -> 3% of each run, Pallas kernels for 10% -> 9%
where the time goes in v4:
time: 87 us; the launch traced here: 86.5 us
  starting transfers between devices  42.1 us (48%)
  waiting for transfers between devices  26.3 us (30%)
  Pallas kernels  13 us (15%)
  local copies, waits for them, and re-layouts  3.92 us (5%)
  between operations  0.92 us (1%)
    ppermute x11, starting transfers between devices, moved(): lax.ppermute(array, 'ctx', [(i, i + by) for i in range(size) if 0 <= i +...  32.3 us
    ppermute x11, waiting for transfers between devices, moved(): lax.ppermute(array, 'ctx', [(i, i + by) for i in range(size) if 0 <= i +...  17.3 us
    ppermute x4, starting transfers between devices, swapped(): return lax.ppermute(array, 'ctx', [(i, i ^ bit) for i in range(size)])  9.77 us
    ppermute x4, waiting for transfers between devices, swapped(): return lax.ppermute(array, 'ctx', [(i, i ^ bit) for i in range(size)])  8.98 us
    pallas_call x1, Pallas kernels, on_device(): kernel(key_last, (half, half), 1, 17, unit * 2 * 6 * ROWS)  4.78 us
    pallas_call x1, Pallas kernels, on_device(): kernel(query_first, (f32(HEADS, ROWS, FIRST), f32(HEADS, ROWS, FIRST)) +...  2.64 us
    pallas_call x1, Pallas kernels, on_device(): kernel(query_gradient, (half,), 1, 13, unit * FIRST)  2.62 us
    unnamed x14, local copies, waits for them, and re-layouts  1.98 us
  transfers between devices with their start and end apart: 15, of which 5 were waited for; matrix products, arithmetic and copies ran while one was open for 3% of the time, Pallas kernels for 9%

profile of v4, /device:TPU:249, one launch (start us, length us, event | category | flops | bytes accessed | tf_op | source)
XLA Modules:
  0.0 86.5 jit_solution(1561972458233263218)
XLA Ops:
  2.6 1.3 %collective-permute-start = (bf16[512,512]{1,0:T(8,128)(2,1)S(1)}, bf16[512,512]{1,0:T(8,128)(2,1)S(1)}, u32[]{:S(2)}, u32[]{:S(2)}) collective-permute-start(bf16[512,512]{1,0:T(8,128)(2,1)S(1)} %constant_dynamic-update-slice_fusion), channel_id=1, source_target_pairs={{0,4},{1,5},{2,6},{3,7},{4,8},{5,9},{6,10},{7,11},{8,12},{9,13},{1... | collective-permute-start | bytes 1572872 | tf_op jit(solution)/shard_map/ppermute | solution.py:245
  5.8 4.0 %collective-permute-start.5 = (bf16[512,512]{1,0:T(8,128)(2,1)S(1)}, bf16[512,512]{1,0:T(8,128)(2,1)S(1)}, u32[]{:S(2)}, u32[]{:S(2)}) collective-permute-start(bf16[512,512]{1,0:T(8,128)(2,1)S(1)} %constant_dynamic-update-slice_fusion.2), channel_id=1, source_target_pairs={{4,0},{5,1},{6,2},{7,3},{8,4},{9,5},{10,6},{11,7},{12,8},{13,9},{1... | collective-permute-start | bytes 1572872 | tf_op jit(solution)/shard_map/ppermute | solution.py:245
  9.9 7.4 %collective-permute-done.kv4 = bf16[512,512]{1,0:T(8,128)(2,1)S(1)} collective-permute-done((bf16[512,512]{1,0:T(8,128)(2,1)S(1)}, bf16[512,512]{1,0:T(8,128)(2,1)S(1)}, u32[]{:S(2)}, u32[]{:S(2)}) %collective-permute-start) | collective-permute-done | bytes 524320 | tf_op jit(solution)/shard_map/ppermute | solution.py:245
  17.3 1.3 %collective-permute-start.3 = (bf16[512,512]{1,0:T(8,128)(2,1)S(1)}, bf16[512,512]{1,0:T(8,128)(2,1)S(1)}, u32[]{:S(2)}, u32[]{:S(2)}) collective-permute-start(bf16[512,512]{1,0:T(8,128)(2,1)S(1)} %broadcast_select_fusion.1), channel_id=1, source_target_pairs={{0,2},{1,3},{2,0},{3,1},{4,6},{5,7},{6,4},{7,5},{8,10},{9,11},{10,... | collective-permute-start | bytes 1572872 | tf_op jit(solution)/shard_map/ppermute | solution.py:250
  18.6 1.3 %collective-permute-start.1 = (bf16[512,512]{1,0:T(8,128)(2,1)S(1)}, bf16[512,512]{1,0:T(8,128)(2,1)S(1)}, u32[]{:S(2)}, u32[]{:S(2)}) collective-permute-start(bf16[512,512]{1,0:T(8,128)(2,1)S(1)} %collective-permute-done.kv4), channel_id=1, source_target_pairs={{0,4},{1,5},{2,6},{3,7},{4,8},{5,9},{6,10},{7,11},{8,12},{9,13},{1... | collective-permute-start | bytes 1572872 | tf_op jit(solution)/shard_map/ppermute | solution.py:245
  20.1 1.3 %collective-permute-start.6 = (bf16[512,512]{1,0:T(8,128)(2,1)S(1)}, bf16[512,512]{1,0:T(8,128)(2,1)S(1)}, u32[]{:S(2)}, u32[]{:S(2)}) collective-permute-start(bf16[512,512]{1,0:T(8,128)(2,1)S(1)} %broadcast_select_fusion), channel_id=1, source_target_pairs={{0,2},{1,3},{2,0},{3,1},{4,6},{5,7},{6,4},{7,5},{8,10},{9,11},{10,... | collective-permute-start | bytes 1572872 | tf_op jit(solution)/shard_map/ppermute | solution.py:250
  21.4 4.1 %collective-permute-start.7 = (bf16[512,512]{1,0:T(8,128)(2,1)S(1)}, bf16[512,512]{1,0:T(8,128)(2,1)S(1)}, u32[]{:S(2)}, u32[]{:S(2)}) collective-permute-start(bf16[512,512]{1,0:T(8,128)(2,1)S(1)} %collective-permute-done.5.qd4), channel_id=1, source_target_pairs={{4,0},{5,1},{6,2},{7,3},{8,4},{9,5},{10,6},{11,7},{12,8},{13,9},{1... | collective-permute-start | bytes 1572872 | tf_op jit(solution)/shard_map/ppermute | solution.py:245
  25.6 3.7 %collective-permute-done.3.kv2 = bf16[512,512]{1,0:T(8,128)(2,1)S(1)} collective-permute-done((bf16[512,512]{1,0:T(8,128)(2,1)S(1)}, bf16[512,512]{1,0:T(8,128)(2,1)S(1)}, u32[]{:S(2)}, u32[]{:S(2)}) %collective-permute-start.3) | collective-permute-done | bytes 524320 | tf_op jit(solution)/shard_map/ppermute | solution.py:250
  29.3 4.6 %collective-permute-start.4 = (bf16[512,512]{1,0:T(8,128)(2,1)S(1)}, bf16[512,512]{1,0:T(8,128)(2,1)S(1)}, u32[]{:S(2)}, u32[]{:S(2)}) collective-permute-start(bf16[512,512]{1,0:T(8,128)(2,1)S(1)} %broadcast_select_fusion.3), channel_id=1, source_target_pairs={{0,1},{1,0},{2,3},{3,2},{4,5},{5,4},{6,7},{7,6},{8,9},{9,8},{10,11... | collective-permute-start | bytes 1572872 | tf_op jit(solution)/shard_map/ppermute | solution.py:250
  34.0 1.3 %collective-permute-start.2 = (bf16[512,512]{1,0:T(8,128)(2,1)S(1)}, bf16[512,512]{1,0:T(8,128)(2,1)S(1)}, u32[]{:S(2)}, u32[]{:S(2)}) collective-permute-start(bf16[512,512]{1,0:T(8,128)(2,1)S(1)} %passed.2.kv8), channel_id=1, source_target_pairs={{0,8},{1,9},{2,10},{3,11},{4,12},{5,13},{6,14},{7,15},{8,16},{9,17... | collective-permute-start | bytes 1572872 | tf_op jit(solution)/shard_map/ppermute | solution.py:245
  35.3 5.3 %collective-permute-done.6.qd2 = bf16[512,512]{1,0:T(8,128)(2,1)S(1)} collective-permute-done((bf16[512,512]{1,0:T(8,128)(2,1)S(1)}, bf16[512,512]{1,0:T(8,128)(2,1)S(1)}, u32[]{:S(2)}, u32[]{:S(2)}) %collective-permute-start.6) | collective-permute-done | bytes 524320 | tf_op jit(solution)/shard_map/ppermute | solution.py:250
  40.6 2.6 %collective-permute-start.8 = (bf16[512,512]{1,0:T(8,128)(2,1)S(1)}, bf16[512,512]{1,0:T(8,128)(2,1)S(1)}, u32[]{:S(2)}, u32[]{:S(2)}) collective-permute-start(bf16[512,512]{1,0:T(8,128)(2,1)S(1)} %broadcast_select_fusion.2), channel_id=1, source_target_pairs={{0,1},{1,0},{2,3},{3,2},{4,5},{5,4},{6,7},{7,6},{8,9},{9,8},{10,11... | collective-permute-start | bytes 1572872 | tf_op jit(solution)/shard_map/ppermute | solution.py:250
  43.2 3.1 %collective-permute-start.9 = (bf16[512,512]{1,0:T(8,128)(2,1)S(1)}, bf16[512,512]{1,0:T(8,128)(2,1)S(1)}, u32[]{:S(2)}, u32[]{:S(2)}) collective-permute-start(bf16[512,512]{1,0:T(8,128)(2,1)S(1)} %passed.3.qd8), channel_id=1, source_target_pairs={{8,0},{9,1},{10,2},{11,3},{12,4},{13,5},{14,6},{15,7},{16,8},{17,9... | collective-permute-start | bytes 1572872 | tf_op jit(solution)/shard_map/ppermute | solution.py:245
  46.3 1.0 %key_first.1 = (f32[4,256,768]{2,1,0:T(8,128)S(1)}, f32[4,256,768]{2,1,0:T(8,128)S(1)}) custom-call(bf16[256,512]{1,0:T(8,128)(2,1)S(1)} %copy-done, bf16[256,512]{1,0:T(8,128)(2,1)S(1)} %copy-done.1, bf16[512,512]{1,0:T(8,128)(2,1)S(1)} %collective-permute-done.6.qd2, bf16[512,512]{1,0:T(8,128)(2,1)S(1)} %collective-permute-done.5.qd4, ...), custom_call_target="tpu_custom_call" | custom-call | flops 402653184 | bytes 2621440 | tf_op jit(solution)/shard_map/key_first/pallas_call | solution.py:302
  47.4 2.6 %query_first.1 = (f32[4,256,512]{2,1,0:T(8,128)S(1)}, f32[4,256,512]{2,1,0:T(8,128)S(1)}, f32[256,512]{1,0:T(8,128)S(1)}, f32[256,512]{1,0:T(8,128)S(1)}, f32[256,512]{1,0:T(8,128)S(1)}) custom-call(s32[4]{0:T(128)S(1)} %copy-done.5, s32[4,4]{1,0:T(4,128)S(1)} %copy-done.4, bf16[256,512]{1,0:T(8,128)(2,1)S(1)} %copy-done.2, bf16[256,512]{1,0:T(8,128)(2,1)S(1)} %copy-done.3, ...), custom_call_target="tpu_custom_call" | custom-call | flops 402653184 | bytes 4194304 | tf_op jit(solution)/shard_map/query_first/pallas_call | solution.py:299
  50.0 9.7 %collective-permute-done.2.kv16 = bf16[512,512]{1,0:T(8,128)(2,1)S(1)} collective-permute-done((bf16[512,512]{1,0:T(8,128)(2,1)S(1)}, bf16[512,512]{1,0:T(8,128)(2,1)S(1)}, u32[]{:S(2)}, u32[]{:S(2)}) %collective-permute-start.2) | collective-permute-done | bytes 524320 | tf_op jit(solution)/shard_map/ppermute | solution.py:245
  59.8 2.0 %query_last.1 = (bf16[256,512]{1,0:T(8,128)(2,1)}, f32[16,256]{1,0:T(8,128)S(1)}, f32[256,512]{1,0:T(8,128)S(1)}, f32[256,512]{1,0:T(8,128)S(1)}) custom-call(s32[4,4]{1,0:T(4,128)S(1)} %copy-done.4, bf16[256,512]{1,0:T(8,128)(2,1)S(1)} %copy-done.2, bf16[256,512]{1,0:T(8,128)(2,1)S(1)} %copy-done.3, bf16[512,512]{1,0:T(8,128)(2,1)S(1)} %collective-permute-done.2.kv16, ...), custom_call_target="tpu_custom_call" | custom-call | flops 33554432 | bytes 3145728 | tf_op jit(solution)/shard_map/query_last/pallas_call | solution.py:303
  61.7 4.7 %collective-permute-start.10 = (f32[16,256]{1,0:T(8,128)S(1)}, f32[16,256]{1,0:T(8,128)S(1)}, u32[]{:S(2)}, u32[]{:S(2)}) collective-permute-start(f32[16,256]{1,0:T(8,128)S(1)} %get-tuple-element.27.st0), channel_id=1, source_target_pairs={{16,0},{17,1},{18,2},{19,3},{20,4},{21,5},{22,6},{23,7},{24,8},{25... | collective-permute-start | bytes 49160 | tf_op jit(solution)/shard_map/ppermute | solution.py:245
  66.4 1.3 %collective-permute-start.11 = (f32[16,256]{1,0:T(8,128)S(1)}, f32[16,256]{1,0:T(8,128)S(1)}, u32[]{:S(2)}, u32[]{:S(2)}) collective-permute-start(f32[16,256]{1,0:T(8,128)S(1)} %get-tuple-element.27.st0), channel_id=1, source_target_pairs={{8,0},{9,1},{10,2},{11,3},{12,4},{13,5},{14,6},{15,7},{16,8},{17,9... | collective-permute-start | bytes 49160 | tf_op jit(solution)/shard_map/ppermute | solution.py:245
  67.7 3.0 %collective-permute-start.12 = (f32[16,256]{1,0:T(8,128)S(1)}, f32[16,256]{1,0:T(8,128)S(1)}, u32[]{:S(2)}, u32[]{:S(2)}) collective-permute-start(f32[16,256]{1,0:T(8,128)S(1)} %get-tuple-element.27.st0), channel_id=1, source_target_pairs={{4,0},{5,1},{6,2},{7,3},{8,4},{9,5},{10,6},{11,7},{12,8},{13,9},{1... | collective-permute-start | bytes 49160 | tf_op jit(solution)/shard_map/ppermute | solution.py:245
  70.7 3.8 %collective-permute-start.13 = (f32[16,256]{1,0:T(8,128)S(1)}, f32[16,256]{1,0:T(8,128)S(1)}, u32[]{:S(2)}, u32[]{:S(2)}) collective-permute-start(f32[16,256]{1,0:T(8,128)S(1)} %get-tuple-element.27.st0), channel_id=1, source_target_pairs={{2,0},{3,1},{4,2},{5,3},{6,4},{7,5},{8,6},{9,7},{10,8},{11,9},{12,... | collective-permute-start | bytes 49160 | tf_op jit(solution)/shard_map/ppermute | solution.py:245
  74.5 4.5 %collective-permute-start.14 = (f32[16,256]{1,0:T(8,128)S(1)}, f32[16,256]{1,0:T(8,128)S(1)}, u32[]{:S(2)}, u32[]{:S(2)}) collective-permute-start(f32[16,256]{1,0:T(8,128)S(1)} %get-tuple-element.27.st0), channel_id=1, source_target_pairs={{1,0},{2,1},{3,2},{4,3},{5,4},{6,5},{7,6},{8,7},{9,8},{10,9},{11,1... | collective-permute-start | bytes 49160 | tf_op jit(solution)/shard_map/ppermute | solution.py:245
  79.0 2.6 %query_gradient.1 = bf16[256,512]{1,0:T(8,128)(2,1)} custom-call(s32[4,4]{1,0:T(4,128)S(1)} %copy-done.4, bf16[256,512]{1,0:T(8,128)(2,1)S(1)} %copy-done.2, bf16[256,512]{1,0:T(8,128)(2,1)S(1)} %copy-done.3, bf16[256,512]{1,0:T(8,128)(2,1)S(1)} %copy-done, bf16[256,512]{1,0:T(8,128)(2,1)S(1)} %copy-done.1, bf16[512,512]{1,0:T(8,128)(2,1)S(1)} %collective-permute-done.4.kv1, ...), custom_call_target="tpu_custom_call" | custom-call | flops 134217728 | bytes 6815744 | tf_op jit(solution)/shard_map/query_gradient/pallas_call | solution.py:313
  81.7 4.8 %key_last.1 = (bf16[256,512]{1,0:T(8,128)(2,1)}, bf16[256,512]{1,0:T(8,128)(2,1)}) custom-call(s32[4]{0:T(128)S(1)} %copy-done.5, bf16[256,512]{1,0:T(8,128)(2,1)S(1)} %copy-done, bf16[256,512]{1,0:T(8,128)(2,1)S(1)} %copy-done.1, bf16[256,512]{1,0:T(8,128)(2,1)S(1)} %copy-done.2, bf16[256,512]{1,0:T(8,128)(2,1)S(1)} %copy-done.3, ...), custom_call_target="tpu_custom_call" | custom-call | flops 805306368 | bytes 8912896 | tf_op jit(solution)/shard_map/key_last/pallas_call | solution.py:316
  (33 shorter events, 4.3 us)
Async XLA Ops:
  2.6 14.7 %collective-permute-start = (bf16[512,512]{1,0:T(8,128)(2,1)S(1)}, bf16[512,512]{1,0:T(8,128)(2,1)S(1)}, u32[]{:S(2)}, u32[]{:S(2)}) collective-permute-start(bf16[512,512]{1,0:T(8,128)(2,1)S(1)} %constant_dynamic-update-slice_fusion), channel_id=1, source_target_pairs={{0,4},{1,5},{2,6},{3,7},{4,8},{5,9},{6,10},{7,11},{8,12},{9,13},{1... | collective-permute-start | bytes 1572872 | tf_op jit(solution)/shard_map/ppermute | solution.py:245
  5.8 14.2 %collective-permute-start.5 = (bf16[512,512]{1,0:T(8,128)(2,1)S(1)}, bf16[512,512]{1,0:T(8,128)(2,1)S(1)}, u32[]{:S(2)}, u32[]{:S(2)}) collective-permute-start(bf16[512,512]{1,0:T(8,128)(2,1)S(1)} %constant_dynamic-update-slice_fusion.2), channel_id=1, source_target_pairs={{4,0},{5,1},{6,2},{7,3},{8,4},{9,5},{10,6},{11,7},{12,8},{13,9},{1... | collective-permute-start | bytes 1572872 | tf_op jit(solution)/shard_map/ppermute | solution.py:245
  17.3 12.0 %collective-permute-start.3 = (bf16[512,512]{1,0:T(8,128)(2,1)S(1)}, bf16[512,512]{1,0:T(8,128)(2,1)S(1)}, u32[]{:S(2)}, u32[]{:S(2)}) collective-permute-start(bf16[512,512]{1,0:T(8,128)(2,1)S(1)} %broadcast_select_fusion.1), channel_id=1, source_target_pairs={{0,2},{1,3},{2,0},{3,1},{4,6},{5,7},{6,4},{7,5},{8,10},{9,11},{10,... | collective-permute-start | bytes 1572872 | tf_op jit(solution)/shard_map/ppermute | solution.py:250
  18.6 15.3 %collective-permute-start.1 = (bf16[512,512]{1,0:T(8,128)(2,1)S(1)}, bf16[512,512]{1,0:T(8,128)(2,1)S(1)}, u32[]{:S(2)}, u32[]{:S(2)}) collective-permute-start(bf16[512,512]{1,0:T(8,128)(2,1)S(1)} %collective-permute-done.kv4), channel_id=1, source_target_pairs={{0,4},{1,5},{2,6},{3,7},{4,8},{5,9},{6,10},{7,11},{8,12},{9,13},{1... | collective-permute-start | bytes 1572872 | tf_op jit(solution)/shard_map/ppermute | solution.py:245
  20.1 20.4 %collective-permute-start.6 = (bf16[512,512]{1,0:T(8,128)(2,1)S(1)}, bf16[512,512]{1,0:T(8,128)(2,1)S(1)}, u32[]{:S(2)}, u32[]{:S(2)}) collective-permute-start(bf16[512,512]{1,0:T(8,128)(2,1)S(1)} %broadcast_select_fusion), channel_id=1, source_target_pairs={{0,2},{1,3},{2,0},{3,1},{4,6},{5,7},{6,4},{7,5},{8,10},{9,11},{10,... | collective-permute-start | bytes 1572872 | tf_op jit(solution)/shard_map/ppermute | solution.py:250
  21.4 21.8 %collective-permute-start.7 = (bf16[512,512]{1,0:T(8,128)(2,1)S(1)}, bf16[512,512]{1,0:T(8,128)(2,1)S(1)}, u32[]{:S(2)}, u32[]{:S(2)}) collective-permute-start(bf16[512,512]{1,0:T(8,128)(2,1)S(1)} %collective-permute-done.5.qd4), channel_id=1, source_target_pairs={{4,0},{5,1},{6,2},{7,3},{8,4},{9,5},{10,6},{11,7},{12,8},{13,9},{1... | collective-permute-start | bytes 1572872 | tf_op jit(solution)/shard_map/ppermute | solution.py:245
  29.3 18.0 %collective-permute-start.4 = (bf16[512,512]{1,0:T(8,128)(2,1)S(1)}, bf16[512,512]{1,0:T(8,128)(2,1)S(1)}, u32[]{:S(2)}, u32[]{:S(2)}) collective-permute-start(bf16[512,512]{1,0:T(8,128)(2,1)S(1)} %broadcast_select_fusion.3), channel_id=1, source_target_pairs={{0,1},{1,0},{2,3},{3,2},{4,5},{5,4},{6,7},{7,6},{8,9},{9,8},{10,11... | collective-permute-start | bytes 1572872 | tf_op jit(solution)/shard_map/ppermute | solution.py:250
  34.0 25.8 %collective-permute-start.2 = (bf16[512,512]{1,0:T(8,128)(2,1)S(1)}, bf16[512,512]{1,0:T(8,128)(2,1)S(1)}, u32[]{:S(2)}, u32[]{:S(2)}) collective-permute-start(bf16[512,512]{1,0:T(8,128)(2,1)S(1)} %passed.2.kv8), channel_id=1, source_target_pairs={{0,8},{1,9},{2,10},{3,11},{4,12},{5,13},{6,14},{7,15},{8,16},{9,17... | collective-permute-start | bytes 1572872 | tf_op jit(solution)/shard_map/ppermute | solution.py:245
  40.6 5.7 %copy-start = (bf16[256,512]{1,0:T(8,128)(2,1)S(1)}, bf16[256,512]{1,0:T(8,128)(2,1)}, u32[]{:S(2)}) copy-start(bf16[256,512]{1,0:T(8,128)(2,1)} %k0.7) | copy-start | bytes 786436
  40.6 5.7 %copy-start.1 = (bf16[256,512]{1,0:T(8,128)(2,1)S(1)}, bf16[256,512]{1,0:T(8,128)(2,1)}, u32[]{:S(2)}) copy-start(bf16[256,512]{1,0:T(8,128)(2,1)} %v0.7) | copy-start | bytes 786436
  40.6 6.7 %copy-start.2 = (bf16[256,512]{1,0:T(8,128)(2,1)S(1)}, bf16[256,512]{1,0:T(8,128)(2,1)}, u32[]{:S(2)}) copy-start(bf16[256,512]{1,0:T(8,128)(2,1)} %q0.1) | copy-start | bytes 786436
  40.6 6.7 %copy-start.3 = (bf16[256,512]{1,0:T(8,128)(2,1)S(1)}, bf16[256,512]{1,0:T(8,128)(2,1)}, u32[]{:S(2)}) copy-start(bf16[256,512]{1,0:T(8,128)(2,1)} %do0.1) | copy-start | bytes 786436
  40.6 6.7 %copy-start.4 = (s32[4,4]{1,0:T(4,128)S(1)}, s32[4,4]{1,0:T(4,128)}, u32[]{:S(2)}) copy-start(s32[4,4]{1,0:T(4,128)} %off.5) | copy-start | bytes 196
  40.6 6.7 %copy-start.5 = (s32[4]{0:T(128)S(1)}, s32[4]{0:T(128)}, u32[]{:S(2)}) copy-start(s32[4]{0:T(128)} %win.3) | copy-start | bytes 52
  40.6 30.1 %collective-permute-start.8 = (bf16[512,512]{1,0:T(8,128)(2,1)S(1)}, bf16[512,512]{1,0:T(8,128)(2,1)S(1)}, u32[]{:S(2)}, u32[]{:S(2)}) collective-permute-start(bf16[512,512]{1,0:T(8,128)(2,1)S(1)} %broadcast_select_fusion.2), channel_id=1, source_target_pairs={{0,1},{1,0},{2,3},{3,2},{4,5},{5,4},{6,7},{7,6},{8,9},{9,8},{10,11... | collective-permute-start | bytes 1572872 | tf_op jit(solution)/shard_map/ppermute | solution.py:250
  43.2 31.3 %collective-permute-start.9 = (bf16[512,512]{1,0:T(8,128)(2,1)S(1)}, bf16[512,512]{1,0:T(8,128)(2,1)S(1)}, u32[]{:S(2)}, u32[]{:S(2)}) collective-permute-start(bf16[512,512]{1,0:T(8,128)(2,1)S(1)} %passed.3.qd8), channel_id=1, source_target_pairs={{8,0},{9,1},{10,2},{11,3},{12,4},{13,5},{14,6},{15,7},{16,8},{17,9... | collective-permute-start | bytes 1572872 | tf_op jit(solution)/shard_map/ppermute | solution.py:245
  61.7 19.9 %collective-permute-start.10 = (f32[16,256]{1,0:T(8,128)S(1)}, f32[16,256]{1,0:T(8,128)S(1)}, u32[]{:S(2)}, u32[]{:S(2)}) collective-permute-start(f32[16,256]{1,0:T(8,128)S(1)} %get-tuple-element.27.st0), channel_id=1, source_target_pairs={{16,0},{17,1},{18,2},{19,3},{20,4},{21,5},{22,6},{23,7},{24,8},{25... | collective-permute-start | bytes 49160 | tf_op jit(solution)/shard_map/ppermute | solution.py:245
  66.4 15.2 %collective-permute-start.11 = (f32[16,256]{1,0:T(8,128)S(1)}, f32[16,256]{1,0:T(8,128)S(1)}, u32[]{:S(2)}, u32[]{:S(2)}) collective-permute-start(f32[16,256]{1,0:T(8,128)S(1)} %get-tuple-element.27.st0), channel_id=1, source_target_pairs={{8,0},{9,1},{10,2},{11,3},{12,4},{13,5},{14,6},{15,7},{16,8},{17,9... | collective-permute-start | bytes 49160 | tf_op jit(solution)/shard_map/ppermute | solution.py:245
  67.7 13.9 %collective-permute-start.12 = (f32[16,256]{1,0:T(8,128)S(1)}, f32[16,256]{1,0:T(8,128)S(1)}, u32[]{:S(2)}, u32[]{:S(2)}) collective-permute-start(f32[16,256]{1,0:T(8,128)S(1)} %get-tuple-element.27.st0), channel_id=1, source_target_pairs={{4,0},{5,1},{6,2},{7,3},{8,4},{9,5},{10,6},{11,7},{12,8},{13,9},{1... | collective-permute-start | bytes 49160 | tf_op jit(solution)/shard_map/ppermute | solution.py:245
  70.7 10.9 %collective-permute-start.13 = (f32[16,256]{1,0:T(8,128)S(1)}, f32[16,256]{1,0:T(8,128)S(1)}, u32[]{:S(2)}, u32[]{:S(2)}) collective-permute-start(f32[16,256]{1,0:T(8,128)S(1)} %get-tuple-element.27.st0), channel_id=1, source_target_pairs={{2,0},{3,1},{4,2},{5,3},{6,4},{7,5},{8,6},{9,7},{10,8},{11,9},{12,... | collective-permute-start | bytes 49160 | tf_op jit(solution)/shard_map/ppermute | solution.py:245
  74.5 7.1 %collective-permute-start.14 = (f32[16,256]{1,0:T(8,128)S(1)}, f32[16,256]{1,0:T(8,128)S(1)}, u32[]{:S(2)}, u32[]{:S(2)}) collective-permute-start(f32[16,256]{1,0:T(8,128)S(1)} %get-tuple-element.27.st0), channel_id=1, source_target_pairs={{1,0},{2,1},{3,2},{4,3},{5,4},{6,5},{7,6},{8,7},{9,8},{10,9},{11,1... | collective-permute-start | bytes 49160 | tf_op jit(solution)/shard_map/ppermute | solution.py:245

commit v5 on v4

--- a/solution.py
+++ b/solution.py
@@ -264,6 +264,26 @@
     )(array)
 
 
+def pack(*refs):
+    count = len(refs) * 2 // 3
+    for i in range(count):
+        refs[count + i // 2][ROWS * (i % 2) : ROWS * (i % 2 + 1), :] = refs[i][...]
+
+
+def packed(*arrays):
+    vmem = pl.BlockSpec(memory_space=pltpu.VMEM)
+    pair = jax.ShapeDtypeStruct((2 * ROWS, FEAT), BF16)
+    return pl.pallas_call(
+        pack,
+        out_shape=(pair,) * (len(arrays) // 2),
+        in_specs=[vmem] * len(arrays),
+        out_specs=(vmem,) * (len(arrays) // 2),
+        compiler_params=pltpu.CompilerParams(vmem_limit_bytes=8 * 2**20),
+        cost_estimate=pl.CostEstimate(flops=0, bytes_accessed=len(arrays) * ROWS * FEAT * 4, transcendentals=0),
+        name="pack",
+    )(*arrays)
+
+
 def kernel(body, out_shape, n_smem, n_vmem, flops, scratch=(), n_any=0):
     smem = pl.BlockSpec(memory_space=pltpu.SMEM)
     vmem = pl.BlockSpec(memory_space=pltpu.VMEM)
@@ -281,8 +301,8 @@
 
 def on_device(queries, keys, values, grad_out, window, offsets):
     rank = lax.axis_index("ctx")
-    kv0 = jnp.concatenate([keys, values], 0)
-    qd0 = jnp.concatenate([queries, grad_out], 0)
+    (kv0,) = packed(keys, values)
+    (qd0,) = packed(queries, grad_out)
     kv4 = moved(kv0, 4)
     qd4 = moved(qd0, -4)
     kv2 = swapped(jnp.where(rank % 4 < 2, kv0, kv4), 2)

time: 87 us -> 87 us (level)
    concatenate x2 -> x0, local copies, waits for them, and re-layouts: 1.94 us -> none  [the longest x1 0.97 us: on_device(): kv0 = jnp.concatenate([keys, values], 0)]
    unnamed x14 -> x20, local copies, waits for them, and re-layouts: 1.98 us -> 3.83 us
  transfers between devices with their start and end apart: 15 -> 15, of which waited for: 5 -> 5; matrix products, arithmetic and copies ran while one was open for 3% -> 0% of each run, Pallas kernels for 9% -> 10%
where the time goes in v5:
time: 87 us; the launch traced here: 86.5 us
  starting transfers between devices  42.1 us (48%)
  waiting for transfers between devices  26.3 us (30%)
  Pallas kernels  13.1 us (15%)
  local copies, waits for them, and re-layouts  3.83 us (4%)
  between operations  0.93 us (1%)
    ppermute x11, starting transfers between devices, moved(): lax.ppermute(array, 'ctx', [(i, i + by) for i in range(size) if 0 <= i +...  32.3 us
    ppermute x11, waiting for transfers between devices, moved(): lax.ppermute(array, 'ctx', [(i, i + by) for i in range(size) if 0 <= i +...  17.3 us
    ppermute x4, starting transfers between devices, swapped(): return lax.ppermute(array, 'ctx', [(i, i ^ bit) for i in range(size)])  9.77 us
    ppermute x4, waiting for transfers between devices, swapped(): return lax.ppermute(array, 'ctx', [(i, i ^ bit) for i in range(size)])  8.98 us
    pallas_call x1, Pallas kernels, on_device(): kernel(key_last, (half, half), 1, 17, unit * 2 * 6 * ROWS)  4.79 us
    unnamed x20, local copies, waits for them, and re-layouts  3.83 us
    pallas_call x1, Pallas kernels, on_device(): kernel(query_first, (f32(HEADS, ROWS, FIRST), f32(HEADS, ROWS, FIRST)) +...  2.64 us
    pallas_call x1, Pallas kernels, on_device(): kernel(query_gradient, (half,), 1, 13, unit * FIRST)  2.62 us
  transfers between devices with their start and end apart: 15, of which 5 were waited for; matrix products, arithmetic and copies ran while one was open for 0% of the time, Pallas kernels for 10%

profile of v5, /device:TPU:249, one launch (start us, length us, event | category | flops | bytes accessed | tf_op | source)
XLA Modules:
  0.0 86.5 jit_solution(3968181099131984156)
XLA Ops:
  2.6 1.3 %collective-permute-start = (bf16[512,512]{1,0:T(8,128)(2,1)S(1)}, bf16[512,512]{1,0:T(8,128)(2,1)S(1)}, u32[]{:S(2)}, u32[]{:S(2)}) collective-permute-start(bf16[512,512]{1,0:T(8,128)(2,1)S(1)} %pack.2), channel_id=1, source_target_pairs={{0,4},{1,5},{2,6},{3,7},{4,8},{5,9},{6,10},{7,11},{8,12},{9,13},{1... | collective-permute-start | bytes 1572872 | tf_op jit(solution)/shard_map/ppermute | solution.py:245
  5.8 4.0 %collective-permute-start.5 = (bf16[512,512]{1,0:T(8,128)(2,1)S(1)}, bf16[512,512]{1,0:T(8,128)(2,1)S(1)}, u32[]{:S(2)}, u32[]{:S(2)}) collective-permute-start(bf16[512,512]{1,0:T(8,128)(2,1)S(1)} %pack.3), channel_id=1, source_target_pairs={{4,0},{5,1},{6,2},{7,3},{8,4},{9,5},{10,6},{11,7},{12,8},{13,9},{1... | collective-permute-start | bytes 1572872 | tf_op jit(solution)/shard_map/ppermute | solution.py:245
  9.9 7.4 %collective-permute-done.kv4 = bf16[512,512]{1,0:T(8,128)(2,1)S(1)} collective-permute-done((bf16[512,512]{1,0:T(8,128)(2,1)S(1)}, bf16[512,512]{1,0:T(8,128)(2,1)S(1)}, u32[]{:S(2)}, u32[]{:S(2)}) %collective-permute-start) | collective-permute-done | bytes 524320 | tf_op jit(solution)/shard_map/ppermute | solution.py:245
  17.3 1.3 %collective-permute-start.3 = (bf16[512,512]{1,0:T(8,128)(2,1)S(1)}, bf16[512,512]{1,0:T(8,128)(2,1)S(1)}, u32[]{:S(2)}, u32[]{:S(2)}) collective-permute-start(bf16[512,512]{1,0:T(8,128)(2,1)S(1)} %broadcast_select_fusion.1), channel_id=1, source_target_pairs={{0,2},{1,3},{2,0},{3,1},{4,6},{5,7},{6,4},{7,5},{8,10},{9,11},{10,... | collective-permute-start | bytes 1572872 | tf_op jit(solution)/shard_map/ppermute | solution.py:250
  18.6 1.3 %collective-permute-start.1 = (bf16[512,512]{1,0:T(8,128)(2,1)S(1)}, bf16[512,512]{1,0:T(8,128)(2,1)S(1)}, u32[]{:S(2)}, u32[]{:S(2)}) collective-permute-start(bf16[512,512]{1,0:T(8,128)(2,1)S(1)} %collective-permute-done.kv4), channel_id=1, source_target_pairs={{0,4},{1,5},{2,6},{3,7},{4,8},{5,9},{6,10},{7,11},{8,12},{9,13},{1... | collective-permute-start | bytes 1572872 | tf_op jit(solution)/shard_map/ppermute | solution.py:245
  20.1 1.3 %collective-permute-start.6 = (bf16[512,512]{1,0:T(8,128)(2,1)S(1)}, bf16[512,512]{1,0:T(8,128)(2,1)S(1)}, u32[]{:S(2)}, u32[]{:S(2)}) collective-permute-start(bf16[512,512]{1,0:T(8,128)(2,1)S(1)} %broadcast_select_fusion), channel_id=1, source_target_pairs={{0,2},{1,3},{2,0},{3,1},{4,6},{5,7},{6,4},{7,5},{8,10},{9,11},{10,... | collective-permute-start | bytes 1572872 | tf_op jit(solution)/shard_map/ppermute | solution.py:250
  21.4 4.1 %collective-permute-start.7 = (bf16[512,512]{1,0:T(8,128)(2,1)S(1)}, bf16[512,512]{1,0:T(8,128)(2,1)S(1)}, u32[]{:S(2)}, u32[]{:S(2)}) collective-permute-start(bf16[512,512]{1,0:T(8,128)(2,1)S(1)} %collective-permute-done.5.qd4), channel_id=1, source_target_pairs={{4,0},{5,1},{6,2},{7,3},{8,4},{9,5},{10,6},{11,7},{12,8},{13,9},{1... | collective-permute-start | bytes 1572872 | tf_op jit(solution)/shard_map/ppermute | solution.py:245
  25.6 3.7 %collective-permute-done.3.kv2 = bf16[512,512]{1,0:T(8,128)(2,1)S(1)} collective-permute-done((bf16[512,512]{1,0:T(8,128)(2,1)S(1)}, bf16[512,512]{1,0:T(8,128)(2,1)S(1)}, u32[]{:S(2)}, u32[]{:S(2)}) %collective-permute-start.3) | collective-permute-done | bytes 524320 | tf_op jit(solution)/shard_map/ppermute | solution.py:250
  29.3 4.6 %collective-permute-start.4 = (bf16[512,512]{1,0:T(8,128)(2,1)S(1)}, bf16[512,512]{1,0:T(8,128)(2,1)S(1)}, u32[]{:S(2)}, u32[]{:S(2)}) collective-permute-start(bf16[512,512]{1,0:T(8,128)(2,1)S(1)} %broadcast_select_fusion.3), channel_id=1, source_target_pairs={{0,1},{1,0},{2,3},{3,2},{4,5},{5,4},{6,7},{7,6},{8,9},{9,8},{10,11... | collective-permute-start | bytes 1572872 | tf_op jit(solution)/shard_map/ppermute | solution.py:250
  34.0 1.3 %collective-permute-start.2 = (bf16[512,512]{1,0:T(8,128)(2,1)S(1)}, bf16[512,512]{1,0:T(8,128)(2,1)S(1)}, u32[]{:S(2)}, u32[]{:S(2)}) collective-permute-start(bf16[512,512]{1,0:T(8,128)(2,1)S(1)} %passed.2.kv8), channel_id=1, source_target_pairs={{0,8},{1,9},{2,10},{3,11},{4,12},{5,13},{6,14},{7,15},{8,16},{9,17... | collective-permute-start | bytes 1572872 | tf_op jit(solution)/shard_map/ppermute | solution.py:245
  35.3 5.3 %collective-permute-done.6.qd2 = bf16[512,512]{1,0:T(8,128)(2,1)S(1)} collective-permute-done((bf16[512,512]{1,0:T(8,128)(2,1)S(1)}, bf16[512,512]{1,0:T(8,128)(2,1)S(1)}, u32[]{:S(2)}, u32[]{:S(2)}) %collective-permute-start.6) | collective-permute-done | bytes 524320 | tf_op jit(solution)/shard_map/ppermute | solution.py:250
  40.6 2.6 %collective-permute-start.8 = (bf16[512,512]{1,0:T(8,128)(2,1)S(1)}, bf16[512,512]{1,0:T(8,128)(2,1)S(1)}, u32[]{:S(2)}, u32[]{:S(2)}) collective-permute-start(bf16[512,512]{1,0:T(8,128)(2,1)S(1)} %broadcast_select_fusion.2), channel_id=1, source_target_pairs={{0,1},{1,0},{2,3},{3,2},{4,5},{5,4},{6,7},{7,6},{8,9},{9,8},{10,11... | collective-permute-start | bytes 1572872 | tf_op jit(solution)/shard_map/ppermute | solution.py:250
  43.2 3.1 %collective-permute-start.9 = (bf16[512,512]{1,0:T(8,128)(2,1)S(1)}, bf16[512,512]{1,0:T(8,128)(2,1)S(1)}, u32[]{:S(2)}, u32[]{:S(2)}) collective-permute-start(bf16[512,512]{1,0:T(8,128)(2,1)S(1)} %passed.3.qd8), channel_id=1, source_target_pairs={{8,0},{9,1},{10,2},{11,3},{12,4},{13,5},{14,6},{15,7},{16,8},{17,9... | collective-permute-start | bytes 1572872 | tf_op jit(solution)/shard_map/ppermute | solution.py:245
  46.3 1.0 %key_first.1 = (f32[4,256,768]{2,1,0:T(8,128)S(1)}, f32[4,256,768]{2,1,0:T(8,128)S(1)}) custom-call(bf16[256,512]{1,0:T(8,128)(2,1)S(1)} %copy-done.1, bf16[256,512]{1,0:T(8,128)(2,1)S(1)} %copy-done.3, bf16[512,512]{1,0:T(8,128)(2,1)S(1)} %collective-permute-done.6.qd2, bf16[512,512]{1,0:T(8,128)(2,1)S(1)} %collective-permute-done.5.qd4, ...), custom_call_target="tpu_custom_call" | custom-call | flops 402653184 | bytes 2621440 | tf_op jit(solution)/shard_map/key_first/pallas_call | solution.py:322
  47.4 2.6 %query_first.1 = (f32[4,256,512]{2,1,0:T(8,128)S(1)}, f32[4,256,512]{2,1,0:T(8,128)S(1)}, f32[256,512]{1,0:T(8,128)S(1)}, f32[256,512]{1,0:T(8,128)S(1)}, f32[256,512]{1,0:T(8,128)S(1)}) custom-call(s32[4]{0:T(128)S(1)} %copy-done.9, s32[4,4]{1,0:T(4,128)S(1)} %copy-done.8, bf16[256,512]{1,0:T(8,128)(2,1)S(1)} %copy-done.5, bf16[256,512]{1,0:T(8,128)(2,1)S(1)} %copy-done.7, ...), custom_call_target="tpu_custom_call" | custom-call | flops 402653184 | bytes 4194304 | tf_op jit(solution)/shard_map/query_first/pallas_call | solution.py:319
  50.0 9.7 %collective-permute-done.2.kv16 = bf16[512,512]{1,0:T(8,128)(2,1)S(1)} collective-permute-done((bf16[512,512]{1,0:T(8,128)(2,1)S(1)}, bf16[512,512]{1,0:T(8,128)(2,1)S(1)}, u32[]{:S(2)}, u32[]{:S(2)}) %collective-permute-start.2) | collective-permute-done | bytes 524320 | tf_op jit(solution)/shard_map/ppermute | solution.py:245
  59.8 2.0 %query_last.1 = (bf16[256,512]{1,0:T(8,128)(2,1)}, f32[16,256]{1,0:T(8,128)S(1)}, f32[256,512]{1,0:T(8,128)S(1)}, f32[256,512]{1,0:T(8,128)S(1)}) custom-call(s32[4,4]{1,0:T(4,128)S(1)} %copy-done.8, bf16[256,512]{1,0:T(8,128)(2,1)S(1)} %copy-done.5, bf16[256,512]{1,0:T(8,128)(2,1)S(1)} %copy-done.7, bf16[512,512]{1,0:T(8,128)(2,1)S(1)} %collective-permute-done.2.kv16, ...), custom_call_target="tpu_custom_call" | custom-call | flops 33554432 | bytes 3145728 | tf_op jit(solution)/shard_map/query_last/pallas_call | solution.py:323
  61.7 4.7 %collective-permute-start.10 = (f32[16,256]{1,0:T(8,128)S(1)}, f32[16,256]{1,0:T(8,128)S(1)}, u32[]{:S(2)}, u32[]{:S(2)}) collective-permute-start(f32[16,256]{1,0:T(8,128)S(1)} %get-tuple-element.27.st0), channel_id=1, source_target_pairs={{16,0},{17,1},{18,2},{19,3},{20,4},{21,5},{22,6},{23,7},{24,8},{25... | collective-permute-start | bytes 49160 | tf_op jit(solution)/shard_map/ppermute | solution.py:245
  66.4 1.3 %collective-permute-start.11 = (f32[16,256]{1,0:T(8,128)S(1)}, f32[16,256]{1,0:T(8,128)S(1)}, u32[]{:S(2)}, u32[]{:S(2)}) collective-permute-start(f32[16,256]{1,0:T(8,128)S(1)} %get-tuple-element.27.st0), channel_id=1, source_target_pairs={{8,0},{9,1},{10,2},{11,3},{12,4},{13,5},{14,6},{15,7},{16,8},{17,9... | collective-permute-start | bytes 49160 | tf_op jit(solution)/shard_map/ppermute | solution.py:245
  67.7 3.0 %collective-permute-start.12 = (f32[16,256]{1,0:T(8,128)S(1)}, f32[16,256]{1,0:T(8,128)S(1)}, u32[]{:S(2)}, u32[]{:S(2)}) collective-permute-start(f32[16,256]{1,0:T(8,128)S(1)} %get-tuple-element.27.st0), channel_id=1, source_target_pairs={{4,0},{5,1},{6,2},{7,3},{8,4},{9,5},{10,6},{11,7},{12,8},{13,9},{1... | collective-permute-start | bytes 49160 | tf_op jit(solution)/shard_map/ppermute | solution.py:245
  70.7 3.8 %collective-permute-start.13 = (f32[16,256]{1,0:T(8,128)S(1)}, f32[16,256]{1,0:T(8,128)S(1)}, u32[]{:S(2)}, u32[]{:S(2)}) collective-permute-start(f32[16,256]{1,0:T(8,128)S(1)} %get-tuple-element.27.st0), channel_id=1, source_target_pairs={{2,0},{3,1},{4,2},{5,3},{6,4},{7,5},{8,6},{9,7},{10,8},{11,9},{12,... | collective-permute-start | bytes 49160 | tf_op jit(solution)/shard_map/ppermute | solution.py:245
  74.5 4.5 %collective-permute-start.14 = (f32[16,256]{1,0:T(8,128)S(1)}, f32[16,256]{1,0:T(8,128)S(1)}, u32[]{:S(2)}, u32[]{:S(2)}) collective-permute-start(f32[16,256]{1,0:T(8,128)S(1)} %get-tuple-element.27.st0), channel_id=1, source_target_pairs={{1,0},{2,1},{3,2},{4,3},{5,4},{6,5},{7,6},{8,7},{9,8},{10,9},{11,1... | collective-permute-start | bytes 49160 | tf_op jit(solution)/shard_map/ppermute | solution.py:245
  79.0 2.6 %query_gradient.1 = bf16[256,512]{1,0:T(8,128)(2,1)} custom-call(s32[4,4]{1,0:T(4,128)S(1)} %copy-done.8, bf16[256,512]{1,0:T(8,128)(2,1)S(1)} %copy-done.5, bf16[256,512]{1,0:T(8,128)(2,1)S(1)} %copy-done.7, bf16[256,512]{1,0:T(8,128)(2,1)S(1)} %copy-done.1, bf16[256,512]{1,0:T(8,128)(2,1)S(1)} %copy-done.3, ...), custom_call_target="tpu_custom_call" | custom-call | flops 134217728 | bytes 6815744 | tf_op jit(solution)/shard_map/query_gradient/pallas_call | solution.py:333
  81.7 4.8 %key_last.1 = (bf16[256,512]{1,0:T(8,128)(2,1)}, bf16[256,512]{1,0:T(8,128)(2,1)}) custom-call(s32[4]{0:T(128)S(1)} %copy-done.9, bf16[256,512]{1,0:T(8,128)(2,1)S(1)} %copy-done.1, bf16[256,512]{1,0:T(8,128)(2,1)S(1)} %copy-done.3, bf16[256,512]{1,0:T(8,128)(2,1)S(1)} %copy-done.5, bf16[256,512]{1,0:T(8,128)(2,1)S(1)} %copy-done.7, ...), custom_call_target="tpu_custom_call" | custom-call | flops 805306368 | bytes 8912896 | tf_op jit(solution)/shard_map/key_last/pallas_call | solution.py:336
  (39 shorter events, 4.3 us)
Async XLA Ops:
  0.6 1.0 %copy-start = (bf16[256,512]{1,0:T(8,128)(2,1)S(1)}, bf16[256,512]{1,0:T(8,128)(2,1)}, u32[]{:S(2)}) copy-start(bf16[256,512]{1,0:T(8,128)(2,1)} %k0.7) | copy-start | bytes 786436
  1.6 0.9 %copy-start.2 = (bf16[256,512]{1,0:T(8,128)(2,1)S(1)}, bf16[256,512]{1,0:T(8,128)(2,1)}, u32[]{:S(2)}) copy-start(bf16[256,512]{1,0:T(8,128)(2,1)} %v0.7) | copy-start | bytes 786436
  2.6 14.7 %collective-permute-start = (bf16[512,512]{1,0:T(8,128)(2,1)S(1)}, bf16[512,512]{1,0:T(8,128)(2,1)S(1)}, u32[]{:S(2)}, u32[]{:S(2)}) collective-permute-start(bf16[512,512]{1,0:T(8,128)(2,1)S(1)} %pack.2), channel_id=1, source_target_pairs={{0,4},{1,5},{2,6},{3,7},{4,8},{5,9},{6,10},{7,11},{8,12},{9,13},{1... | collective-permute-start | bytes 1572872 | tf_op jit(solution)/shard_map/ppermute | solution.py:245
  3.9 1.0 %copy-start.4 = (bf16[256,512]{1,0:T(8,128)(2,1)S(1)}, bf16[256,512]{1,0:T(8,128)(2,1)}, u32[]{:S(2)}) copy-start(bf16[256,512]{1,0:T(8,128)(2,1)} %q0.1) | copy-start | bytes 786436
  5.8 14.2 %collective-permute-start.5 = (bf16[512,512]{1,0:T(8,128)(2,1)S(1)}, bf16[512,512]{1,0:T(8,128)(2,1)S(1)}, u32[]{:S(2)}, u32[]{:S(2)}) collective-permute-start(bf16[512,512]{1,0:T(8,128)(2,1)S(1)} %pack.3), channel_id=1, source_target_pairs={{4,0},{5,1},{6,2},{7,3},{8,4},{9,5},{10,6},{11,7},{12,8},{13,9},{1... | collective-permute-start | bytes 1572872 | tf_op jit(solution)/shard_map/ppermute | solution.py:245
  17.3 12.0 %collective-permute-start.3 = (bf16[512,512]{1,0:T(8,128)(2,1)S(1)}, bf16[512,512]{1,0:T(8,128)(2,1)S(1)}, u32[]{:S(2)}, u32[]{:S(2)}) collective-permute-start(bf16[512,512]{1,0:T(8,128)(2,1)S(1)} %broadcast_select_fusion.1), channel_id=1, source_target_pairs={{0,2},{1,3},{2,0},{3,1},{4,6},{5,7},{6,4},{7,5},{8,10},{9,11},{10,... | collective-permute-start | bytes 1572872 | tf_op jit(solution)/shard_map/ppermute | solution.py:250
  18.6 15.3 %collective-permute-start.1 = (bf16[512,512]{1,0:T(8,128)(2,1)S(1)}, bf16[512,512]{1,0:T(8,128)(2,1)S(1)}, u32[]{:S(2)}, u32[]{:S(2)}) collective-permute-start(bf16[512,512]{1,0:T(8,128)(2,1)S(1)} %collective-permute-done.kv4), channel_id=1, source_target_pairs={{0,4},{1,5},{2,6},{3,7},{4,8},{5,9},{6,10},{7,11},{8,12},{9,13},{1... | collective-permute-start | bytes 1572872 | tf_op jit(solution)/shard_map/ppermute | solution.py:245
  20.1 20.4 %collective-permute-start.6 = (bf16[512,512]{1,0:T(8,128)(2,1)S(1)}, bf16[512,512]{1,0:T(8,128)(2,1)S(1)}, u32[]{:S(2)}, u32[]{:S(2)}) collective-permute-start(bf16[512,512]{1,0:T(8,128)(2,1)S(1)} %broadcast_select_fusion), channel_id=1, source_target_pairs={{0,2},{1,3},{2,0},{3,1},{4,6},{5,7},{6,4},{7,5},{8,10},{9,11},{10,... | collective-permute-start | bytes 1572872 | tf_op jit(solution)/shard_map/ppermute | solution.py:250
  21.4 21.8 %collective-permute-start.7 = (bf16[512,512]{1,0:T(8,128)(2,1)S(1)}, bf16[512,512]{1,0:T(8,128)(2,1)S(1)}, u32[]{:S(2)}, u32[]{:S(2)}) collective-permute-start(bf16[512,512]{1,0:T(8,128)(2,1)S(1)} %collective-permute-done.5.qd4), channel_id=1, source_target_pairs={{4,0},{5,1},{6,2},{7,3},{8,4},{9,5},{10,6},{11,7},{12,8},{13,9},{1... | collective-permute-start | bytes 1572872 | tf_op jit(solution)/shard_map/ppermute | solution.py:245
  29.3 18.0 %collective-permute-start.4 = (bf16[512,512]{1,0:T(8,128)(2,1)S(1)}, bf16[512,512]{1,0:T(8,128)(2,1)S(1)}, u32[]{:S(2)}, u32[]{:S(2)}) collective-permute-start(bf16[512,512]{1,0:T(8,128)(2,1)S(1)} %broadcast_select_fusion.3), channel_id=1, source_target_pairs={{0,1},{1,0},{2,3},{3,2},{4,5},{5,4},{6,7},{7,6},{8,9},{9,8},{10,11... | collective-permute-start | bytes 1572872 | tf_op jit(solution)/shard_map/ppermute | solution.py:250
  34.0 25.8 %collective-permute-start.2 = (bf16[512,512]{1,0:T(8,128)(2,1)S(1)}, bf16[512,512]{1,0:T(8,128)(2,1)S(1)}, u32[]{:S(2)}, u32[]{:S(2)}) collective-permute-start(bf16[512,512]{1,0:T(8,128)(2,1)S(1)} %passed.2.kv8), channel_id=1, source_target_pairs={{0,8},{1,9},{2,10},{3,11},{4,12},{5,13},{6,14},{7,15},{8,16},{9,17... | collective-permute-start | bytes 1572872 | tf_op jit(solution)/shard_map/ppermute | solution.py:245
  40.6 5.7 %copy-start.1 = (bf16[256,512]{1,0:T(8,128)(2,1)S(1)}, bf16[256,512]{1,0:T(8,128)(2,1)}, u32[]{:S(2)}) copy-start(bf16[256,512]{1,0:T(8,128)(2,1)} %k0.7) | copy-start | bytes 786436
  40.6 5.7 %copy-start.3 = (bf16[256,512]{1,0:T(8,128)(2,1)S(1)}, bf16[256,512]{1,0:T(8,128)(2,1)}, u32[]{:S(2)}) copy-start(bf16[256,512]{1,0:T(8,128)(2,1)} %v0.7) | copy-start | bytes 786436
  40.6 6.7 %copy-start.5 = (bf16[256,512]{1,0:T(8,128)(2,1)S(1)}, bf16[256,512]{1,0:T(8,128)(2,1)}, u32[]{:S(2)}) copy-start(bf16[256,512]{1,0:T(8,128)(2,1)} %q0.1) | copy-start | bytes 786436
  40.6 6.7 %copy-start.7 = (bf16[256,512]{1,0:T(8,128)(2,1)S(1)}, bf16[256,512]{1,0:T(8,128)(2,1)}, u32[]{:S(2)}) copy-start(bf16[256,512]{1,0:T(8,128)(2,1)} %do0.1) | copy-start | bytes 786436
  40.6 6.7 %copy-start.8 = (s32[4,4]{1,0:T(4,128)S(1)}, s32[4,4]{1,0:T(4,128)}, u32[]{:S(2)}) copy-start(s32[4,4]{1,0:T(4,128)} %off.5) | copy-start | bytes 196
  40.6 6.7 %copy-start.9 = (s32[4]{0:T(128)S(1)}, s32[4]{0:T(128)}, u32[]{:S(2)}) copy-start(s32[4]{0:T(128)} %win.3) | copy-start | bytes 52
  40.6 30.1 %collective-permute-start.8 = (bf16[512,512]{1,0:T(8,128)(2,1)S(1)}, bf16[512,512]{1,0:T(8,128)(2,1)S(1)}, u32[]{:S(2)}, u32[]{:S(2)}) collective-permute-start(bf16[512,512]{1,0:T(8,128)(2,1)S(1)} %broadcast_select_fusion.2), channel_id=1, source_target_pairs={{0,1},{1,0},{2,3},{3,2},{4,5},{5,4},{6,7},{7,6},{8,9},{9,8},{10,11... | collective-permute-start | bytes 1572872 | tf_op jit(solution)/shard_map/ppermute | solution.py:250
  43.2 31.3 %collective-permute-start.9 = (bf16[512,512]{1,0:T(8,128)(2,1)S(1)}, bf16[512,512]{1,0:T(8,128)(2,1)S(1)}, u32[]{:S(2)}, u32[]{:S(2)}) collective-permute-start(bf16[512,512]{1,0:T(8,128)(2,1)S(1)} %passed.3.qd8), channel_id=1, source_target_pairs={{8,0},{9,1},{10,2},{11,3},{12,4},{13,5},{14,6},{15,7},{16,8},{17,9... | collective-permute-start | bytes 1572872 | tf_op jit(solution)/shard_map/ppermute | solution.py:245
  61.7 19.9 %collective-permute-start.10 = (f32[16,256]{1,0:T(8,128)S(1)}, f32[16,256]{1,0:T(8,128)S(1)}, u32[]{:S(2)}, u32[]{:S(2)}) collective-permute-start(f32[16,256]{1,0:T(8,128)S(1)} %get-tuple-element.27.st0), channel_id=1, source_target_pairs={{16,0},{17,1},{18,2},{19,3},{20,4},{21,5},{22,6},{23,7},{24,8},{25... | collective-permute-start | bytes 49160 | tf_op jit(solution)/shard_map/ppermute | solution.py:245
  66.4 15.2 %collective-permute-start.11 = (f32[16,256]{1,0:T(8,128)S(1)}, f32[16,256]{1,0:T(8,128)S(1)}, u32[]{:S(2)}, u32[]{:S(2)}) collective-permute-start(f32[16,256]{1,0:T(8,128)S(1)} %get-tuple-element.27.st0), channel_id=1, source_target_pairs={{8,0},{9,1},{10,2},{11,3},{12,4},{13,5},{14,6},{15,7},{16,8},{17,9... | collective-permute-start | bytes 49160 | tf_op jit(solution)/shard_map/ppermute | solution.py:245
  67.7 13.9 %collective-permute-start.12 = (f32[16,256]{1,0:T(8,128)S(1)}, f32[16,256]{1,0:T(8,128)S(1)}, u32[]{:S(2)}, u32[]{:S(2)}) collective-permute-start(f32[16,256]{1,0:T(8,128)S(1)} %get-tuple-element.27.st0), channel_id=1, source_target_pairs={{4,0},{5,1},{6,2},{7,3},{8,4},{9,5},{10,6},{11,7},{12,8},{13,9},{1... | collective-permute-start | bytes 49160 | tf_op jit(solution)/shard_map/ppermute | solution.py:245
  70.7 10.9 %collective-permute-start.13 = (f32[16,256]{1,0:T(8,128)S(1)}, f32[16,256]{1,0:T(8,128)S(1)}, u32[]{:S(2)}, u32[]{:S(2)}) collective-permute-start(f32[16,256]{1,0:T(8,128)S(1)} %get-tuple-element.27.st0), channel_id=1, source_target_pairs={{2,0},{3,1},{4,2},{5,3},{6,4},{7,5},{8,6},{9,7},{10,8},{11,9},{12,... | collective-permute-start | bytes 49160 | tf_op jit(solution)/shard_map/ppermute | solution.py:245
  74.5 7.1 %collective-permute-start.14 = (f32[16,256]{1,0:T(8,128)S(1)}, f32[16,256]{1,0:T(8,128)S(1)}, u32[]{:S(2)}, u32[]{:S(2)}) collective-permute-start(f32[16,256]{1,0:T(8,128)S(1)} %get-tuple-element.27.st0), channel_id=1, source_target_pairs={{1,0},{2,1},{3,2},{4,3},{5,4},{6,5},{7,6},{8,7},{9,8},{10,9},{11,1... | collective-permute-start | bytes 49160 | tf_op jit(solution)/shard_map/ppermute | solution.py:245
  (1 other events, 0.9 us)
